TPU v7x, 32 devices: a whole 2x2x4 slice. The times are simulated.
32 devices in a mesh: gx: 8 (over z, core), gy: 4 (over y, x).
Axes of the slice: x: 2, y: 2, z: 4, core: 2. Of those that a mesh axis runs over, the one named last changes fastest.
Arguments:
- positions: float32 [3, 2048], P(None, ('gx', 'gy')), may hold values from -6 to 6
- block_prev: float32 [32, 3, 2048], P(None, None, ('gx', 'gy')), may hold values from -6 to 6
- block_cur: float32 [32, 3, 2048], P(None, None, ('gx', 'gy')), may hold values from -6 to 6
- neighbours: int32 [32, 2048], P(None, ('gx', 'gy')), may hold values from 0 to 319
- counts: int32 [2048], P(('gx', 'gy')), may hold values from 1 to 32
- x_lists: int32 [32, 2, 64], P(('gx', 'gy')), may hold values from 0 to 63, as said below
- y_lists: int32 [32, 2, 64], P(('gx', 'gy')), may hold values from 0 to 191, as said below
- w_radial: float32 [8, 128], replicated, may hold values from -0.375 to 0.375
- w_vector: float32 [8, 128], replicated, may hold values from -1.5 to 1.5
- w_mix: float32 [128, 128], replicated, may hold values from -0.5 to 0.5
- w_out: float32 [128], replicated, may hold values from -0.5 to 0.5
Outputs:
- new_blocks: float32 [2, 32, 3, 2048], P(None, None, None, ('gx', 'gy'))
- factors: float32 [2, 32, 32], replicated
Inputs may be any that keep to these rules, and one draw needn't show every extreme that they name: `x_lists`: the two lists of a domain each hold distinct indices of the domain's own atoms. `y_lists`: the two lists of a domain each hold distinct indices into the domain's widened atoms (own atoms, then the two received gx lists).
All inputs are finite; a program needn't handle non-finite values.
Results may differ from a plain program's by a relative error of at most 0.0003.
Values sent between devices are 32-bit elements; how exact they have to be, the bound alone decides.
No kernel may reach another device: no remote copies, remote signals or barrier semaphores. Data moves between devices by JAX's collectives and lax.ppermute only.
A program may use at most 64 MiB of HBM per device.

v0:
```python
import functools

import jax
import jax.numpy as jnp
from jax import lax
from jax.experimental import pallas as pl
from jax.experimental.pallas import tpu as pltpu
from jax.sharding import PartitionSpec as P

SOFTEN = 0.25
CUTOFF = 5.0
GAUSS_WIDTH = 2.0
EXACT = lax.Precision.HIGHEST
VMEM_BYTES = 48 * 1024 * 1024
NN = (((1,), (0,)), ((), ()))
NT = (((1,), (1,)), ((), ()))
TN = (((0,), (0,)), ((), ()))


def dot16(left, right, dims=NN):
    return lax.dot_general(left, right, dims, preferred_element_type=jnp.float32)


def dot32(left, right, dims=NN):
    return lax.dot_general(
        left, right, dims, precision=EXACT, preferred_element_type=jnp.float32
    )


def split(values, parts):
    pieces = []
    for _ in range(parts):
        piece = values.astype(jnp.bfloat16)
        pieces.append(piece)
        values = values - piece.astype(jnp.float32)
    return jnp.concatenate(pieces, axis=0)


def dot_split(left, right, dims=NN):
    if dims == TN:
        left = left.T
        dims = NN
    rows = left.shape[0]
    both = split(left, 2)
    high = right.astype(jnp.bfloat16)
    low = (right - high.astype(jnp.float32)).astype(jnp.bfloat16)
    first = dot16(both, high, dims)
    return first[:rows] + first[rows:] + dot16(both[:rows], low, dims)


def component(block, comp, half):
    start = comp * half
    return jnp.concatenate(
        [block[start : start + half], block[3 * half + start : 3 * half + start + half]], axis=0
    )


def unpack(packed, atoms):
    return jnp.concatenate([packed[:, :atoms], packed[:, atoms:]], axis=0)


def pick_matrix(index_row, patch_rows):
    extended = index_row.shape[1]
    rows = lax.broadcasted_iota(jnp.int32, (patch_rows, extended), 0)
    return (rows == index_row).astype(jnp.float32).astype(jnp.bfloat16)


def difference_matrix(dm_ref, nb, extended, atoms):
    half = nb.shape[0] // 2
    lanes = 2 * atoms
    paired = jnp.concatenate([nb[:half], nb[half:]], axis=1)
    rows = lax.broadcasted_iota(jnp.int32, (extended, lanes), 0)
    lane = lax.broadcasted_iota(jnp.int32, (extended, lanes), 1)
    own = (rows == jnp.where(lane < atoms, lane, lane - atoms)).astype(jnp.float32)
    for j in range(half):
        hit = (rows == paired[j : j + 1, :]).astype(jnp.float32)
        dm_ref[:, j * lanes : (j + 1) * lanes] = (hit - own).astype(jnp.bfloat16)


def fill_patch(patch_ref, sources, first, rows, atoms):
    for y, source in enumerate(sources):
        for x in range(3):
            block = source(x, first, rows)
            at = (3 * y + x) * atoms
            patch_ref[0:rows, at : at + atoms] = block[:, :atoms]
            patch_ref[rows : 2 * rows, at : at + atoms] = block[:, atoms:]


def apply_operator(parts16, dm_ref, ef_ref, ee_ref, e8_ref, p_ref, r_ref, mv_ref, eo_ref, xs_ref, sx_ref, cs_ref, atoms, moved_ready=False):
    lanes = 2 * atoms
    edges = dm_ref.shape[1]
    groups = edges // lanes
    basis = ef_ref.shape[0]
    vec3 = mv_ref.shape[0]
    half = vec3 // 6
    pairs = 2 * basis
    tiles = vec3 // 24
    lower = lax.broadcasted_iota(jnp.int32, (8, lanes), 1) < atoms

    def rows_of(tile, comp):
        per_half = half // 8
        return (tile // per_half) * 3 * half + comp * half + (tile % per_half) * 8

    if not moved_ready:
        wide = 2 * lanes
        for j in range(edges // wide):
            got = dot16(parts16, dm_ref[:, j * wide : (j + 1) * wide])
            mv_ref[:, j * wide : (j + 1) * wide] = got[:vec3] + got[vec3 : 2 * vec3]

    for tile in range(tiles):

        def gather_step(j, acc, tile=tile):
            at = pl.ds(pl.multiple_of(j * lanes, lanes), lanes)
            m = [mv_ref[rows_of(tile, c) : rows_of(tile, c) + 8, at] for c in range(3)]
            head = [e8_ref[c : c + 1, at] for c in range(3)]
            u = head[0] * m[0] + head[1] * m[1] + head[2] * m[2]
            along = [head[c] * u for c in range(3)]
            across = [m[c] - along[c] for c in range(3)]
            new = list(acc)
            for k in range(basis):
                slope = ef_ref[k : k + 1, at]
                even = ee_ref[k : k + 1, at]
                new[k] = new[k] + slope * u
                for c in range(3):
                    i = (c + 1) * basis + k
                    new[i] = new[i] + (slope * along[c] + even * across[c])
            return tuple(new)

        zero = jnp.zeros((8, lanes), jnp.float32)
        acc = lax.fori_loop(0, groups, gather_step, (zero,) * (4 * basis))
        for i in range(pairs):
            a, b = acc[i], acc[i + pairs]
            x = jnp.where(lower, a, b) + pltpu.roll(jnp.where(lower, b, a), atoms, 1)
            xs_ref[i, tile * 8 : tile * 8 + 8, :] = x
            sx_ref[i, tile * 8 : tile * 8 + 8, :] = pltpu.roll(x, atoms, 1)

    wide_lower = lax.broadcasted_iota(jnp.int32, (8 * tiles, lanes), 1) < atoms

    def mix_step(kappa, carry):
        at = pl.ds(pl.multiple_of(kappa * pairs, pairs), pairs)
        straight = p_ref[at, :]
        crossed = r_ref[at, :]
        y = jnp.zeros((8 * tiles, lanes), jnp.float32)
        for i in range(pairs):
            y = y + straight[i : i + 1, :] * xs_ref[i] + crossed[i : i + 1, :] * sx_ref[i]
        turned = pltpu.roll(y, atoms, 1)
        cs_ref[kappa] = jnp.where(wide_lower, y, turned)
        cs_ref[kappa + pairs] = jnp.where(wide_lower, turned, y)
        return carry

    lax.fori_loop(0, pairs, mix_step, 0)

    for tile in range(tiles):
        coeff = [cs_ref[i, tile * 8 : tile * 8 + 8, :] for i in range(4 * basis)]

        def spread_step(j, carry, tile=tile, coeff=coeff):
            at = pl.ds(pl.multiple_of(j * lanes, lanes), lanes)
            m = [mv_ref[rows_of(tile, c) : rows_of(tile, c) + 8, at] for c in range(3)]
            row = [e8_ref[i : i + 1, at] for i in range(8)]
            head, turn = row[0:3], row[5:8]
            u = head[0] * m[0] + head[1] * m[1] + head[2] * m[2]
            radial = jnp.zeros((8, lanes), jnp.float32)
            sums = [radial, radial, radial]
            evens = [radial, radial, radial]
            for k in range(basis):
                slope = ef_ref[k : k + 1, at]
                even = ee_ref[k : k + 1, at]
                radial = radial + slope * coeff[k]
                for c in range(3):
                    i = (c + 1) * basis + k
                    sums[c] = sums[c] + slope * coeff[i]
                    evens[c] = evens[c] + even * coeff[i]
            inner = radial + row[4] * u
            for c in range(3):
                inner = inner + head[c] * (sums[c] - evens[c]) + turn[c] * m[c]
            for c in range(3):
                out = evens[c] + head[c] * inner + row[3] * m[c] + turn[c] * u
                eo_ref[rows_of(tile, c) : rows_of(tile, c) + 8, at] = out
            return carry

        lax.fori_loop(0, groups, spread_step, 0)

    spread = dot16(split(eo_ref[...], 2), dm_ref[...], NT)
    return spread[:vec3] + spread[vec3:]


def store_patch(outs, extended_rows, pick, atoms):
    vec3 = extended_rows.shape[0]
    half3 = vec3 // 2
    both = dot16(split(extended_rows, 2), pick, NT)
    patch = both[:vec3] + both[vec3:]
    for x in range(3):
        for y in range(3):
            at = (3 * y + x) * atoms
            tile = patch[:, at : at + atoms]
            outs[x][y * half3 : (y + 1) * half3, 0:atoms] = tile[:half3]
            outs[x][y * half3 : (y + 1) * half3, atoms : 2 * atoms] = tile[half3:]


def pack_kernel(cur_ref, prev_ref, pos_ref, xl_ref, yl_ref, out_ref):
    vectors, _, atoms = cur_ref.shape
    half = vectors // 2
    for which, ref in enumerate((cur_ref, prev_ref)):
        for c in range(3):
            rows = ref[:, c, :]
            at = which * 3 * half + c * half
            out_ref[at : at + half, 0:atoms] = rows[:half]
            out_ref[at : at + half, atoms : 2 * atoms] = rows[half:]
    base = 6 * half
    out_ref[base : base + 8, :] = jnp.zeros((8, 2 * atoms), jnp.float32)
    out_ref[base : base + 3, 0:atoms] = pos_ref[...]
    halo = xl_ref.shape[1]
    out_ref[base : base + 2, atoms : atoms + halo] = xl_ref[...].astype(jnp.float32)
    out_ref[base + 2 : base + 4, atoms : atoms + halo] = yl_ref[...].astype(jnp.float32)


def index_row(sides, own3_ref, base, atoms, halo):
    even_x = sides[0] == 0
    even_y = sides[1] == 0

    def lists(ref_y, x, row):
        return ref_y[x, base + row : base + row + 1, atoms : atoms + halo]

    before_x, after_x = jnp.where(even_x, 2.0, 0.0), jnp.where(even_x, 0.0, 2.0)
    before_y, after_y = jnp.where(even_y, 2.0, 0.0), jnp.where(even_y, 0.0, 2.0)

    def pick_x(ref_y):
        low = jnp.where(even_x, lists(ref_y, 2, 0), lists(ref_y, 0, 0)) + before_x * atoms
        high = jnp.where(even_x, lists(ref_y, 0, 1), lists(ref_y, 2, 1)) + after_x * atoms
        own = lax.broadcasted_iota(jnp.int32, (1, atoms), 1).astype(jnp.float32) + atoms
        return jnp.concatenate([own, low, high], axis=1)

    refs = own3_ref
    row_y = 3.0 * atoms
    pieces = [pick_x(refs[1]) + row_y]
    tables = [pick_x(refs[0]), pick_x(refs[2])]
    for row, place, mate_has in ((2, before_y, False), (3, after_y, True)):
        use_mate = even_y == mate_has if isinstance(mate_has, bool) else mate_has
        mate_list, other_list = lists(refs[0], 1, row), lists(refs[2], 1, row)
        if mate_has:
            chosen = jnp.where(even_y, mate_list, other_list)
            table = jnp.where(even_y, tables[0], tables[1])
        else:
            chosen = jnp.where(even_y, other_list, mate_list)
            table = jnp.where(even_y, tables[1], tables[0])
        widened = table.shape[1]
        hits = lax.broadcasted_iota(jnp.int32, (widened, halo), 0) == chosen.astype(jnp.int32)
        found = dot32(jnp.broadcast_to(table, (8, widened)), hits.astype(jnp.float32))
        pieces.append(found[0:1] + place * row_y)
    return jnp.round(jnp.concatenate(pieces, axis=1)).astype(jnp.int32)


def first_kernel(
    sides, own3, mate3, other3, nb, count, w_rad, w_vec, w_mix, w_out,
    out_m, out_o, out_x, sums, cext, pext, index, ef, ee, e8, pmat, rmat,
    dm, patch, mv, eo, xs, sx, cs, f2s, hs, qs,
    *, vectors, atoms, halo,
):
    half = vectors // 2
    half3 = 3 * half
    vec3 = 6 * half
    base = 2 * half3
    lanes = 2 * atoms
    slots = nb.shape[0]
    edges = slots * atoms
    extended = cext.shape[1]
    basis, channels = w_rad.shape
    pairs = 2 * basis
    refs = (mate3, own3, other3)

    difference_matrix(dm, nb[...], extended, atoms)
    places = index_row(sides, refs, base, atoms, halo)
    index[...] = jnp.broadcast_to(places, index.shape)
    pick = pick_matrix(places, 9 * atoms)

    sources = [lambda x, first, rows, ref=ref: ref[x, first : first + rows, :] for ref in refs]
    fill_patch(patch, sources, 0, half3, atoms)
    current = split(patch[...], 2)
    fill_patch(patch, sources, half3, half3, atoms)
    previous = split(patch[...], 2)
    patch[24:32, :] = jnp.zeros((8, 9 * atoms), jnp.float32)
    for y in range(3):
        for x in range(3):
            at = (3 * y + x) * atoms
            for c in range(3):
                line = refs[y][x, base + c : base + c + 1, 0:atoms]
                patch[8 * c : 8 * c + 8, at : at + atoms] = jnp.broadcast_to(line, (8, atoms))
    place = split(patch[0:32, :], 3)
    chosen = dot16(jnp.concatenate([current, previous, place], axis=0), pick)
    cext[...] = chosen[0:vec3] + chosen[vec3 : 2 * vec3]
    pext[...] = chosen[2 * vec3 : 3 * vec3] + chosen[3 * vec3 : 4 * vec3]
    parts16 = jnp.concatenate([chosen[: 2 * vec3], chosen[4 * vec3 :]], axis=0).astype(jnp.bfloat16)

    wide = 2 * lanes
    centre = (lax.broadcasted_iota(jnp.int32, (basis, wide), 0).astype(jnp.float32) + 0.5) * (CUTOFF / basis)
    counts = count[...]
    slot_lane = lax.broadcasted_iota(jnp.int32, (1, lanes), 1)
    slot_half = jnp.where(slot_lane < atoms, 0, slots // 2)
    counts2 = jnp.concatenate([counts, counts], axis=1)
    totals = [jnp.zeros((basis, lanes), jnp.float32) for _ in range(4)]
    for j in range(edges // wide):
        at = slice(j * wide, (j + 1) * wide)
        got = dot16(parts16, dm[:, at])
        mv[:, at] = got[:vec3] + got[vec3 : 2 * vec3]
        third = 2 * vec3
        delta = got[third : third + 24] + got[third + 32 : third + 56] + got[third + 64 : third + 88]
        d = [delta[8 * c : 8 * c + 8] for c in range(3)]
        squared = d[0] * d[0] + d[1] * d[1] + d[2] * d[2] + SOFTEN
        radius = jnp.sqrt(squared)
        inverse = 1.0 / radius
        head = [d[c] * inverse for c in range(3)]
        valid = jnp.concatenate(
            [(slot_half + (2 * j + i) < counts2).astype(jnp.float32) for i in range(2)], axis=1
        )
        tau = jnp.maximum(1.0 - squared * (1.0 / (CUTOFF * CUTOFF)), 0.0)
        cut = 1.0 / (CUTOFF * CUTOFF)
        env = tau * tau * tau
        env1 = (-6.0 * cut) * radius * tau * tau
        env2 = (24.0 * cut * cut) * squared * tau - (6.0 * cut) * tau * tau
        off = radius - centre
        gauss = jnp.exp(-GAUSS_WIDTH * off * off) * valid
        gauss1 = (-2.0 * GAUSS_WIDTH) * off * gauss
        gauss2 = (4.0 * GAUSS_WIDTH * GAUSS_WIDTH * off * off - 2.0 * GAUSS_WIDTH) * gauss
        value = gauss * env
        ef[:, at] = gauss1 * env + gauss * env1
        ee[:, at] = value * inverse
        f2s[:, at] = gauss2 * env + 2.0 * gauss1 * env1 + gauss * env2
        for c in range(3):
            hs[8 * c : 8 * c + 8, at] = head[c]
        hs[24:32, at] = inverse
        terms = [value, value * head[0], value * head[1], value * head[2]]
        totals = [t + v[:, :lanes] + v[:, lanes:] for t, v in zip(totals, terms)]
    descr = [t + pltpu.roll(t, atoms, 1) for t in totals]

    lower = lax.broadcasted_iota(jnp.int32, (channels, lanes), 1) < atoms
    rad = w_rad[...]
    vec = w_vec[...]
    mix = w_mix[...]
    rad_t = rad.T
    vec_t = vec.T
    mix_t = mix.T
    out_t = jnp.broadcast_to(w_out[...], (8, channels)).T[:, 0:1]
    flow = [dot32(vec_t, descr[c + 1]) for c in range(3)]
    mixed = dot32(rad_t, descr[0]) + flow[0] * flow[0] + flow[1] * flow[1] + flow[2] * flow[2]
    hidden = dot_split(mix_t, mixed)
    gate = 1.0 / (1.0 + jnp.exp(-hidden))
    slope = gate * (1.0 + hidden * (1.0 - gate)) * out_t
    bend = gate * (1.0 - gate) * (2.0 + hidden * (1.0 - 2.0 * gate)) * out_t
    u = dot_split(mix, slope)
    alpha = dot32(rad, u)
    beta = [2.0 * dot32(vec, flow[c] * u) for c in range(3)]

    for j in range(edges // lanes):
        at = slice(j * lanes, (j + 1) * lanes)
        head = [hs[8 * c : 8 * c + 8, at] for c in range(3)]
        inverse = hs[24:32, at]
        slope_k, even_k, second = ef[:, at], ee[:, at], f2s[:, at]
        even1 = (slope_k - even_k) * inverse
        even2 = (second - 2.0 * even1) * inverse

        def over(values):
            return jnp.sum(values, axis=0, keepdims=True)

        first = over(alpha * slope_k)
        bend_r = over(alpha * second)
        turn = [over(beta[c] * even1) for c in range(3)]
        twist = [over(beta[c] * even2) for c in range(3)]
        inv1 = inverse[0:1]
        h1 = [head[c][0:1] for c in range(3)]
        radius = 1.0 / inv1
        line = h1[0] * turn[0] + h1[1] * turn[1] + h1[2] * turn[2]
        isotropic = first * inv1 + line
        radial = bend_r + (h1[0] * twist[0] + h1[1] * twist[1] + h1[2] * twist[2]) * radius - isotropic
        e8[:, at] = jnp.concatenate(h1 + [isotropic, radial] + turn, axis=0)

    lift0 = 2.0 * jnp.where(lower, flow[0], flow[2])
    lift1 = 2.0 * flow[1]
    for i in range(pairs):
        k = i % basis
        if i < basis:
            side = jnp.where(lower, jnp.broadcast_to(rad_t[:, k : k + 1], lower.shape), lift1 * vec_t[:, k : k + 1])
        else:
            side = lift0 * vec_t[:, k : k + 1]
        qs[:, i * lanes : (i + 1) * lanes] = dot_split(mix_t, side)
    both = [2.0 * dot32(vec * vec[k : k + 1, :], u) for k in range(basis)]
    low_row = lax.broadcasted_iota(jnp.int32, (1, lanes), 1) < atoms
    for i in range(pairs):
        q_i = qs[:, i * lanes : (i + 1) * lanes] * bend
        for k in range(i + 1):
            q_k = qs[:, k * lanes : (k + 1) * lanes]
            straight = jnp.sum(q_i * q_k, axis=0, keepdims=True)
            crossed = jnp.sum(q_i * pltpu.roll(q_k, atoms, 1), axis=0, keepdims=True)
            if (i < basis) == (k < basis):
                extra = both[i % basis][k % basis : k % basis + 1, :]
                straight = straight + (jnp.where(low_row, 0.0, extra) if i < basis else extra)
            pmat[i * pairs + k : i * pairs + k + 1, :] = straight
            rmat[i * pairs + k : i * pairs + k + 1, :] = crossed
            if k < i:
                pmat[k * pairs + i : k * pairs + i + 1, :] = straight
                rmat[k * pairs + i : k * pairs + i + 1, :] = pltpu.roll(crossed, atoms, 1)

    rows = apply_operator(None, dm, ef, ee, e8, pmat, rmat, mv, eo, xs, sx, cs, atoms, True)
    store_patch((out_m, out_o, out_x), rows, pick, atoms)

    basis_dot = jnp.zeros((2 * vectors, vectors), jnp.float32)
    gram = jnp.zeros((2 * vectors, 2 * vectors), jnp.float32)
    for c in range(3):
        old = jnp.concatenate([component(cext[...], c, half), component(pext[...], c, half)], axis=0)
        basis_dot = basis_dot + dot_split(old, component(rows, c, half), NT)
        own = old[:, :atoms]
        gram = gram + dot_split(own, own, NT)
    blank = jnp.zeros((2 * vectors, sums.shape[1] - 3 * vectors), jnp.float32)
    sums[...] = jnp.concatenate([gram, basis_dot, blank], axis=1)


def second_kernel(
    order, own, mate, other, far, cext, pext, index, nb, ef, ee, e8, pmat, rmat,
    out_m, out_o, out_x, sums, rown,
    dm, patch, mv, eo, xs, sx, cs, ring,
    *, vectors, atoms, total_rows,
):
    half = vectors // 2
    half3 = 3 * half
    vec3 = 6 * half
    tail = 3 * half3
    extended = cext.shape[1]
    difference_matrix(dm, nb[...], extended, atoms)
    pick = pick_matrix(index[0:1, :], 9 * atoms)
    for i, part in enumerate((own, mate, other)):
        ring[order[i]] = part[tail:, :]
    ring[order[3]] = far[...]
    total = ((ring[0] + ring[1]) + (ring[2] + ring[3])) * (1.0 / total_rows)
    sums[...] = total
    coef = total[:, 2 * vectors : 3 * vectors]

    refs = (mate, own, other)
    for x, ref in enumerate(refs):
        for y in range(3):
            at = (3 * y + x) * atoms
            block = ref[y * half3 : (y + 1) * half3, :]
            patch[0:half3, at : at + atoms] = block[:, :atoms]
            patch[half3:vec3, at : at + atoms] = block[:, atoms:]
    both = dot16(split(patch[...], 2), pick)
    work = both[:vec3] + both[vec3:]
    pieces = []
    for c in range(3):
        old = jnp.concatenate([component(cext[...], c, half), component(pext[...], c, half)], axis=0)
        pieces.append(dot_split(coef.T, old))
    lower = [p[:half] for p in pieces]
    upper = [p[half:] for p in pieces]
    resid = work - jnp.concatenate(lower + upper, axis=0)
    rown[...] = jnp.concatenate([resid[:half3, :atoms], resid[half3:, :atoms]], axis=1)
    rows = apply_operator(split(resid, 2), dm, ef, ee, e8, pmat, rmat, mv, eo, xs, sx, cs, atoms)
    store_patch((out_m, out_o, out_x), rows, pick, atoms)


def gram_kernel(rown, y0, ym, yo, out, yown, *, vectors, atoms):
    half = vectors // 2
    work = y0[...] + ym[...] + yo[...]
    yown[...] = work
    gram = jnp.zeros((2 * vectors, 2 * vectors), jnp.float32)
    for c in range(3):
        at = slice(c * half, (c + 1) * half)
        r, y = rown[at, :], work[at, :]
        stacked = jnp.concatenate(
            [r[:, :atoms], r[:, atoms:], y[:, :atoms], y[:, atoms:]], axis=0
        )
        gram = gram + dot_split(stacked, stacked, NT)
    full = jnp.concatenate([gram, jnp.zeros_like(gram)], axis=1)
    out[...] = jnp.broadcast_to(full[None], out.shape)


def cholesky(matrix):
    size = matrix.shape[0]
    rows = lax.broadcasted_iota(jnp.int32, (size, 2 * size), 0)
    lane = lax.broadcasted_iota(jnp.int32, (size, 2 * size), 1)
    unit = (lane - size == rows).astype(jnp.float32)
    work = jnp.concatenate([matrix, jnp.zeros_like(matrix)], axis=1) + unit
    done = jnp.zeros_like(work)
    for j in range(size):
        line = work[j : j + 1, :]
        pivot = work[j : j + 1, j : j + 1]
        scale = lax.rsqrt(pivot)
        scale = scale * (1.5 - 0.5 * pivot * scale * scale)
        line = line * scale
        column = work[:, j : j + 1] * scale
        done = jnp.where(rows == j, line, done)
        work = work - column * line
    upper = jnp.where(lane >= rows, done, 0.0)[:, :size]
    return upper, done[:, size:]


def final_kernel(got, sums, rown, yown, cown, blocks, factors, *, vectors, atoms, total_rows):
    half = vectors // 2
    half3 = 3 * half
    devices = got.shape[0]
    total = got[0]
    for i in range(1, devices):
        total = total + got[i]
    total = total * (1.0 / total_rows)
    v = vectors
    rr, ry, yy = total[:v, :v], total[:v, v : 2 * v], total[v : 2 * v, v : 2 * v]
    shared = sums[...]
    gram_old = shared[:, : 2 * v]
    coef1 = shared[:, 2 * v : 3 * v]
    rows = lax.broadcasted_iota(jnp.int32, (v, v), 0)
    cols = lax.broadcasted_iota(jnp.int32, (v, v), 1)
    unit = (rows == cols).astype(jnp.float32)

    upper1, inv1 = cholesky(rr)
    left = coef1 - dot32(gram_old, coef1)
    wr = rr + dot32(coef1, left, TN)
    coef_x = dot32(dot32(inv1, ry), inv1, NT)
    coef_c = dot32(wr, inv1, NT)
    cross = dot32(left[:v], inv1, NT)
    yy1 = dot32(dot32(inv1, yy), inv1, NT)
    coef2 = jnp.concatenate([coef_x, coef_c], axis=0)
    basis = jnp.concatenate(
        [
            jnp.concatenate([-unit, cross.T], axis=1),
            jnp.concatenate([cross, gram_old[:v, :v] - 2.0 * unit], axis=1),
        ],
        axis=0,
    )
    gram2 = yy1 + dot32(coef2, dot32(basis, coef2), TN)
    upper2, inv2 = cholesky(gram2)
    by_x = dot32(inv2, coef_x, NT)
    m_y = dot32(inv2, inv1)
    m_r = -dot32(by_x, inv1)
    m_c = -dot32(inv2, coef_c, NT)
    weights = jnp.concatenate([m_y, m_r, m_c], axis=1)
    factors[0] = upper1.T
    factors[1] = upper2.T
    for c in range(3):
        at = slice(c * half, (c + 1) * half)
        r, y, old = unpack(rown[at, :], atoms), unpack(yown[at, :], atoms), unpack(cown[at, :], atoms)
        blocks[0, :, c, :] = dot32(inv1, r)
        blocks[1, :, c, :] = dot32(weights, jnp.concatenate([y, r, old], axis=0))


def mates(count):
    mate = [i ^ 1 for i in range(count)]
    other = [(i - 1) % count if i % 2 == 0 else (i + 1) % count for i in range(count)]
    return mate, other


def fetch(values, axis, sources):
    return lax.ppermute(values, axis, [(s, i) for i, s in enumerate(sources)])


def vmem_call(kernel, outs, scratch=(), scalars=0, **cost):
    def call(*operands):
        spaces = [pltpu.SMEM] * scalars + [pltpu.VMEM] * (len(operands) - scalars)
        return pl.pallas_call(
            kernel,
            out_shape=outs,
            in_specs=[pl.BlockSpec(memory_space=s) for s in spaces],
            out_specs=jax.tree.map(lambda _: pl.BlockSpec(memory_space=pltpu.VMEM), outs),
            scratch_shapes=list(scratch),
            compiler_params=pltpu.CompilerParams(vmem_limit_bytes=VMEM_BYTES),
            cost_estimate=pl.CostEstimate(
                flops=cost.get("flops", 1 << 20), bytes_accessed=1 << 16, transcendentals=0
            ),
        )(*operands)

    return call


def f32(*shape):
    return jax.ShapeDtypeStruct(shape, jnp.float32)


def shards(positions, block_prev, block_cur, neighbours, counts, x_lists, y_lists, w_radial, w_vector, w_mix, w_out):
    vectors, _, atoms = block_cur.shape
    halo = x_lists.shape[2]
    slots = neighbours.shape[0]
    basis, channels = w_radial.shape
    n_x, n_y = lax.axis_size("gx"), lax.axis_size("gy")
    total_rows = 3.0 * atoms * n_x * n_y
    half3 = 3 * vectors // 2
    vec3 = 3 * vectors
    lanes = 2 * atoms
    edges = slots * atoms
    extended = atoms + 4 * halo
    pairs = 2 * basis
    mate_x, other_x = mates(n_x)
    mate_y, other_y = mates(n_y)
    at_x, at_y = lax.axis_index("gx"), lax.axis_index("gy")
    sides = jnp.stack([at_x % 2, at_y % 2]).astype(jnp.int32)
    own_rows = 2 * half3 + 8

    own = vmem_call(pack_kernel, f32(own_rows, lanes))(
        block_cur, block_prev, positions, x_lists[0], y_lists[0]
    )
    from_mate = fetch(own, "gx", mate_x)
    from_other = fetch(own, "gx", other_x)
    own3 = jnp.stack([from_mate, own, from_other])
    mate3 = fetch(own3, "gy", mate_y)
    other3 = fetch(own3, "gy", other_y)

    extent = pltpu.VMEM((extended, edges), jnp.bfloat16)
    work_scratch = [
        extent,
        pltpu.VMEM((vec3, 9 * atoms), jnp.float32),
        pltpu.VMEM((vec3, edges), jnp.float32),
        pltpu.VMEM((vec3, edges), jnp.float32),
        pltpu.VMEM((pairs, vectors, lanes), jnp.float32),
        pltpu.VMEM((pairs, vectors, lanes), jnp.float32),
        pltpu.VMEM((2 * pairs, vectors, lanes), jnp.float32),
    ]
    first = vmem_call(
        functools.partial(first_kernel, vectors=vectors, atoms=atoms, halo=halo),
        [
            f32(3 * half3, lanes),
            f32(3 * half3, lanes),
            f32(3 * half3, lanes),
            f32(2 * vectors, lanes),
            f32(vec3, extended),
            f32(vec3, extended),
            jax.ShapeDtypeStruct((8, extended), jnp.int32),
            f32(basis, edges),
            f32(basis, edges),
            f32(8, edges),
            f32(pairs * pairs, lanes),
            f32(pairs * pairs, lanes),
        ],
        work_scratch
        + [
            pltpu.VMEM((basis, edges), jnp.float32),
            pltpu.VMEM((32, edges), jnp.float32),
            pltpu.VMEM((channels, pairs * lanes), jnp.float32),
        ],
        scalars=1,
        flops=1 << 31,
    )
    part_m, part_0, part_o, local, cext, pext, index, ef, ee, e8, pmat, rmat = first(
        sides, own3, mate3, other3, neighbours, counts[None], w_radial, w_vector, w_mix, w_out[None]
    )

    back_m = fetch(part_m, "gx", mate_x)
    back_o = fetch(part_o, "gx", other_x)
    strided = [local] + [
        fetch(local, "gx", [(i + d) % n_x for i in range(n_x)]) for d in range(4, n_x, 4)
    ]
    if len(strided) == 2:
        local = strided[0] + strided[1]
    else:
        local = jnp.sum(jnp.roll(jnp.stack(strided), at_x // 4, axis=0), axis=0)
    folded = part_0 + back_m + back_o
    f_m, f_0, f_o = folded[:half3], folded[half3 : 2 * half3], folded[2 * half3 :]

    far_m = [other_y[m] for m in mate_y]
    far_o = [mate_y[o] for o in other_y]
    got_m = fetch(jnp.concatenate([f_0, f_m, local]), "gy", mate_y)
    got_o = fetch(jnp.concatenate([f_0, f_o, local]), "gy", other_y)
    if far_m == far_o:
        got_2 = fetch(jnp.concatenate([f_m, f_o, local]), "gy", far_m)
        far_mate, far_other = got_2[half3 : 2 * half3], got_2[:half3]
        sums = (local + got_m[2 * half3 :]) + (got_o[2 * half3 :] + got_2[2 * half3 :])
    else:
        far_mate = fetch(f_o, "gy", far_m)
        far_other = fetch(f_m, "gy", far_o)
        terms = [local] + [
            fetch(local, "gy", [(i + d) % n_y for i in range(n_y)]) for d in range(1, n_y)
        ]
        sums = jnp.sum(jnp.roll(jnp.stack(terms), at_y, axis=0), axis=0)
    w_m = got_m[:half3] + f_m + far_mate
    w_0 = f_0 + got_m[half3 : 2 * half3] + got_o[half3 : 2 * half3]
    w_o = got_o[:half3] + far_other + f_o
    column = jnp.concatenate([w_m, w_0, w_o, sums])

    col_m = fetch(column, "gx", mate_x)
    col_o = fetch(column, "gx", other_x)
    far = fetch(sums, "gx", [(i + 2) % n_x for i in range(n_x)])
    order = jnp.stack(
        [at_x % 4, (at_x ^ 1) % 4, (at_x - 1 + 2 * (at_x % 2)) % 4, (at_x + 2) % 4]
    ).astype(jnp.int32)

    second = vmem_call(
        functools.partial(second_kernel, vectors=vectors, atoms=atoms, total_rows=total_rows),
        [
            f32(3 * half3, lanes),
            f32(3 * half3, lanes),
            f32(3 * half3, lanes),
            f32(2 * vectors, lanes),
            f32(half3, lanes),
        ],
        work_scratch + [pltpu.VMEM((4, 2 * vectors, lanes), jnp.float32)],
        scalars=1,
        flops=1 << 30,
    )
    part_m, part_0, part_o, shared, rown = second(
        order, column, col_m, col_o, far, cext, pext, index, neighbours, ef, ee, e8, pmat, rmat
    )
    back_m = fetch(part_m, "gx", mate_x)
    back_o = fetch(part_o, "gx", other_x)
    folded = part_0 + back_m + back_o
    y_m = fetch(folded[:half3], "gy", mate_y)
    y_o = fetch(folded[2 * half3 :], "gy", other_y)

    devices = n_x * n_y
    spread, yown = vmem_call(
        functools.partial(gram_kernel, vectors=vectors, atoms=atoms),
        [f32(devices, 2 * vectors, lanes), f32(half3, lanes)],
    )(rown, folded[half3 : 2 * half3], y_m, y_o)
    got = lax.all_to_all(spread, ("gx", "gy"), 0, 0)
    blocks, factors = vmem_call(
        functools.partial(final_kernel, vectors=vectors, atoms=atoms, total_rows=total_rows),
        [f32(2, vectors, 3, atoms), f32(2, vectors, vectors)],
    )(got, shared, rown, yown, own[:half3])
    return blocks, factors


def solution(mesh):
    placed = (
        P(None, ("gx", "gy")),
        P(None, None, ("gx", "gy")),
        P(None, None, ("gx", "gy")),
        P(None, ("gx", "gy")),
        P(("gx", "gy")),
        P(("gx", "gy"), None, None),
        P(("gx", "gy"), None, None),
        P(),
        P(),
        P(),
        P(),
    )
    return jax.shard_map(
        shards,
        mesh=mesh,
        in_specs=placed,
        out_specs=(P(None, None, None, ("gx", "gy")), P()),
        check_vma=False,
    )
```

profile of v0, /device:TPU:0, one launch (start us, length us, event | category | flops | bytes accessed | tf_op | source)
XLA Modules:
  0.0 115.9 jit_solution(12680131129572349018)
XLA Ops:
  0.6 0.8 copy.14.prev_ref
  1.5 0.0 copy-start.2
  1.6 0.0 copy-start
  1.6 0.0 copy-start.1
  1.6 0.6 copy-done.2
  2.2 0.1 copy-done
  2.2 0.0 copy-done.1
  2.3 0.1 shard_map.122
  2.4 4.5 %collective-permute-start.1 = (f32[104,128]{1,0:T(8,128)S(1)}, f32[104,128]{1,0:T(8,128)S(1)}, u32[]{:S(2)}, u32[]{:S(2)}) collective-permute-start(f32[104,128]{1,0:T(8,128)S(1)} %shard_map.122), channel_id=1, source_target_pairs={{28,0},{8,4},{4,8},{16,12},{12,16},{24,20},{20,24},{0,28},{29,1},{... | collective-permute-start | bytes 159752 | tf_op jit(solution)/shard_map/ppermute | solution.py:548
  6.9 0.0 collective-permute-start
  6.9 1.9 %collective-permute-done.1 = f32[104,128]{1,0:T(8,128)S(1)} collective-permute-done((f32[104,128]{1,0:T(8,128)S(1)}, f32[104,128]{1,0:T(8,128)S(1)}, u32[]{:S(2)}, u32[]{:S(2)}) %collective-permute-start.1) | collective-permute-done | bytes 53280 | tf_op jit(solution)/shard_map/ppermute | solution.py:548
  8.8 0.0 collective-permute-done
  8.9 3.2 %collective-permute-start.3 = (f32[3,104,128]{2,1,0:T(8,128)S(1)}, f32[3,104,128]{2,1,0:T(8,128)S(1)}, u32[]{:S(2)}, u32[]{:S(2)}) collective-permute-start(f32[3,104,128]{2,1,0:T(8,128)S(1)} %pad_maximum_fusion.own3), channel_id=1, source_target_pairs={{3,0},{2,1},{1,2},{0,3},{7,4},{6,5},{5,6},{4,7},{11,8},{10,9},{9,1... | collective-permute-start | bytes 479240 | tf_op jit(solution)/shard_map/ppermute | solution.py:548
  12.1 0.5 collective-permute-start.2
  12.6 0.1 pad_add_fusion.1.sides
  12.7 4.3 %collective-permute-done.3.other3 = f32[3,104,128]{2,1,0:T(8,128)S(1)} collective-permute-done((f32[3,104,128]{2,1,0:T(8,128)S(1)}, f32[3,104,128]{2,1,0:T(8,128)S(1)}, u32[]{:S(2)}, u32[]{:S(2)}) %collective-permute-start.3) | collective-permute-done | bytes 159776 | tf_op jit(solution)/shard_map/ppermute | solution.py:548
  17.0 1.8 %collective-permute-done.2.mate3 = f32[3,104,128]{2,1,0:T(8,128)S(1)} collective-permute-done((f32[3,104,128]{2,1,0:T(8,128)S(1)}, f32[3,104,128]{2,1,0:T(8,128)S(1)}, u32[]{:S(2)}, u32[]{:S(2)}) %collective-permute-start.2) | collective-permute-done | bytes 159776 | tf_op jit(solution)/shard_map/ppermute | solution.py:548
  18.8 0.6 copy-done.7
  19.4 0.0 copy-done.8
  19.5 14.3 %shard_map.123 = (f32[144,128]{1,0:T(8,128)S(1)}, f32[144,128]{1,0:T(8,128)S(1)}, f32[144,128]{1,0:T(8,128)S(1)}, f32[64,128]{1,0:T(8,128)S(1)}, f32[96,320]{1,0...) custom-call(s32[2]{0:T(128)S(1)} %pad_add_fusion.1.sides, ...), custom_call_target="tpu_custom_call" | custom-call | flops 2147483648 | bytes 65536 | tf_op jit(solution)/shard_map/pallas_call | solution.py:554
  33.8 0.1 collective-permute-start.4
  33.9 3.2 %collective-permute-start.5 = (f32[144,128]{1,0:T(8,128)S(1)}, f32[144,128]{1,0:T(8,128)S(1)}, u32[]{:S(2)}, u32[]{:S(2)}) collective-permute-start(f32[144,128]{1,0:T(8,128)S(1)} %get-tuple-element.23), channel_id=1, source_target_pairs={{28,0},{8,4},{4,8},{16,12},{12,16},{24,20},{20,24},{0,28},{29,1},{... | collective-permute-start | bytes 221192 | tf_op jit(solution)/shard_map/ppermute | solution.py:548
  37.1 4.8 %collective-permute-done.6 = f32[64,128]{1,0:T(8,128)S(1)} collective-permute-done((f32[64,128]{1,0:T(8,128)S(1)}, f32[64,128]{1,0:T(8,128)S(1)}, u32[]{:S(2)}, u32[]{:S(2)}) %collective-permute-start.6) | collective-permute-done | bytes 32800 | tf_op jit(solution)/shard_map/ppermute | solution.py:548
  42.0 1.6 %collective-permute-start.7 = (f32[160,128]{1,0:T(8,128)S(1)}, f32[160,128]{1,0:T(8,128)S(1)}, u32[]{:S(2)}, u32[]{:S(2)}) collective-permute-start(f32[160,128]{1,0:T(8,128)S(1)} %get-tuple-element.51), channel_id=1, source_target_pairs={{1,0},{0,1},{3,2},{2,3},{5,4},{4,5},{7,6},{6,7},{9,8},{8,9},{11,10... | collective-permute-start | bytes 245768 | tf_op jit(solution)/shard_map/ppermute | solution.py:548
  43.5 0.5 collective-permute-start.8
  44.0 1.5 %collective-permute-start.9 = (f32[160,128]{1,0:T(8,128)S(1)}, f32[160,128]{1,0:T(8,128)S(1)}, u32[]{:S(2)}, u32[]{:S(2)}) collective-permute-start(f32[160,128]{1,0:T(8,128)S(1)} %get-tuple-element.53), channel_id=1, source_target_pairs={{3,0},{2,1},{1,2},{0,3},{7,4},{6,5},{5,6},{4,7},{11,8},{10,9},{9,1... | collective-permute-start | bytes 245768 | tf_op jit(solution)/shard_map/ppermute | solution.py:548
  45.5 1.1 collective-permute-done.7
  46.6 1.3 %collective-permute-done.8 = f32[160,128]{1,0:T(8,128)S(1)} collective-permute-done((f32[160,128]{1,0:T(8,128)S(1)}, f32[160,128]{1,0:T(8,128)S(1)}, u32[]{:S(2)}, u32[]{:S(2)}) %collective-permute-start.8) | collective-permute-done | bytes 81952 | tf_op jit(solution)/shard_map/ppermute | solution.py:548
  48.0 1.4 %collective-permute-done.9 = f32[160,128]{1,0:T(8,128)S(1)} collective-permute-done((f32[160,128]{1,0:T(8,128)S(1)}, f32[160,128]{1,0:T(8,128)S(1)}, u32[]{:S(2)}, u32[]{:S(2)}) %collective-permute-start.9) | collective-permute-done | bytes 81952 | tf_op jit(solution)/shard_map/ppermute | solution.py:548
  49.4 1.5 %collective-permute-start.12 = (f32[64,128]{1,0:T(8,128)S(1)}, f32[64,128]{1,0:T(8,128)S(1)}, u32[]{:S(2)}, u32[]{:S(2)}) collective-permute-start(f32[64,128]{1,0:T(8,128)S(1)} %fusion), channel_id=1, source_target_pairs={{8,0},{12,4},{16,8},{20,12},{24,16},{28,20},{0,24},{4,28},{9,1},{1... | collective-permute-start | bytes 98312 | tf_op jit(solution)/shard_map/ppermute | solution.py:548
  50.9 0.1 collective-permute-start.11
  51.0 0.7 collective-permute-start.10
  51.7 0.1 pad_add_fusion.order
  51.8 1.6 %collective-permute-done.12.far = f32[64,128]{1,0:T(8,128)S(1)} collective-permute-done((f32[64,128]{1,0:T(8,128)S(1)}, f32[64,128]{1,0:T(8,128)S(1)}, u32[]{:S(2)}, u32[]{:S(2)}) %collective-permute-start.12) | collective-permute-done | bytes 32800 | tf_op jit(solution)/shard_map/ppermute | solution.py:548
  53.4 3.6 %collective-permute-done.11.other = f32[208,128]{1,0:T(8,128)S(1)} collective-permute-done((f32[208,128]{1,0:T(8,128)S(1)}, f32[208,128]{1,0:T(8,128)S(1)}, u32[]{:S(2)}, u32[]{:S(2)}) %collective-permute-start.11) | collective-permute-done | bytes 106528 | tf_op jit(solution)/shard_map/ppermute | solution.py:548
  56.9 9.4 %shard_map.124 = (f32[144,128]{1,0:T(8,128)S(1)}, f32[144,128]{1,0:T(8,128)S(1)}, f32[144,128]{1,0:T(8,128)S(1)}, f32[64,128]{1,0:T(8,128)S(1)}, f32[48,128]{1,0:T(8,128)S(1)}) custom-call(s32[4]{0:T(128)S(1)} %pad_add_fusion.order, f32[208,128]{1,0:T(8,128)S(1)} %pad_maximum_fusion.4.own, f32[208,128]{1,0:T(8,128)S(1)} %collective-permute-done.10.mate, ...), custom_call_target="tpu_custom_call" | custom-call | flops 1073741824 | bytes 65536 | tf_op jit(solution)/shard_map/pallas_call | solution.py:554
  66.4 0.1 collective-permute-start.13
  66.4 1.5 %collective-permute-start.14 = (f32[144,128]{1,0:T(8,128)S(1)}, f32[144,128]{1,0:T(8,128)S(1)}, u32[]{:S(2)}, u32[]{:S(2)}) collective-permute-start(f32[144,128]{1,0:T(8,128)S(1)} %get-tuple-element.36), channel_id=1, source_target_pairs={{28,0},{8,4},{4,8},{16,12},{12,16},{24,20},{20,24},{0,28},{29,1},{... | collective-permute-start | bytes 221192 | tf_op jit(solution)/shard_map/ppermute | solution.py:548
  67.9 4.2 %collective-permute-done.14 = f32[144,128]{1,0:T(8,128)S(1)} collective-permute-done((f32[144,128]{1,0:T(8,128)S(1)}, f32[144,128]{1,0:T(8,128)S(1)}, u32[]{:S(2)}, u32[]{:S(2)}) %collective-permute-start.14) | collective-permute-done | bytes 73760 | tf_op jit(solution)/shard_map/ppermute | solution.py:548
  72.1 1.1 collective-permute-start.16
  73.2 1.4 %collective-permute-start.15 = (f32[48,128]{1,0:T(8,128)S(1)}, f32[48,128]{1,0:T(8,128)S(1)}, u32[]{:S(2)}, u32[]{:S(2)}) collective-permute-start(f32[48,128]{1,0:T(8,128)S(1)} %get-tuple-element.46), channel_id=1, source_target_pairs={{1,0},{0,1},{3,2},{2,3},{5,4},{4,5},{7,6},{6,7},{9,8},{8,9},{11,10... | collective-permute-start | bytes 73736 | tf_op jit(solution)/shard_map/ppermute | solution.py:548
  74.5 2.4 %collective-permute-done.16.yo = f32[48,128]{1,0:T(8,128)S(1)} collective-permute-done((f32[48,128]{1,0:T(8,128)S(1)}, f32[48,128]{1,0:T(8,128)S(1)}, u32[]{:S(2)}, u32[]{:S(2)}) %collective-permute-start.16) | collective-permute-done | bytes 24608 | tf_op jit(solution)/shard_map/ppermute | solution.py:548
  76.9 0.1 collective-permute-done.15.ym
  77.0 1.3 %shard_map.125 = (f32[32,64,128]{2,1,0:T(8,128)}, f32[48,128]{1,0:T(8,128)S(1)}) custom-call(f32[48,128]{1,0:T(8,128)S(1)} %get-tuple-element.33.rown, f32[48,128]{1,0:T(8,128)S(1)} %get-tuple-element.47.y0, f32[48,128]{1,0:T(8,128)S(1)} %collective-permute-done.15.ym, f32[48,128]{1,0:T(8,128)S(1)} %collective-permute-done.16.yo), custom_call_target="tpu_custom_call" | custom-call | flops 1048576 | bytes 65536 | tf_op jit(solution)/shard_map/pallas_call | solution.py:554
  78.3 2.6 %all-to-all-start = ((f32[32,64,128]{2,1,0:T(8,128)}), f32[32,64,128]{2,1,0:T(8,128)S(1)}, u32[]{:S(2)}, u32[]{:S(2)}) async-start(f32[32,64,128]{2,1,0:T(8,128)} %get-tuple-element.37), calls=%async_computation | async-start | bytes 2097152 | tf_op jit(solution)/shard_map/all_to_all | solution.py:706
  81.0 26.4 %all-to-all-done.got = f32[32,64,128]{2,1,0:T(8,128)S(1)} async-done(((f32[32,64,128]{2,1,0:T(8,128)}), f32[32,64,128]{2,1,0:T(8,128)S(1)}, u32[]{:S(2)}, u32[]{:S(2)}) %all-to-all-start) | async-done | bytes 1048608 | tf_op jit(solution)/shard_map/all_to_all | solution.py:706
  107.4 7.9 %shard_map.126 = (f32[2,32,3,64]{3,2,1,0:T(4,128)S(1)}, f32[2,32,32]{2,1,0:T(8,128)}) custom-call(f32[32,64,128]{2,1,0:T(8,128)S(1)} %all-to-all-done.got, f32[64,128]{1,0:T(8,128)S(1)} %get-tuple-element.38.sums, f32[48,128]{1,0:T(8,128)S(1)} %get-tuple-element.33.rown, f32[48,128]{1,0:T(8,128)S(1)} %get-tuple-element.39.yown, f32[48,128]{1,0:T(8,128)S(1)} %slice.84.cown), custom_call_target="tpu_custom_call" | custom-call | flops 1048576 | bytes 65536 | tf_op jit(solution)/shard_map/pallas_call | solution.py:554
  115.3 0.6 copy.15
  (30 shorter events, 0.2 us)
Async XLA Ops:
  0.6 0.9 copy-start.9
  1.5 0.7 copy-start.2
  1.6 0.7 copy-start
  1.6 0.7 copy-start.1
  2.4 6.5 %collective-permute-start.1 = (f32[104,128]{1,0:T(8,128)S(1)}, f32[104,128]{1,0:T(8,128)S(1)}, u32[]{:S(2)}, u32[]{:S(2)}) collective-permute-start(f32[104,128]{1,0:T(8,128)S(1)} %shard_map.122), channel_id=1, source_target_pairs={{28,0},{8,4},{4,8},{16,12},{12,16},{24,20},{20,24},{0,28},{29,1},{... | collective-permute-start | bytes 159752 | tf_op jit(solution)/shard_map/ppermute | solution.py:548
  6.9 1.9 %collective-permute-start = (f32[104,128]{1,0:T(8,128)S(1)}, f32[104,128]{1,0:T(8,128)S(1)}, u32[]{:S(2)}, u32[]{:S(2)}) collective-permute-start(f32[104,128]{1,0:T(8,128)S(1)} %shard_map.122), channel_id=1, source_target_pairs={{4,0},{0,4},{12,8},{8,12},{20,16},{16,20},{28,24},{24,28},{5,1},{1... | collective-permute-start | bytes 159752 | tf_op jit(solution)/shard_map/ppermute | solution.py:548
  8.8 10.0 %copy-start.3 = (f32[128,128]{1,0:T(8,128)S(1)}, f32[128,128]{1,0:T(8,128)}, u32[]{:S(2)}) copy-start(f32[128,128]{1,0:T(8,128)} %w_mix.1) | copy-start | bytes 196612
  8.9 8.2 %collective-permute-start.3 = (f32[3,104,128]{2,1,0:T(8,128)S(1)}, f32[3,104,128]{2,1,0:T(8,128)S(1)}, u32[]{:S(2)}, u32[]{:S(2)}) collective-permute-start(f32[3,104,128]{2,1,0:T(8,128)S(1)} %pad_maximum_fusion.own3), channel_id=1, source_target_pairs={{3,0},{2,1},{1,2},{0,3},{7,4},{6,5},{5,6},{4,7},{11,8},{10,9},{9,1... | collective-permute-start | bytes 479240 | tf_op jit(solution)/shard_map/ppermute | solution.py:548
  12.1 6.7 %collective-permute-start.2 = (f32[3,104,128]{2,1,0:T(8,128)S(1)}, f32[3,104,128]{2,1,0:T(8,128)S(1)}, u32[]{:S(2)}, u32[]{:S(2)}) collective-permute-start(f32[3,104,128]{2,1,0:T(8,128)S(1)} %pad_maximum_fusion.own3), channel_id=1, source_target_pairs={{1,0},{0,1},{3,2},{2,3},{5,4},{4,5},{7,6},{6,7},{9,8},{8,9},{11,10... | collective-permute-start | bytes 479240 | tf_op jit(solution)/shard_map/ppermute | solution.py:548
  12.6 6.2 %copy-start.4 = (s32[32,64]{1,0:T(8,128)S(1)}, s32[32,64]{1,0:T(8,128)}, u32[]{:S(2)}) copy-start(s32[32,64]{1,0:T(8,128)} %nb.3) | copy-start | bytes 24580
  12.6 6.2 %copy-start.6 = (f32[8,128]{1,0:T(8,128)S(1)}, f32[8,128]{1,0:T(8,128)}, u32[]{:S(2)}) copy-start(f32[8,128]{1,0:T(8,128)} %w_vec.1) | copy-start | bytes 12292
  12.6 6.2 %copy-start.5 = (f32[8,128]{1,0:T(8,128)S(1)}, f32[8,128]{1,0:T(8,128)}, u32[]{:S(2)}) copy-start(f32[8,128]{1,0:T(8,128)} %w_rad.1) | copy-start | bytes 12292
  18.8 0.7 copy-start.7
  18.8 0.7 copy-start.8
  33.8 8.1 %collective-permute-start.4 = (f32[144,128]{1,0:T(8,128)S(1)}, f32[144,128]{1,0:T(8,128)S(1)}, u32[]{:S(2)}, u32[]{:S(2)}) collective-permute-start(f32[144,128]{1,0:T(8,128)S(1)} %get-tuple-element.22), channel_id=1, source_target_pairs={{4,0},{0,4},{12,8},{8,12},{20,16},{16,20},{28,24},{24,28},{5,1},{1... | collective-permute-start | bytes 221192 | tf_op jit(solution)/shard_map/ppermute | solution.py:548
  33.9 8.0 %collective-permute-start.5 = (f32[144,128]{1,0:T(8,128)S(1)}, f32[144,128]{1,0:T(8,128)S(1)}, u32[]{:S(2)}, u32[]{:S(2)}) collective-permute-start(f32[144,128]{1,0:T(8,128)S(1)} %get-tuple-element.23), channel_id=1, source_target_pairs={{28,0},{8,4},{4,8},{16,12},{12,16},{24,20},{20,24},{0,28},{29,1},{... | collective-permute-start | bytes 221192 | tf_op jit(solution)/shard_map/ppermute | solution.py:548
  37.1 4.8 %collective-permute-start.6 = (f32[64,128]{1,0:T(8,128)S(1)}, f32[64,128]{1,0:T(8,128)S(1)}, u32[]{:S(2)}, u32[]{:S(2)}) collective-permute-start(f32[64,128]{1,0:T(8,128)S(1)} %get-tuple-element.24), channel_id=1, source_target_pairs={{16,0},{20,4},{24,8},{28,12},{0,16},{4,20},{8,24},{12,28},{17,1},{... | collective-permute-start | bytes 98312 | tf_op jit(solution)/shard_map/ppermute | solution.py:548
  42.0 4.7 %collective-permute-start.7 = (f32[160,128]{1,0:T(8,128)S(1)}, f32[160,128]{1,0:T(8,128)S(1)}, u32[]{:S(2)}, u32[]{:S(2)}) collective-permute-start(f32[160,128]{1,0:T(8,128)S(1)} %get-tuple-element.51), channel_id=1, source_target_pairs={{1,0},{0,1},{3,2},{2,3},{5,4},{4,5},{7,6},{6,7},{9,8},{8,9},{11,10... | collective-permute-start | bytes 245768 | tf_op jit(solution)/shard_map/ppermute | solution.py:548
  43.5 4.4 %collective-permute-start.8 = (f32[160,128]{1,0:T(8,128)S(1)}, f32[160,128]{1,0:T(8,128)S(1)}, u32[]{:S(2)}, u32[]{:S(2)}) collective-permute-start(f32[160,128]{1,0:T(8,128)S(1)} %get-tuple-element.52), channel_id=1, source_target_pairs={{2,0},{3,1},{0,2},{1,3},{6,4},{7,5},{4,6},{5,7},{10,8},{11,9},{8,1... | collective-permute-start | bytes 245768 | tf_op jit(solution)/shard_map/ppermute | solution.py:548
  44.0 5.3 %collective-permute-start.9 = (f32[160,128]{1,0:T(8,128)S(1)}, f32[160,128]{1,0:T(8,128)S(1)}, u32[]{:S(2)}, u32[]{:S(2)}) collective-permute-start(f32[160,128]{1,0:T(8,128)S(1)} %get-tuple-element.53), channel_id=1, source_target_pairs={{3,0},{2,1},{1,2},{0,3},{7,4},{6,5},{5,6},{4,7},{11,8},{10,9},{9,1... | collective-permute-start | bytes 245768 | tf_op jit(solution)/shard_map/ppermute | solution.py:548
  49.4 4.0 %collective-permute-start.12 = (f32[64,128]{1,0:T(8,128)S(1)}, f32[64,128]{1,0:T(8,128)S(1)}, u32[]{:S(2)}, u32[]{:S(2)}) collective-permute-start(f32[64,128]{1,0:T(8,128)S(1)} %fusion), channel_id=1, source_target_pairs={{8,0},{12,4},{16,8},{20,12},{24,16},{28,20},{0,24},{4,28},{9,1},{1... | collective-permute-start | bytes 98312 | tf_op jit(solution)/shard_map/ppermute | solution.py:548
  50.9 6.0 %collective-permute-start.11 = (f32[208,128]{1,0:T(8,128)S(1)}, f32[208,128]{1,0:T(8,128)S(1)}, u32[]{:S(2)}, u32[]{:S(2)}) collective-permute-start(f32[208,128]{1,0:T(8,128)S(1)} %pad_maximum_fusion.4.own), channel_id=1, source_target_pairs={{28,0},{8,4},{4,8},{16,12},{12,16},{24,20},{20,24},{0,28},{29,1},{... | collective-permute-start | bytes 319496 | tf_op jit(solution)/shard_map/ppermute | solution.py:548
  51.0 5.9 %collective-permute-start.10 = (f32[208,128]{1,0:T(8,128)S(1)}, f32[208,128]{1,0:T(8,128)S(1)}, u32[]{:S(2)}, u32[]{:S(2)}) collective-permute-start(f32[208,128]{1,0:T(8,128)S(1)} %pad_maximum_fusion.4.own), channel_id=1, source_target_pairs={{4,0},{0,4},{12,8},{8,12},{20,16},{16,20},{28,24},{24,28},{5,1},{1... | collective-permute-start | bytes 319496 | tf_op jit(solution)/shard_map/ppermute | solution.py:548
  66.4 1.5 %collective-permute-start.13 = (f32[144,128]{1,0:T(8,128)S(1)}, f32[144,128]{1,0:T(8,128)S(1)}, u32[]{:S(2)}, u32[]{:S(2)}) collective-permute-start(f32[144,128]{1,0:T(8,128)S(1)} %get-tuple-element.35), channel_id=1, source_target_pairs={{4,0},{0,4},{12,8},{8,12},{20,16},{16,20},{28,24},{24,28},{5,1},{1... | collective-permute-start | bytes 221192 | tf_op jit(solution)/shard_map/ppermute | solution.py:548
  66.4 5.6 %collective-permute-start.14 = (f32[144,128]{1,0:T(8,128)S(1)}, f32[144,128]{1,0:T(8,128)S(1)}, u32[]{:S(2)}, u32[]{:S(2)}) collective-permute-start(f32[144,128]{1,0:T(8,128)S(1)} %get-tuple-element.36), channel_id=1, source_target_pairs={{28,0},{8,4},{4,8},{16,12},{12,16},{24,20},{20,24},{0,28},{29,1},{... | collective-permute-start | bytes 221192 | tf_op jit(solution)/shard_map/ppermute | solution.py:548
  72.1 4.8 %collective-permute-start.16 = (f32[48,128]{1,0:T(8,128)S(1)}, f32[48,128]{1,0:T(8,128)S(1)}, u32[]{:S(2)}, u32[]{:S(2)}) collective-permute-start(f32[48,128]{1,0:T(8,128)S(1)} %get-tuple-element.45), channel_id=1, source_target_pairs={{3,0},{2,1},{1,2},{0,3},{7,4},{6,5},{5,6},{4,7},{11,8},{10,9},{9,1... | collective-permute-start | bytes 73736 | tf_op jit(solution)/shard_map/ppermute | solution.py:548
  73.2 3.8 %collective-permute-start.15 = (f32[48,128]{1,0:T(8,128)S(1)}, f32[48,128]{1,0:T(8,128)S(1)}, u32[]{:S(2)}, u32[]{:S(2)}) collective-permute-start(f32[48,128]{1,0:T(8,128)S(1)} %get-tuple-element.46), channel_id=1, source_target_pairs={{1,0},{0,1},{3,2},{2,3},{5,4},{4,5},{7,6},{6,7},{9,8},{8,9},{11,10... | collective-permute-start | bytes 73736 | tf_op jit(solution)/shard_map/ppermute | solution.py:548
  78.3 29.1 %all-to-all-start = ((f32[32,64,128]{2,1,0:T(8,128)}), f32[32,64,128]{2,1,0:T(8,128)S(1)}, u32[]{:S(2)}, u32[]{:S(2)}) async-start(f32[32,64,128]{2,1,0:T(8,128)} %get-tuple-element.37), calls=%async_computation | async-start | bytes 2097152 | tf_op jit(solution)/shard_map/all_to_all | solution.py:706
where the time goes:
time: 116 us
  waiting for transfers between devices  54.9 us (47%)
  Pallas kernels  33 us (28%)
  starting transfers between devices  23.9 us (21%)
  local copies, waits for them, and re-layouts  2.9 us (2%)
    pallas_call x5, Pallas kernels, call(): pl.pallas_call(kernel, out_shape=outs, in_specs=[pl.BlockSpec(memory_spac...  33 us
    ppermute x17, waiting for transfers between devices, fetch(): return lax.ppermute(values, axis, [(s, i) for i, s in enumerate(sources)])  28.5 us
    all_to_all x1, waiting for transfers between devices, shards(): got = lax.all_to_all(spread, ('gx', 'gy'), 0, 0)  26.4 us
    ppermute x17, starting transfers between devices, fetch(): return lax.ppermute(values, axis, [(s, i) for i, s in enumerate(sources)])  21.3 us
    all_to_all x1, starting transfers between devices, shards(): got = lax.all_to_all(spread, ('gx', 'gy'), 0, 0)  2.64 us
  transfers between devices with their start and end apart: 18, of which 13 were waited for; matrix products, arithmetic and copies ran while one was open for 0% of the time, Pallas kernels for 0%

commit v1 on v0

--- a/solution.py
+++ b/solution.py
@@ -48,15 +48,17 @@
     return first[:rows] + first[rows:] + dot16(both[:rows], low, dims)
 
 
-def component(block, comp, half):
-    start = comp * half
-    return jnp.concatenate(
-        [block[start : start + half], block[3 * half + start : 3 * half + start + half]], axis=0
-    )
+def component(block, comp, vectors):
+    return block[comp * vectors : (comp + 1) * vectors]
 
 
 def unpack(packed, atoms):
     return jnp.concatenate([packed[:, :atoms], packed[:, atoms:]], axis=0)
+
+
+def pack(rows):
+    half = rows.shape[0] // 2
+    return jnp.concatenate([rows[:half], rows[half:]], axis=1)
 
 
 def pick_matrix(index_row, patch_rows):
@@ -65,25 +67,58 @@
     return (rows == index_row).astype(jnp.float32).astype(jnp.bfloat16)
 
 
-def difference_matrix(dm_ref, nb, extended, atoms):
-    half = nb.shape[0] // 2
-    lanes = 2 * atoms
-    paired = jnp.concatenate([nb[:half], nb[half:]], axis=1)
-    rows = lax.broadcasted_iota(jnp.int32, (extended, lanes), 0)
-    lane = lax.broadcasted_iota(jnp.int32, (extended, lanes), 1)
-    own = (rows == jnp.where(lane < atoms, lane, lane - atoms)).astype(jnp.float32)
-    for j in range(half):
-        hit = (rows == paired[j : j + 1, :]).astype(jnp.float32)
-        dm_ref[:, j * lanes : (j + 1) * lanes] = (hit - own).astype(jnp.bfloat16)
-
-
-def fill_patch(patch_ref, sources, first, rows, atoms):
-    for y, source in enumerate(sources):
-        for x in range(3):
-            block = source(x, first, rows)
-            at = (3 * y + x) * atoms
-            patch_ref[0:rows, at : at + atoms] = block[:, :atoms]
-            patch_ref[rows : 2 * rows, at : at + atoms] = block[:, atoms:]
+def select(rows, first, second):
+    picks = jnp.concatenate([first, second], axis=1)
+    hits = lax.broadcasted_iota(jnp.int32, (rows.shape[1], picks.shape[1]), 0) == picks
+    got = dot16(split(rows, 3), hits.astype(jnp.float32).astype(jnp.bfloat16))
+    count = rows.shape[0]
+    return got[:count] + (got[count : 2 * count] + got[2 * count :])
+
+
+def rows_and_cols(size):
+    return (
+        lax.broadcasted_iota(jnp.int32, (size, size), 0),
+        lax.broadcasted_iota(jnp.int32, (size, size), 1),
+    )
+
+
+def join_triangles(lower, upper):
+    rows, cols = rows_and_cols(lower.shape[0])
+    return jnp.where(rows >= cols, lower, upper)
+
+
+def with_diagonal(lower, source):
+    size = lower.shape[0]
+    rows, cols = rows_and_cols(size)
+    line = jnp.sum(jnp.where(rows == cols, source, 0.0), axis=0, keepdims=True)
+    upper = jnp.where(rows == 0, line, jnp.where((rows == 1) & (cols == size - 1), source[0:1, 0:1], 0.0))
+    return jnp.where(rows >= cols, lower, upper)
+
+
+def from_lower(joined):
+    rows, cols = rows_and_cols(joined.shape[0])
+    strict = jnp.where(rows > cols, joined, 0.0)
+    return jnp.where(rows >= cols, joined, 0.0) + strict.T
+
+
+def from_upper(joined, holder):
+    size = joined.shape[0]
+    rows, cols = rows_and_cols(size)
+    strict = jnp.where(rows < cols, joined, 0.0)
+    line = jnp.where(cols[0:1] >= 1, holder[0:1], holder[1:2, size - 1 : size])
+    return strict + strict.T + jnp.where(rows == cols, line, 0.0)
+
+
+def flatten(square, lanes):
+    size = square.shape[0]
+    rows = size * size // lanes
+    return jnp.concatenate([square[i * rows : (i + 1) * rows] for i in range(lanes // size)], axis=1)
+
+
+def unflatten(flat, size):
+    return jnp.concatenate(
+        [flat[:, i * size : (i + 1) * size] for i in range(flat.shape[1] // size)], axis=0
+    )
 
 
 def apply_operator(parts16, dm_ref, ef_ref, ee_ref, e8_ref, p_ref, r_ref, mv_ref, eo_ref, xs_ref, sx_ref, cs_ref, atoms, moved_ready=False):
@@ -92,14 +127,13 @@
     groups = edges // lanes
     basis = ef_ref.shape[0]
     vec3 = mv_ref.shape[0]
-    half = vec3 // 6
+    vectors = vec3 // 3
     pairs = 2 * basis
     tiles = vec3 // 24
     lower = lax.broadcasted_iota(jnp.int32, (8, lanes), 1) < atoms
 
     def rows_of(tile, comp):
-        per_half = half // 8
-        return (tile // per_half) * 3 * half + comp * half + (tile % per_half) * 8
+        return comp * vectors + tile * 8
 
     if not moved_ready:
         wide = 2 * lanes
@@ -197,106 +231,85 @@
             outs[x][y * half3 : (y + 1) * half3, atoms : 2 * atoms] = tile[half3:]
 
 
-def pack_kernel(cur_ref, prev_ref, pos_ref, xl_ref, yl_ref, out_ref):
-    vectors, _, atoms = cur_ref.shape
-    half = vectors // 2
-    for which, ref in enumerate((cur_ref, prev_ref)):
-        for c in range(3):
-            rows = ref[:, c, :]
-            at = which * 3 * half + c * half
-            out_ref[at : at + half, 0:atoms] = rows[:half]
-            out_ref[at : at + half, atoms : 2 * atoms] = rows[half:]
-    base = 6 * half
-    out_ref[base : base + 8, :] = jnp.zeros((8, 2 * atoms), jnp.float32)
-    out_ref[base : base + 3, 0:atoms] = pos_ref[...]
-    halo = xl_ref.shape[1]
-    out_ref[base : base + 2, atoms : atoms + halo] = xl_ref[...].astype(jnp.float32)
-    out_ref[base + 2 : base + 4, atoms : atoms + halo] = yl_ref[...].astype(jnp.float32)
-
-
-def index_row(sides, own3_ref, base, atoms, halo):
-    even_x = sides[0] == 0
-    even_y = sides[1] == 0
-
-    def lists(ref_y, x, row):
-        return ref_y[x, base + row : base + row + 1, atoms : atoms + halo]
-
-    before_x, after_x = jnp.where(even_x, 2.0, 0.0), jnp.where(even_x, 0.0, 2.0)
-    before_y, after_y = jnp.where(even_y, 2.0, 0.0), jnp.where(even_y, 0.0, 2.0)
-
-    def pick_x(ref_y):
-        low = jnp.where(even_x, lists(ref_y, 2, 0), lists(ref_y, 0, 0)) + before_x * atoms
-        high = jnp.where(even_x, lists(ref_y, 0, 1), lists(ref_y, 2, 1)) + after_x * atoms
-        own = lax.broadcasted_iota(jnp.int32, (1, atoms), 1).astype(jnp.float32) + atoms
-        return jnp.concatenate([own, low, high], axis=1)
-
-    refs = own3_ref
-    row_y = 3.0 * atoms
-    pieces = [pick_x(refs[1]) + row_y]
-    tables = [pick_x(refs[0]), pick_x(refs[2])]
-    for row, place, mate_has in ((2, before_y, False), (3, after_y, True)):
-        use_mate = even_y == mate_has if isinstance(mate_has, bool) else mate_has
-        mate_list, other_list = lists(refs[0], 1, row), lists(refs[2], 1, row)
-        if mate_has:
-            chosen = jnp.where(even_y, mate_list, other_list)
-            table = jnp.where(even_y, tables[0], tables[1])
-        else:
-            chosen = jnp.where(even_y, other_list, mate_list)
-            table = jnp.where(even_y, tables[1], tables[0])
-        widened = table.shape[1]
-        hits = lax.broadcasted_iota(jnp.int32, (widened, halo), 0) == chosen.astype(jnp.int32)
-        found = dot32(jnp.broadcast_to(table, (8, widened)), hits.astype(jnp.float32))
-        pieces.append(found[0:1] + place * row_y)
-    return jnp.round(jnp.concatenate(pieces, axis=1)).astype(jnp.int32)
-
-
-def first_kernel(
-    sides, own3, mate3, other3, nb, count, w_rad, w_vec, w_mix, w_out,
-    out_m, out_o, out_x, sums, cext, pext, index, ef, ee, e8, pmat, rmat,
-    dm, patch, mv, eo, xs, sx, cs, f2s, hs, qs,
-    *, vectors, atoms, halo,
-):
-    half = vectors // 2
-    half3 = 3 * half
-    vec3 = 6 * half
-    base = 2 * half3
+def select_x_kernel(sides, cur, prev, pos, lists, to_mate, to_other):
+    half3 = cur.shape[0] // 2
+    atoms = cur.shape[1]
+    own = lax.broadcasted_iota(jnp.int32, (1, atoms), 1).astype(jnp.float32)
+    rows = jnp.concatenate([cur[...], prev[...], pos[...], own, jnp.zeros((4, atoms), jnp.float32)], axis=0)
+    emit(sides[0], rows, lists, to_mate, to_other, half3)
+
+
+def emit(side, rows, lists, to_mate, to_other, half3):
+    even = side == 0
+    low, high = lists[0:1, :], lists[1:2, :]
+    got = select(rows, jnp.where(even, low, high), jnp.where(even, high, low))
+    halo = low.shape[1]
+    for which, out in enumerate((to_mate, to_other)):
+        part = got[:, which * halo : (which + 1) * halo]
+        out[0:half3, :] = pack(part[0 : 2 * half3])
+        out[half3 : 2 * half3, :] = pack(part[2 * half3 : 4 * half3])
+        out[2 * half3 :, 0:halo] = part[4 * half3 :]
+        out[2 * half3 :, halo:] = jnp.zeros_like(part[4 * half3 :])
+
+
+def unpack_rows(block, half3, halo):
+    return jnp.concatenate(
+        [unpack(block[0:half3], halo), unpack(block[half3 : 2 * half3], halo), block[2 * half3 :, 0:halo]],
+        axis=0,
+    )
+
+
+def beside(rows, mate, other, even, step, half3, halo):
+    line = rows.shape[0] - 5
+    at = (lax.broadcasted_iota(jnp.int32, (rows.shape[0], 1), 0) == line).astype(jnp.float32) * step
+    mate, other = unpack_rows(mate, half3, halo), unpack_rows(other, half3, halo) + 2.0 * at
+    return jnp.concatenate(
+        [rows + at, jnp.where(even, other, mate), jnp.where(even, mate, other)], axis=1
+    )
+
+
+def select_y_kernel(sides, cur, prev, pos, from_mate, from_other, lists, to_mate, to_other, wide):
+    half3 = cur.shape[0] // 2
+    atoms = cur.shape[1]
+    own = lax.broadcasted_iota(jnp.int32, (1, atoms), 1).astype(jnp.float32)
+    rows = jnp.concatenate([cur[...], prev[...], pos[...], own, jnp.zeros((4, atoms), jnp.float32)], axis=0)
+    rows = beside(rows, from_mate[...], from_other[...], sides[0] == 0, float(atoms), half3, lists.shape[1])
+    wide[...] = rows
+    emit(sides[1], rows, lists, to_mate, to_other, half3)
+
+
+def prepare_kernel(nb, count, w_rad, w_vec, w_mix, w_out, dm, valid, rad_t, vec_t, mix_t, out_t):
+    slots, atoms = nb.shape
     lanes = 2 * atoms
-    slots = nb.shape[0]
-    edges = slots * atoms
-    extended = cext.shape[1]
-    basis, channels = w_rad.shape
-    pairs = 2 * basis
-    refs = (mate3, own3, other3)
-
-    difference_matrix(dm, nb[...], extended, atoms)
-    places = index_row(sides, refs, base, atoms, halo)
-    index[...] = jnp.broadcast_to(places, index.shape)
-    pick = pick_matrix(places, 9 * atoms)
-
-    sources = [lambda x, first, rows, ref=ref: ref[x, first : first + rows, :] for ref in refs]
-    fill_patch(patch, sources, 0, half3, atoms)
-    current = split(patch[...], 2)
-    fill_patch(patch, sources, half3, half3, atoms)
-    previous = split(patch[...], 2)
-    patch[24:32, :] = jnp.zeros((8, 9 * atoms), jnp.float32)
-    for y in range(3):
-        for x in range(3):
-            at = (3 * y + x) * atoms
-            for c in range(3):
-                line = refs[y][x, base + c : base + c + 1, 0:atoms]
-                patch[8 * c : 8 * c + 8, at : at + atoms] = jnp.broadcast_to(line, (8, atoms))
-    place = split(patch[0:32, :], 3)
-    chosen = dot16(jnp.concatenate([current, previous, place], axis=0), pick)
-    cext[...] = chosen[0:vec3] + chosen[vec3 : 2 * vec3]
-    pext[...] = chosen[2 * vec3 : 3 * vec3] + chosen[3 * vec3 : 4 * vec3]
-    parts16 = jnp.concatenate([chosen[: 2 * vec3], chosen[4 * vec3 :]], axis=0).astype(jnp.bfloat16)
-
+    difference_matrix(dm, nb[...], dm.shape[0], atoms)
+    lane = lax.broadcasted_iota(jnp.int32, (8, lanes), 1)
+    first = jnp.where(lane < atoms, 0, slots // 2)
+    limit = jnp.concatenate([count[...], count[...]], axis=1)
+    for j in range(slots // 2):
+        valid[:, j * lanes : (j + 1) * lanes] = (first + j < limit).astype(jnp.float32)
+    rad_t[...] = w_rad[...].T
+    vec_t[...] = w_vec[...].T
+    mix_t[...] = w_mix[...].T
+    out_t[...] = jnp.broadcast_to(w_out[...], (8, w_out.shape[1])).T
+
+
+def difference_matrix(dm_ref, nb, extended, atoms):
+    half = nb.shape[0] // 2
+    lanes = 2 * atoms
+    paired = jnp.concatenate([nb[:half], nb[half:]], axis=1)
+    rows = lax.broadcasted_iota(jnp.int32, (extended, lanes), 0)
+    lane = lax.broadcasted_iota(jnp.int32, (extended, lanes), 1)
+    own = (rows == jnp.where(lane < atoms, lane, lane - atoms)).astype(jnp.float32)
+    for j in range(half):
+        hit = (rows == paired[j : j + 1, :]).astype(jnp.float32)
+        dm_ref[:, j * lanes : (j + 1) * lanes] = (hit - own).astype(jnp.bfloat16)
+
+
+def gather_edges(parts16, dm, valid, mv, ef, ee, f2s, hs, vec3, lanes):
+    basis, edges = ef.shape
     wide = 2 * lanes
+    cut = 1.0 / (CUTOFF * CUTOFF)
     centre = (lax.broadcasted_iota(jnp.int32, (basis, wide), 0).astype(jnp.float32) + 0.5) * (CUTOFF / basis)
-    counts = count[...]
-    slot_lane = lax.broadcasted_iota(jnp.int32, (1, lanes), 1)
-    slot_half = jnp.where(slot_lane < atoms, 0, slots // 2)
-    counts2 = jnp.concatenate([counts, counts], axis=1)
     totals = [jnp.zeros((basis, lanes), jnp.float32) for _ in range(4)]
     for j in range(edges // wide):
         at = slice(j * wide, (j + 1) * wide)
@@ -309,16 +322,12 @@
         radius = jnp.sqrt(squared)
         inverse = 1.0 / radius
         head = [d[c] * inverse for c in range(3)]
-        valid = jnp.concatenate(
-            [(slot_half + (2 * j + i) < counts2).astype(jnp.float32) for i in range(2)], axis=1
-        )
-        tau = jnp.maximum(1.0 - squared * (1.0 / (CUTOFF * CUTOFF)), 0.0)
-        cut = 1.0 / (CUTOFF * CUTOFF)
+        tau = jnp.maximum(1.0 - squared * cut, 0.0)
         env = tau * tau * tau
         env1 = (-6.0 * cut) * radius * tau * tau
         env2 = (24.0 * cut * cut) * squared * tau - (6.0 * cut) * tau * tau
         off = radius - centre
-        gauss = jnp.exp(-GAUSS_WIDTH * off * off) * valid
+        gauss = jnp.exp(-GAUSS_WIDTH * off * off) * valid[:, at]
         gauss1 = (-2.0 * GAUSS_WIDTH) * off * gauss
         gauss2 = (4.0 * GAUSS_WIDTH * GAUSS_WIDTH * off * off - 2.0 * GAUSS_WIDTH) * gauss
         value = gauss * env
@@ -330,27 +339,11 @@
         hs[24:32, at] = inverse
         terms = [value, value * head[0], value * head[1], value * head[2]]
         totals = [t + v[:, :lanes] + v[:, lanes:] for t, v in zip(totals, terms)]
-    descr = [t + pltpu.roll(t, atoms, 1) for t in totals]
-
-    lower = lax.broadcasted_iota(jnp.int32, (channels, lanes), 1) < atoms
-    rad = w_rad[...]
-    vec = w_vec[...]
-    mix = w_mix[...]
-    rad_t = rad.T
-    vec_t = vec.T
-    mix_t = mix.T
-    out_t = jnp.broadcast_to(w_out[...], (8, channels)).T[:, 0:1]
-    flow = [dot32(vec_t, descr[c + 1]) for c in range(3)]
-    mixed = dot32(rad_t, descr[0]) + flow[0] * flow[0] + flow[1] * flow[1] + flow[2] * flow[2]
-    hidden = dot_split(mix_t, mixed)
-    gate = 1.0 / (1.0 + jnp.exp(-hidden))
-    slope = gate * (1.0 + hidden * (1.0 - gate)) * out_t
-    bend = gate * (1.0 - gate) * (2.0 + hidden * (1.0 - 2.0 * gate)) * out_t
-    u = dot_split(mix, slope)
-    alpha = dot32(rad, u)
-    beta = [2.0 * dot32(vec, flow[c] * u) for c in range(3)]
-
-    for j in range(edges // lanes):
+    return [t + pltpu.roll(t, lanes // 2, 1) for t in totals]
+
+
+def edge_rows(alpha, beta, ef, ee, f2s, hs, e8, lanes):
+    for j in range(ef.shape[1] // lanes):
         at = slice(j * lanes, (j + 1) * lanes)
         head = [hs[8 * c : 8 * c + 8, at] for c in range(3)]
         inverse = hs[24:32, at]
@@ -373,15 +366,24 @@
         radial = bend_r + (h1[0] * twist[0] + h1[1] * twist[1] + h1[2] * twist[2]) * radius - isotropic
         e8[:, at] = jnp.concatenate(h1 + [isotropic, radial] + turn, axis=0)
 
+
+def channel_lift(flow, rad_t, vec_t, mix_t, qs, lanes, atoms):
+    channels, basis = rad_t.shape
+    lower = lax.broadcasted_iota(jnp.int32, (channels, lanes), 1) < atoms
     lift0 = 2.0 * jnp.where(lower, flow[0], flow[2])
     lift1 = 2.0 * flow[1]
-    for i in range(pairs):
+    for i in range(2 * basis):
         k = i % basis
         if i < basis:
             side = jnp.where(lower, jnp.broadcast_to(rad_t[:, k : k + 1], lower.shape), lift1 * vec_t[:, k : k + 1])
         else:
             side = lift0 * vec_t[:, k : k + 1]
         qs[:, i * lanes : (i + 1) * lanes] = dot_split(mix_t, side)
+
+
+def descriptor_curvature(vec, u, bend, qs, pmat, rmat, lanes, atoms):
+    basis = vec.shape[0]
+    pairs = 2 * basis
     both = [2.0 * dot32(vec * vec[k : k + 1, :], u) for k in range(basis)]
     low_row = lax.broadcasted_iota(jnp.int32, (1, lanes), 1) < atoms
     for i in range(pairs):
@@ -399,75 +401,125 @@
                 pmat[k * pairs + i : k * pairs + i + 1, :] = straight
                 rmat[k * pairs + i : k * pairs + i + 1, :] = pltpu.roll(crossed, atoms, 1)
 
-    rows = apply_operator(None, dm, ef, ee, e8, pmat, rmat, mv, eo, xs, sx, cs, atoms, True)
-    store_patch((out_m, out_o, out_x), rows, pick, atoms)
-
-    basis_dot = jnp.zeros((2 * vectors, vectors), jnp.float32)
-    gram = jnp.zeros((2 * vectors, 2 * vectors), jnp.float32)
-    for c in range(3):
-        old = jnp.concatenate([component(cext[...], c, half), component(pext[...], c, half)], axis=0)
-        basis_dot = basis_dot + dot_split(old, component(rows, c, half), NT)
-        own = old[:, :atoms]
-        gram = gram + dot_split(own, own, NT)
-    blank = jnp.zeros((2 * vectors, sums.shape[1] - 3 * vectors), jnp.float32)
-    sums[...] = jnp.concatenate([gram, basis_dot, blank], axis=1)
+
+def first_kernel(
+    sides, wide, from_mate, from_other, dm, valid, w_rad, w_vec, w_mix, rad_t, vec_t, mix_t, out_t,
+    out_m, out_o, out_x, sums, cext, pext, index, ef, ee, e8, pmat, rmat,
+    mv, eo, xs, sx, cs, f2s, hs, qs,
+    *, vectors, atoms, halo,
+):
+    half3 = 3 * vectors // 2
+    vec3 = 2 * half3
+    lanes = 2 * atoms
+    rows = beside(wide[...], from_mate[...], from_other[...], sides[1] == 0, 3.0 * atoms, half3, halo)
+    cext[...] = rows[:vec3]
+    pext[...] = rows[vec3 : 2 * vec3]
+    base = 2 * vec3
+    places = jnp.round(rows[base + 3 : base + 4]).astype(jnp.int32)
+    index[...] = jnp.broadcast_to(places, index.shape)
+    shape = (8, rows.shape[1])
+    place = jnp.concatenate(
+        [jnp.broadcast_to(rows[base + c : base + c + 1], shape) for c in range(3)] + [jnp.zeros(shape, jnp.float32)],
+        axis=0,
+    )
+    parts16 = jnp.concatenate([split(rows[:vec3], 2), split(place, 3)], axis=0)
+    descr = gather_edges(parts16, dm, valid, mv, ef, ee, f2s, hs, vec3, lanes)
+
+    rad, vec, mix = w_rad[...], w_vec[...], w_mix[...]
+    radt, vect, mixt, outt = rad_t[...], vec_t[...], mix_t[...], out_t[:, 0:1]
+    flow = [dot32(vect, descr[c + 1]) for c in range(3)]
+    mixed = dot32(radt, descr[0]) + flow[0] * flow[0] + flow[1] * flow[1] + flow[2] * flow[2]
+    hidden = dot_split(mixt, mixed)
+    gate = 1.0 / (1.0 + jnp.exp(-hidden))
+    slope = gate * (1.0 + hidden * (1.0 - gate)) * outt
+    bend = gate * (1.0 - gate) * (2.0 + hidden * (1.0 - 2.0 * gate)) * outt
+    u = dot_split(mix, slope)
+    alpha = dot32(rad, u)
+    beta = [2.0 * dot32(vec, flow[c] * u) for c in range(3)]
+    edge_rows(alpha, beta, ef, ee, f2s, hs, e8, lanes)
+    channel_lift(flow, radt, vect, mixt, qs, lanes, atoms)
+    descriptor_curvature(vec, u, bend, qs, pmat, rmat, lanes, atoms)
+
+    result = apply_operator(None, dm, ef, ee, e8, pmat, rmat, mv, eo, xs, sx, cs, atoms, True)
+    store_patch((out_m, out_o, out_x), result, pick_matrix(places, 9 * atoms), atoms)
+
+    def gram(left, right, width):
+        total = jnp.zeros((vectors, vectors), jnp.float32)
+        for c in range(3):
+            total = total + dot_split(
+                component(left, c, vectors)[:, :width], component(right, c, vectors)[:, :width], NT
+            )
+        return total
+
+    old_c, old_p = rows[:vec3], rows[vec3 : 2 * vec3]
+    extended = rows.shape[1]
+    cw, pw = gram(old_c, result, extended), gram(old_p, result, extended)
+    cc, cp, pp = gram(old_c, old_c, atoms), gram(old_c, old_p, atoms), gram(old_p, old_p, atoms)
+    sums[...] = jnp.concatenate([with_diagonal(cw, pp), pw, cp, join_triangles(cc, pp)], axis=1)
 
 
 def second_kernel(
-    order, own, mate, other, far, cext, pext, index, nb, ef, ee, e8, pmat, rmat,
-    out_m, out_o, out_x, sums, rown,
-    dm, patch, mv, eo, xs, sx, cs, ring,
+    order, own, mate, other, far, cext, pext, index, dm, ef, ee, e8, pmat, rmat,
+    out_m, out_o, out_x, shared, rown,
+    mv, eo, xs, sx, cs, patch, ring,
     *, vectors, atoms, total_rows,
 ):
-    half = vectors // 2
-    half3 = 3 * half
-    vec3 = 6 * half
+    half3 = 3 * vectors // 2
+    vec3 = 2 * half3
     tail = 3 * half3
-    extended = cext.shape[1]
-    difference_matrix(dm, nb[...], extended, atoms)
     pick = pick_matrix(index[0:1, :], 9 * atoms)
     for i, part in enumerate((own, mate, other)):
         ring[order[i]] = part[tail:, :]
     ring[order[3]] = far[...]
     total = ((ring[0] + ring[1]) + (ring[2] + ring[3])) * (1.0 / total_rows)
-    sums[...] = total
-    coef = total[:, 2 * vectors : 3 * vectors]
-
-    refs = (mate, own, other)
-    for x, ref in enumerate(refs):
+    v = vectors
+    held, pw, cp, joined = (total[:, i * v : (i + 1) * v] for i in range(4))
+    coef = jnp.concatenate([from_lower(held), pw], axis=0)
+    cc, pp = from_lower(joined), from_upper(joined, held)
+    gram_old = jnp.concatenate(
+        [jnp.concatenate([cc, cp], axis=1), jnp.concatenate([cp.T, pp], axis=1)], axis=0
+    )
+    shared[...] = jnp.concatenate([gram_old, coef, jnp.zeros_like(coef)], axis=1)
+
+    for x, ref in enumerate((mate, own, other)):
         for y in range(3):
             at = (3 * y + x) * atoms
-            block = ref[y * half3 : (y + 1) * half3, :]
-            patch[0:half3, at : at + atoms] = block[:, :atoms]
-            patch[half3:vec3, at : at + atoms] = block[:, atoms:]
+            patch[:, at : at + atoms] = unpack(ref[y * half3 : (y + 1) * half3, :], atoms)
     both = dot16(split(patch[...], 2), pick)
     work = both[:vec3] + both[vec3:]
-    pieces = []
-    for c in range(3):
-        old = jnp.concatenate([component(cext[...], c, half), component(pext[...], c, half)], axis=0)
-        pieces.append(dot_split(coef.T, old))
-    lower = [p[:half] for p in pieces]
-    upper = [p[half:] for p in pieces]
-    resid = work - jnp.concatenate(lower + upper, axis=0)
-    rown[...] = jnp.concatenate([resid[:half3, :atoms], resid[half3:, :atoms]], axis=1)
+    turned = coef.T
+    resid = work - jnp.concatenate(
+        [
+            dot_split(
+                turned,
+                jnp.concatenate(
+                    [component(cext[...], c, vectors), component(pext[...], c, vectors)], axis=0
+                ),
+            )
+            for c in range(3)
+        ],
+        axis=0,
+    )
+    rown[...] = pack(resid[:, :atoms])
     rows = apply_operator(split(resid, 2), dm, ef, ee, e8, pmat, rmat, mv, eo, xs, sx, cs, atoms)
     store_patch((out_m, out_o, out_x), rows, pick, atoms)
 
 
 def gram_kernel(rown, y0, ym, yo, out, yown, *, vectors, atoms):
-    half = vectors // 2
     work = y0[...] + ym[...] + yo[...]
     yown[...] = work
+    r, y = unpack(rown[...], atoms), unpack(work, atoms)
     gram = jnp.zeros((2 * vectors, 2 * vectors), jnp.float32)
     for c in range(3):
-        at = slice(c * half, (c + 1) * half)
-        r, y = rown[at, :], work[at, :]
-        stacked = jnp.concatenate(
-            [r[:, :atoms], r[:, atoms:], y[:, :atoms], y[:, atoms:]], axis=0
-        )
+        stacked = jnp.concatenate([component(r, c, vectors), component(y, c, vectors)], axis=0)
         gram = gram + dot_split(stacked, stacked, NT)
-    full = jnp.concatenate([gram, jnp.zeros_like(gram)], axis=1)
-    out[...] = jnp.broadcast_to(full[None], out.shape)
+    v = vectors
+    rr, ry, yy = gram[:v, :v], gram[:v, v:], gram[v:, v:]
+    lanes = out.shape[2]
+    sent = jnp.concatenate(
+        [flatten(join_triangles(rr, yy), lanes), flatten(with_diagonal(ry, yy), lanes)], axis=0
+    )
+    out[...] = jnp.broadcast_to(sent[None], out.shape)
 
 
 def cholesky(matrix):
@@ -491,15 +543,15 @@
 
 
 def final_kernel(got, sums, rown, yown, cown, blocks, factors, *, vectors, atoms, total_rows):
-    half = vectors // 2
-    half3 = 3 * half
     devices = got.shape[0]
     total = got[0]
     for i in range(1, devices):
         total = total + got[i]
     total = total * (1.0 / total_rows)
     v = vectors
-    rr, ry, yy = total[:v, :v], total[:v, v : 2 * v], total[v : 2 * v, v : 2 * v]
+    count = total.shape[0] // 2
+    joined, held = unflatten(total[:count], v), unflatten(total[count:], v)
+    rr, ry, yy = from_lower(joined), from_lower(held), from_upper(joined, held)
     shared = sums[...]
     gram_old = shared[:, : 2 * v]
     coef1 = shared[:, 2 * v : 3 * v]
@@ -531,11 +583,11 @@
     weights = jnp.concatenate([m_y, m_r, m_c], axis=1)
     factors[0] = upper1.T
     factors[1] = upper2.T
+    r, y, old = unpack(rown[...], atoms), unpack(yown[...], atoms), cown[...]
     for c in range(3):
-        at = slice(c * half, (c + 1) * half)
-        r, y, old = unpack(rown[at, :], atoms), unpack(yown[at, :], atoms), unpack(cown[at, :], atoms)
-        blocks[0, :, c, :] = dot32(inv1, r)
-        blocks[1, :, c, :] = dot32(weights, jnp.concatenate([y, r, old], axis=0))
+        parts = [component(part, c, vectors) for part in (y, r, old)]
+        blocks[0, c] = dot32(inv1, parts[1])
+        blocks[1, c] = dot32(weights, jnp.concatenate(parts, axis=0))
 
 
 def mates(count):
@@ -589,19 +641,33 @@
     sides = jnp.stack([at_x % 2, at_y % 2]).astype(jnp.int32)
     own_rows = 2 * half3 + 8
 
-    own = vmem_call(pack_kernel, f32(own_rows, lanes))(
-        block_cur, block_prev, positions, x_lists[0], y_lists[0]
-    )
-    from_mate = fetch(own, "gx", mate_x)
-    from_other = fetch(own, "gx", other_x)
-    own3 = jnp.stack([from_mate, own, from_other])
-    mate3 = fetch(own3, "gy", mate_y)
-    other3 = fetch(own3, "gy", other_y)
-
-    extent = pltpu.VMEM((extended, edges), jnp.bfloat16)
+    cur = block_cur.transpose(1, 0, 2).reshape(vec3, atoms)
+    prev = block_prev.transpose(1, 0, 2).reshape(vec3, atoms)
+    slab = f32(own_rows, lanes)
+    to_mate, to_other = vmem_call(select_x_kernel, [slab, slab], scalars=1)(
+        sides, cur, prev, positions, x_lists[0]
+    )
+    mate1 = fetch(to_mate, "gx", mate_x)
+    other1 = fetch(to_other, "gx", other_x)
+    dm, valid, rad_t, vec_t, mix_t, out_t = vmem_call(
+        prepare_kernel,
+        [
+            jax.ShapeDtypeStruct((extended, edges), jnp.bfloat16),
+            f32(8, edges),
+            f32(channels, basis),
+            f32(channels, basis),
+            f32(channels, channels),
+            f32(channels, 8),
+        ],
+        flops=1 << 24,
+    )(neighbours, counts[None], w_radial, w_vector, w_mix, w_out[None])
+    to_mate, to_other, wide = vmem_call(
+        select_y_kernel, [slab, slab, f32(2 * vec3 + 8, atoms + 2 * halo)], scalars=1
+    )(sides, cur, prev, positions, mate1, other1, y_lists[0])
+    mate2 = fetch(to_mate, "gy", mate_y)
+    other2 = fetch(to_other, "gy", other_y)
+
     work_scratch = [
-        extent,
-        pltpu.VMEM((vec3, 9 * atoms), jnp.float32),
         pltpu.VMEM((vec3, edges), jnp.float32),
         pltpu.VMEM((vec3, edges), jnp.float32),
         pltpu.VMEM((pairs, vectors, lanes), jnp.float32),
@@ -614,7 +680,7 @@
             f32(3 * half3, lanes),
             f32(3 * half3, lanes),
             f32(3 * half3, lanes),
-            f32(2 * vectors, lanes),
+            f32(vectors, lanes),
             f32(vec3, extended),
             f32(vec3, extended),
             jax.ShapeDtypeStruct((8, extended), jnp.int32),
@@ -634,7 +700,7 @@
         flops=1 << 31,
     )
     part_m, part_0, part_o, local, cext, pext, index, ef, ee, e8, pmat, rmat = first(
-        sides, own3, mate3, other3, neighbours, counts[None], w_radial, w_vector, w_mix, w_out[None]
+        sides, wide, mate2, other2, dm, valid, w_radial, w_vector, w_mix, rad_t, vec_t, mix_t, out_t
     )
 
     back_m = fetch(part_m, "gx", mate_x)
@@ -685,12 +751,13 @@
             f32(2 * vectors, lanes),
             f32(half3, lanes),
         ],
-        work_scratch + [pltpu.VMEM((4, 2 * vectors, lanes), jnp.float32)],
+        work_scratch
+        + [pltpu.VMEM((vec3, 9 * atoms), jnp.float32), pltpu.VMEM((4, vectors, lanes), jnp.float32)],
         scalars=1,
         flops=1 << 30,
     )
     part_m, part_0, part_o, shared, rown = second(
-        order, column, col_m, col_o, far, cext, pext, index, neighbours, ef, ee, e8, pmat, rmat
+        order, column, col_m, col_o, far, cext, pext, index, dm, ef, ee, e8, pmat, rmat
     )
     back_m = fetch(part_m, "gx", mate_x)
     back_o = fetch(part_o, "gx", other_x)
@@ -698,17 +765,17 @@
     y_m = fetch(folded[:half3], "gy", mate_y)
     y_o = fetch(folded[2 * half3 :], "gy", other_y)
 
-    devices = n_x * n_y
+    sent_rows = 2 * vectors * vectors // lanes
     spread, yown = vmem_call(
         functools.partial(gram_kernel, vectors=vectors, atoms=atoms),
-        [f32(devices, 2 * vectors, lanes), f32(half3, lanes)],
+        [f32(n_x * n_y, sent_rows, lanes), f32(half3, lanes)],
     )(rown, folded[half3 : 2 * half3], y_m, y_o)
     got = lax.all_to_all(spread, ("gx", "gy"), 0, 0)
     blocks, factors = vmem_call(
         functools.partial(final_kernel, vectors=vectors, atoms=atoms, total_rows=total_rows),
-        [f32(2, vectors, 3, atoms), f32(2, vectors, vectors)],
-    )(got, shared, rown, yown, own[:half3])
-    return blocks, factors
+        [f32(2, 3, vectors, atoms), f32(2, vectors, vectors)],
+    )(got, shared, rown, yown, cur)
+    return blocks.transpose(0, 2, 1, 3), factors
 
 
 def solution(mesh):

time: 116 us -> 103 us (0.89)
  waiting for transfers between devices: 54.9 us -> 22 us
  blocking collectives: 0 us -> 12.9 us
  local copies, waits for them, and re-layouts: 2.9 us -> 10.1 us
  starting transfers between devices: 23.9 us -> 20.6 us
  Pallas kernels: 33 us -> 35.5 us
    all_to_all x1 -> x0, waiting for transfers between devices: 26.4 us -> none  [shards(): got = lax.all_to_all(spread, ('gx', 'gy'), 0, 0)]
    all_to_all x0 -> x1, blocking collectives: none -> 12.9 us  [shards(): got = lax.all_to_all(spread, ('gx', 'gy'), 0, 0)]
    unnamed x22 -> x30, local copies, waits for them, and re-layouts: 2.23 us -> 10.1 us
    ppermute x17, waiting for transfers between devices: 28.5 us -> 22 us  [fetch(): return lax.ppermute(values, axis, [(s, i) for i, s in enumerate(sources)])]
    all_to_all x1 -> x0, starting transfers between devices: 2.64 us -> none  [shards(): got = lax.all_to_all(spread, ('gx', 'gy'), 0, 0)]
    pallas_call x5 -> x7, Pallas kernels: 33 us -> 35.5 us  [call(): pl.pallas_call(kernel, out_shape=outs, in_specs=[pl.BlockSpec(memory_spac...]
  transfers between devices with their start and end apart: 18 -> 17, of which waited for: 13 -> 11; matrix products, arithmetic and copies ran while one was open for 0% -> 0% of each run, Pallas kernels for 0% -> 1%
where the time goes in v1:
time: 103 us; the launch traced here: 102 us
  Pallas kernels  35.5 us (34%)
  waiting for transfers between devices  22 us (21%)
  starting transfers between devices  20.6 us (20%)
  blocking collectives  12.9 us (13%)
  local copies, waits for them, and re-layouts  10.1 us (10%)
    pallas_call x7, Pallas kernels, call(): pl.pallas_call(kernel, out_shape=outs, in_specs=[pl.BlockSpec(memory_spac...  35.5 us
    ppermute x17, waiting for transfers between devices, fetch(): return lax.ppermute(values, axis, [(s, i) for i, s in enumerate(sources)])  22 us
    ppermute x17, starting transfers between devices, fetch(): return lax.ppermute(values, axis, [(s, i) for i, s in enumerate(sources)])  20.6 us
    all_to_all x1, blocking collectives, shards(): got = lax.all_to_all(spread, ('gx', 'gy'), 0, 0)  12.9 us
    unnamed x30, local copies, waits for them, and re-layouts  10.1 us
  transfers between devices with their start and end apart: 17, of which 11 were waited for; matrix products, arithmetic and copies ran while one was open for 0% of the time, Pallas kernels for 1%

profile of v1, /device:TPU:0, one launch (start us, length us, event | category | flops | bytes accessed | tf_op | source)
XLA Modules:
  0.0 102.1 jit_solution(6764517023297293553)
XLA Ops:
  0.6 0.1 pad_add_fusion.1.sides
  0.7 0.8 copy-done
  1.5 0.8 copy-done.2
  2.3 0.7 copy-done.6
  3.0 0.7 copy-done.11
  3.7 0.9 shard_map.122
  4.6 0.5 collective-permute-start
  5.1 4.7 %collective-permute-start.1 = (f32[104,128]{1,0:T(8,128)S(1)}, f32[104,128]{1,0:T(8,128)S(1)}, u32[]{:S(2)}, u32[]{:S(2)}) collective-permute-start(f32[104,128]{1,0:T(8,128)S(1)} %get-tuple-element.35), channel_id=1, source_target_pairs={{28,0},{8,4},{4,8},{16,12},{12,16},{24,20},{20,24},{0,28},{29,1},{... | collective-permute-start | bytes 159752 | tf_op jit(solution)/shard_map/ppermute | solution.py:600
  9.8 1.9 %collective-permute-done.1.from_other = f32[104,128]{1,0:T(8,128)S(1)} collective-permute-done((f32[104,128]{1,0:T(8,128)S(1)}, f32[104,128]{1,0:T(8,128)S(1)}, u32[]{:S(2)}, u32[]{:S(2)}) %collective-permute-start.1) | collective-permute-done | bytes 53280 | tf_op jit(solution)/shard_map/ppermute | solution.py:600
  11.7 0.7 copy-done.12
  12.4 1.0 shard_map.123
  13.4 1.6 %collective-permute-start.2 = (f32[104,128]{1,0:T(8,128)S(1)}, f32[104,128]{1,0:T(8,128)S(1)}, u32[]{:S(2)}, u32[]{:S(2)}) collective-permute-start(f32[104,128]{1,0:T(8,128)S(1)} %get-tuple-element.37), channel_id=1, source_target_pairs={{1,0},{0,1},{3,2},{2,3},{5,4},{4,5},{7,6},{6,7},{9,8},{8,9},{11,10... | collective-permute-start | bytes 159752 | tf_op jit(solution)/shard_map/ppermute | solution.py:600
  14.9 1.5 %collective-permute-start.3 = (f32[104,128]{1,0:T(8,128)S(1)}, f32[104,128]{1,0:T(8,128)S(1)}, u32[]{:S(2)}, u32[]{:S(2)}) collective-permute-start(f32[104,128]{1,0:T(8,128)S(1)} %get-tuple-element.38), channel_id=1, source_target_pairs={{3,0},{2,1},{1,2},{0,3},{7,4},{6,5},{5,6},{4,7},{11,8},{10,9},{9,1... | collective-permute-start | bytes 159752 | tf_op jit(solution)/shard_map/ppermute | solution.py:600
  16.4 0.8 copy-done.3
  17.3 0.7 copy-done.5
  18.0 0.7 copy-done.7
  18.7 0.7 copy-done.9
  19.3 0.7 copy-done.13
  20.0 0.7 copy-done.14
  20.7 0.7 shard_map.124
  21.4 0.8 copy-done.4
  22.3 0.7 copy-done.8
  23.0 0.7 copy-done.10
  23.7 15.0 %shard_map.125 = (f32[144,128]{1,0:T(8,128)S(1)}, f32[144,128]{1,0:T(8,128)S(1)}, f32[144,128]{1,0:T(8,128)S(1)}, f32[32,128]{1,0:T(8,128)S(1)}, f32[96,320]{1,0...) custom-call(s32[2]{0:T(128)S(1)} %pad_add_fusion.1.sides, ...), custom_call_target="tpu_custom_call" | custom-call | flops 2147483648 | bytes 65536 | tf_op jit(solution)/shard_map/pallas_call | solution.py:606
  38.7 2.9 %collective-permute-start.5 = (f32[144,128]{1,0:T(8,128)S(1)}, f32[144,128]{1,0:T(8,128)S(1)}, u32[]{:S(2)}, u32[]{:S(2)}) collective-permute-start(f32[144,128]{1,0:T(8,128)S(1)} %get-tuple-element.47), channel_id=1, source_target_pairs={{28,0},{8,4},{4,8},{16,12},{12,16},{24,20},{20,24},{0,28},{29,1},{... | collective-permute-start | bytes 221192 | tf_op jit(solution)/shard_map/ppermute | solution.py:600
  41.6 4.6 %collective-permute-done.6 = f32[32,128]{1,0:T(8,128)S(1)} collective-permute-done((f32[32,128]{1,0:T(8,128)S(1)}, f32[32,128]{1,0:T(8,128)S(1)}, u32[]{:S(2)}, u32[]{:S(2)}) %collective-permute-start.6) | collective-permute-done | bytes 16416 | tf_op jit(solution)/shard_map/ppermute | solution.py:600
  46.4 1.6 %collective-permute-start.7 = (f32[128,128]{1,0:T(8,128)S(1)}, f32[128,128]{1,0:T(8,128)S(1)}, u32[]{:S(2)}, u32[]{:S(2)}) collective-permute-start(f32[128,128]{1,0:T(8,128)S(1)} %get-tuple-element.75), channel_id=1, source_target_pairs={{1,0},{0,1},{3,2},{2,3},{5,4},{4,5},{7,6},{6,7},{9,8},{8,9},{11,10... | collective-permute-start | bytes 196616 | tf_op jit(solution)/shard_map/ppermute | solution.py:600
  47.9 0.5 collective-permute-start.8
  48.4 1.5 %collective-permute-start.9 = (f32[128,128]{1,0:T(8,128)S(1)}, f32[128,128]{1,0:T(8,128)S(1)}, u32[]{:S(2)}, u32[]{:S(2)}) collective-permute-start(f32[128,128]{1,0:T(8,128)S(1)} %get-tuple-element.77), channel_id=1, source_target_pairs={{3,0},{2,1},{1,2},{0,3},{7,4},{6,5},{5,6},{4,7},{11,8},{10,9},{9,1... | collective-permute-start | bytes 196616 | tf_op jit(solution)/shard_map/ppermute | solution.py:600
  49.9 0.8 collective-permute-done.7
  50.7 1.5 %collective-permute-done.8 = f32[128,128]{1,0:T(8,128)S(1)} collective-permute-done((f32[128,128]{1,0:T(8,128)S(1)}, f32[128,128]{1,0:T(8,128)S(1)}, u32[]{:S(2)}, u32[]{:S(2)}) %collective-permute-start.8) | collective-permute-done | bytes 65568 | tf_op jit(solution)/shard_map/ppermute | solution.py:600
  52.2 1.4 %collective-permute-done.9 = f32[128,128]{1,0:T(8,128)S(1)} collective-permute-done((f32[128,128]{1,0:T(8,128)S(1)}, f32[128,128]{1,0:T(8,128)S(1)}, u32[]{:S(2)}, u32[]{:S(2)}) %collective-permute-start.9) | collective-permute-done | bytes 65568 | tf_op jit(solution)/shard_map/ppermute | solution.py:600
  53.6 1.0 collective-permute-start.12
  54.7 1.2 %collective-permute-start.10 = (f32[176,128]{1,0:T(8,128)S(1)}, f32[176,128]{1,0:T(8,128)S(1)}, u32[]{:S(2)}, u32[]{:S(2)}) collective-permute-start(f32[176,128]{1,0:T(8,128)S(1)} %pad_maximum_fusion.3.own), channel_id=1, source_target_pairs={{4,0},{0,4},{12,8},{8,12},{20,16},{16,20},{28,24},{24,28},{5,1},{1... | collective-permute-start | bytes 270344 | tf_op jit(solution)/shard_map/ppermute | solution.py:600
  55.9 0.1 pad_add_fusion.order
  56.0 1.4 %collective-permute-done.12.far = f32[32,128]{1,0:T(8,128)S(1)} collective-permute-done((f32[32,128]{1,0:T(8,128)S(1)}, f32[32,128]{1,0:T(8,128)S(1)}, u32[]{:S(2)}, u32[]{:S(2)}) %collective-permute-start.12) | collective-permute-done | bytes 16416 | tf_op jit(solution)/shard_map/ppermute | solution.py:600
  57.4 3.1 %collective-permute-done.11.other = f32[176,128]{1,0:T(8,128)S(1)} collective-permute-done((f32[176,128]{1,0:T(8,128)S(1)}, f32[176,128]{1,0:T(8,128)S(1)}, u32[]{:S(2)}, u32[]{:S(2)}) %collective-permute-start.11) | collective-permute-done | bytes 90144 | tf_op jit(solution)/shard_map/ppermute | solution.py:600
  60.5 9.4 %shard_map.126 = (f32[144,128]{1,0:T(8,128)S(1)}, f32[144,128]{1,0:T(8,128)S(1)}, f32[144,128]{1,0:T(8,128)S(1)}, f32[64,128]{1,0:T(8,128)S(1)}, f32[48,128]{1,0:T(8,128)S(1)}) custom-call(s32[4]{0:T(128)S(1)} %pad_add_fusion.order, f32[176,128]{1,0:T(8,128)S(1)} %pad_maximum_fusion.3.own, f32[176,128]{1,0:T(8,128)S(1)} %collective-permute-done.10.mate, ...), custom_call_target="tpu_custom_call" | custom-call | flops 1073741824 | bytes 65536 | tf_op jit(solution)/shard_map/pallas_call | solution.py:606
  69.9 0.7 collective-permute-start.14
  70.7 0.5 collective-permute-done.13
  71.2 4.4 %collective-permute-done.14 = f32[144,128]{1,0:T(8,128)S(1)} collective-permute-done((f32[144,128]{1,0:T(8,128)S(1)}, f32[144,128]{1,0:T(8,128)S(1)}, u32[]{:S(2)}, u32[]{:S(2)}) %collective-permute-start.14) | collective-permute-done | bytes 73760 | tf_op jit(solution)/shard_map/ppermute | solution.py:600
  75.6 1.3 %collective-permute-start.16 = (f32[48,128]{1,0:T(8,128)S(1)}, f32[48,128]{1,0:T(8,128)S(1)}, u32[]{:S(2)}, u32[]{:S(2)}) collective-permute-start(f32[48,128]{1,0:T(8,128)S(1)} %get-tuple-element.69), channel_id=1, source_target_pairs={{3,0},{2,1},{1,2},{0,3},{7,4},{6,5},{5,6},{4,7},{11,8},{10,9},{9,1... | collective-permute-start | bytes 73736 | tf_op jit(solution)/shard_map/ppermute | solution.py:600
  76.9 1.5 %collective-permute-start.15 = (f32[48,128]{1,0:T(8,128)S(1)}, f32[48,128]{1,0:T(8,128)S(1)}, u32[]{:S(2)}, u32[]{:S(2)}) collective-permute-start(f32[48,128]{1,0:T(8,128)S(1)} %get-tuple-element.70), channel_id=1, source_target_pairs={{1,0},{0,1},{3,2},{2,3},{5,4},{4,5},{7,6},{6,7},{9,8},{8,9},{11,10... | collective-permute-start | bytes 73736 | tf_op jit(solution)/shard_map/ppermute | solution.py:600
  78.4 2.0 %collective-permute-done.16.yo = f32[48,128]{1,0:T(8,128)S(1)} collective-permute-done((f32[48,128]{1,0:T(8,128)S(1)}, f32[48,128]{1,0:T(8,128)S(1)}, u32[]{:S(2)}, u32[]{:S(2)}) %collective-permute-start.16) | collective-permute-done | bytes 24608 | tf_op jit(solution)/shard_map/ppermute | solution.py:600
  80.4 0.3 collective-permute-done.15.ym
  80.7 0.4 shard_map.127
  81.1 12.9 %all_to_all.5.got = f32[32,16,128]{2,1,0:T(8,128)S(1)} all-to-all(f32[32,16,128]{2,1,0:T(8,128)S(1)} %get-tuple-element.61), channel_id=1, replica_groups=mesh['gx'=8,'gy'=4] {'gx','gy'}, dimensions={0} | all-to-all | bytes 524288 | tf_op jit(solution)/shard_map/all_to_all | solution.py:773
  94.0 8.1 %shard_map.128 = (f32[2,3,32,64]{3,2,1,0:T(8,128)}, f32[2,32,32]{2,1,0:T(8,128)}) custom-call(f32[32,16,128]{2,1,0:T(8,128)S(1)} %all_to_all.5.got, f32[64,128]{1,0:T(8,128)S(1)} %get-tuple-element.62.sums, f32[48,128]{1,0:T(8,128)S(1)} %get-tuple-element.57.rown, f32[48,128]{1,0:T(8,128)S(1)} %get-tuple-element.63.yown, f32[96,64]{1,0:T(8,128)S(1)} %bitcast.19), custom_call_target="tpu_custom_call" | custom-call | flops 1048576 | bytes 65536 | tf_op jit(solution)/shard_map/pallas_call | solution.py:606
  (36 shorter events, 0.3 us)
Async XLA Ops:
  0.7 0.8 copy-start
  1.5 0.8 copy-start.2
  2.3 0.7 copy-start.6
  3.0 0.7 copy-start.11
  4.6 5.2 %collective-permute-start = (f32[104,128]{1,0:T(8,128)S(1)}, f32[104,128]{1,0:T(8,128)S(1)}, u32[]{:S(2)}, u32[]{:S(2)}) collective-permute-start(f32[104,128]{1,0:T(8,128)S(1)} %get-tuple-element.34), channel_id=1, source_target_pairs={{4,0},{0,4},{12,8},{8,12},{20,16},{16,20},{28,24},{24,28},{5,1},{1... | collective-permute-start | bytes 159752 | tf_op jit(solution)/shard_map/ppermute | solution.py:600
  5.1 6.6 %collective-permute-start.1 = (f32[104,128]{1,0:T(8,128)S(1)}, f32[104,128]{1,0:T(8,128)S(1)}, u32[]{:S(2)}, u32[]{:S(2)}) collective-permute-start(f32[104,128]{1,0:T(8,128)S(1)} %get-tuple-element.35), channel_id=1, source_target_pairs={{28,0},{8,4},{4,8},{16,12},{12,16},{24,20},{20,24},{0,28},{29,1},{... | collective-permute-start | bytes 159752 | tf_op jit(solution)/shard_map/ppermute | solution.py:600
  11.7 0.7 copy-start.12
  13.4 8.1 %collective-permute-start.2 = (f32[104,128]{1,0:T(8,128)S(1)}, f32[104,128]{1,0:T(8,128)S(1)}, u32[]{:S(2)}, u32[]{:S(2)}) collective-permute-start(f32[104,128]{1,0:T(8,128)S(1)} %get-tuple-element.37), channel_id=1, source_target_pairs={{1,0},{0,1},{3,2},{2,3},{5,4},{4,5},{7,6},{6,7},{9,8},{8,9},{11,10... | collective-permute-start | bytes 159752 | tf_op jit(solution)/shard_map/ppermute | solution.py:600
  14.9 6.5 %collective-permute-start.3 = (f32[104,128]{1,0:T(8,128)S(1)}, f32[104,128]{1,0:T(8,128)S(1)}, u32[]{:S(2)}, u32[]{:S(2)}) collective-permute-start(f32[104,128]{1,0:T(8,128)S(1)} %get-tuple-element.38), channel_id=1, source_target_pairs={{3,0},{2,1},{1,2},{0,3},{7,4},{6,5},{5,6},{4,7},{11,8},{10,9},{9,1... | collective-permute-start | bytes 159752 | tf_op jit(solution)/shard_map/ppermute | solution.py:600
  16.4 0.8 copy-start.3
  17.3 0.7 copy-start.5
  18.0 0.7 copy-start.7
  18.7 0.7 copy-start.9
  19.3 0.7 copy-start.13
  20.0 0.7 copy-start.14
  21.4 0.8 copy-start.4
  22.3 0.7 copy-start.8
  23.0 0.7 copy-start.10
  38.6 7.6 %collective-permute-start.4 = (f32[144,128]{1,0:T(8,128)S(1)}, f32[144,128]{1,0:T(8,128)S(1)}, u32[]{:S(2)}, u32[]{:S(2)}) collective-permute-start(f32[144,128]{1,0:T(8,128)S(1)} %get-tuple-element.46), channel_id=1, source_target_pairs={{4,0},{0,4},{12,8},{8,12},{20,16},{16,20},{28,24},{24,28},{5,1},{1... | collective-permute-start | bytes 221192 | tf_op jit(solution)/shard_map/ppermute | solution.py:600
  38.7 7.6 %collective-permute-start.5 = (f32[144,128]{1,0:T(8,128)S(1)}, f32[144,128]{1,0:T(8,128)S(1)}, u32[]{:S(2)}, u32[]{:S(2)}) collective-permute-start(f32[144,128]{1,0:T(8,128)S(1)} %get-tuple-element.47), channel_id=1, source_target_pairs={{28,0},{8,4},{4,8},{16,12},{12,16},{24,20},{20,24},{0,28},{29,1},{... | collective-permute-start | bytes 221192 | tf_op jit(solution)/shard_map/ppermute | solution.py:600
  41.6 4.6 %collective-permute-start.6 = (f32[32,128]{1,0:T(8,128)S(1)}, f32[32,128]{1,0:T(8,128)S(1)}, u32[]{:S(2)}, u32[]{:S(2)}) collective-permute-start(f32[32,128]{1,0:T(8,128)S(1)} %get-tuple-element.48), channel_id=1, source_target_pairs={{16,0},{20,4},{24,8},{28,12},{0,16},{4,20},{8,24},{12,28},{17,1},{... | collective-permute-start | bytes 49160 | tf_op jit(solution)/shard_map/ppermute | solution.py:600
  46.4 4.3 %collective-permute-start.7 = (f32[128,128]{1,0:T(8,128)S(1)}, f32[128,128]{1,0:T(8,128)S(1)}, u32[]{:S(2)}, u32[]{:S(2)}) collective-permute-start(f32[128,128]{1,0:T(8,128)S(1)} %get-tuple-element.75), channel_id=1, source_target_pairs={{1,0},{0,1},{3,2},{2,3},{5,4},{4,5},{7,6},{6,7},{9,8},{8,9},{11,10... | collective-permute-start | bytes 196616 | tf_op jit(solution)/shard_map/ppermute | solution.py:600
  47.9 4.3 %collective-permute-start.8 = (f32[128,128]{1,0:T(8,128)S(1)}, f32[128,128]{1,0:T(8,128)S(1)}, u32[]{:S(2)}, u32[]{:S(2)}) collective-permute-start(f32[128,128]{1,0:T(8,128)S(1)} %get-tuple-element.76), channel_id=1, source_target_pairs={{2,0},{3,1},{0,2},{1,3},{6,4},{7,5},{4,6},{5,7},{10,8},{11,9},{8,1... | collective-permute-start | bytes 196616 | tf_op jit(solution)/shard_map/ppermute | solution.py:600
  48.4 5.2 %collective-permute-start.9 = (f32[128,128]{1,0:T(8,128)S(1)}, f32[128,128]{1,0:T(8,128)S(1)}, u32[]{:S(2)}, u32[]{:S(2)}) collective-permute-start(f32[128,128]{1,0:T(8,128)S(1)} %get-tuple-element.77), channel_id=1, source_target_pairs={{3,0},{2,1},{1,2},{0,3},{7,4},{6,5},{5,6},{4,7},{11,8},{10,9},{9,1... | collective-permute-start | bytes 196616 | tf_op jit(solution)/shard_map/ppermute | solution.py:600
  53.6 3.8 %collective-permute-start.12 = (f32[32,128]{1,0:T(8,128)S(1)}, f32[32,128]{1,0:T(8,128)S(1)}, u32[]{:S(2)}, u32[]{:S(2)}) collective-permute-start(f32[32,128]{1,0:T(8,128)S(1)} %fusion.1), channel_id=1, source_target_pairs={{8,0},{12,4},{16,8},{20,12},{24,16},{28,20},{0,24},{4,28},{9,1},{1... | collective-permute-start | bytes 49160 | tf_op jit(solution)/shard_map/ppermute | solution.py:600
  54.6 5.8 %collective-permute-start.11 = (f32[176,128]{1,0:T(8,128)S(1)}, f32[176,128]{1,0:T(8,128)S(1)}, u32[]{:S(2)}, u32[]{:S(2)}) collective-permute-start(f32[176,128]{1,0:T(8,128)S(1)} %pad_maximum_fusion.3.own), channel_id=1, source_target_pairs={{28,0},{8,4},{4,8},{16,12},{12,16},{24,20},{20,24},{0,28},{29,1},{... | collective-permute-start | bytes 270344 | tf_op jit(solution)/shard_map/ppermute | solution.py:600
  54.7 5.7 %collective-permute-start.10 = (f32[176,128]{1,0:T(8,128)S(1)}, f32[176,128]{1,0:T(8,128)S(1)}, u32[]{:S(2)}, u32[]{:S(2)}) collective-permute-start(f32[176,128]{1,0:T(8,128)S(1)} %pad_maximum_fusion.3.own), channel_id=1, source_target_pairs={{4,0},{0,4},{12,8},{8,12},{20,16},{16,20},{28,24},{24,28},{5,1},{1... | collective-permute-start | bytes 270344 | tf_op jit(solution)/shard_map/ppermute | solution.py:600
  60.5 33.5 %copy-start.1 = (f32[32,3,64]{2,0,1:T(8,128)S(1)}, f32[32,3,64]{2,0,1:T(8,128)}, u32[]{:S(2)}) copy-start(f32[32,3,64]{2,0,1:T(8,128)} %param.13) | copy-start | bytes 73732
  69.9 1.3 %collective-permute-start.13 = (f32[144,128]{1,0:T(8,128)S(1)}, f32[144,128]{1,0:T(8,128)S(1)}, u32[]{:S(2)}, u32[]{:S(2)}) collective-permute-start(f32[144,128]{1,0:T(8,128)S(1)} %get-tuple-element.59), channel_id=1, source_target_pairs={{4,0},{0,4},{12,8},{8,12},{20,16},{16,20},{28,24},{24,28},{5,1},{1... | collective-permute-start | bytes 221192 | tf_op jit(solution)/shard_map/ppermute | solution.py:600
  69.9 5.6 %collective-permute-start.14 = (f32[144,128]{1,0:T(8,128)S(1)}, f32[144,128]{1,0:T(8,128)S(1)}, u32[]{:S(2)}, u32[]{:S(2)}) collective-permute-start(f32[144,128]{1,0:T(8,128)S(1)} %get-tuple-element.60), channel_id=1, source_target_pairs={{28,0},{8,4},{4,8},{16,12},{12,16},{24,20},{20,24},{0,28},{29,1},{... | collective-permute-start | bytes 221192 | tf_op jit(solution)/shard_map/ppermute | solution.py:600
  75.6 4.8 %collective-permute-start.16 = (f32[48,128]{1,0:T(8,128)S(1)}, f32[48,128]{1,0:T(8,128)S(1)}, u32[]{:S(2)}, u32[]{:S(2)}) collective-permute-start(f32[48,128]{1,0:T(8,128)S(1)} %get-tuple-element.69), channel_id=1, source_target_pairs={{3,0},{2,1},{1,2},{0,3},{7,4},{6,5},{5,6},{4,7},{11,8},{10,9},{9,1... | collective-permute-start | bytes 73736 | tf_op jit(solution)/shard_map/ppermute | solution.py:600
  76.9 3.8 %collective-permute-start.15 = (f32[48,128]{1,0:T(8,128)S(1)}, f32[48,128]{1,0:T(8,128)S(1)}, u32[]{:S(2)}, u32[]{:S(2)}) collective-permute-start(f32[48,128]{1,0:T(8,128)S(1)} %get-tuple-element.70), channel_id=1, source_target_pairs={{1,0},{0,1},{3,2},{2,3},{5,4},{4,5},{7,6},{6,7},{9,8},{8,9},{11,10... | collective-permute-start | bytes 73736 | tf_op jit(solution)/shard_map/ppermute | solution.py:600

commit v2 on v1

--- a/solution.py
+++ b/solution.py
@@ -161,7 +161,7 @@
             return tuple(new)
 
         zero = jnp.zeros((8, lanes), jnp.float32)
-        acc = lax.fori_loop(0, groups, gather_step, (zero,) * (4 * basis))
+        acc = lax.fori_loop(0, groups, gather_step, (zero,) * (4 * basis), unroll=groups)
         for i in range(pairs):
             a, b = acc[i], acc[i + pairs]
             x = jnp.where(lower, a, b) + pltpu.roll(jnp.where(lower, b, a), atoms, 1)
@@ -182,7 +182,7 @@
         cs_ref[kappa + pairs] = jnp.where(wide_lower, turned, y)
         return carry
 
-    lax.fori_loop(0, pairs, mix_step, 0)
+    lax.fori_loop(0, pairs, mix_step, 0, unroll=4)
 
     for tile in range(tiles):
         coeff = [cs_ref[i, tile * 8 : tile * 8 + 8, :] for i in range(4 * basis)]
@@ -193,29 +193,43 @@
             row = [e8_ref[i : i + 1, at] for i in range(8)]
             head, turn = row[0:3], row[5:8]
             u = head[0] * m[0] + head[1] * m[1] + head[2] * m[2]
-            radial = jnp.zeros((8, lanes), jnp.float32)
-            sums = [radial, radial, radial]
-            evens = [radial, radial, radial]
+            radial = row[4] * u + (turn[0] * m[0] + turn[1] * m[1] + turn[2] * m[2])
+            sums, evens = [None] * 3, [None] * 3
             for k in range(basis):
                 slope = ef_ref[k : k + 1, at]
                 even = ee_ref[k : k + 1, at]
                 radial = radial + slope * coeff[k]
                 for c in range(3):
                     i = (c + 1) * basis + k
-                    sums[c] = sums[c] + slope * coeff[i]
-                    evens[c] = evens[c] + even * coeff[i]
-            inner = radial + row[4] * u
+                    more, plus = slope * coeff[i], even * coeff[i]
+                    sums[c] = more if k == 0 else sums[c] + more
+                    evens[c] = plus if k == 0 else evens[c] + plus
             for c in range(3):
-                inner = inner + head[c] * (sums[c] - evens[c]) + turn[c] * m[c]
+                radial = radial + head[c] * (sums[c] - evens[c])
             for c in range(3):
-                out = evens[c] + head[c] * inner + row[3] * m[c] + turn[c] * u
+                out = evens[c] + head[c] * radial + (row[3] * m[c] + turn[c] * u)
                 eo_ref[rows_of(tile, c) : rows_of(tile, c) + 8, at] = out
             return carry
 
-        lax.fori_loop(0, groups, spread_step, 0)
+        lax.fori_loop(0, groups, spread_step, 0, unroll=groups)
 
     spread = dot16(split(eo_ref[...], 2), dm_ref[...], NT)
     return spread[:vec3] + spread[vec3:]
+
+
+def stacked_sums(parts):
+    row = lax.broadcasted_iota(jnp.int32, parts[0].shape, 0)
+
+    def moved(values, by):
+        return values + pltpu.roll(values, by % 8, 0)
+
+    upper = row < 4
+    fours = [
+        jnp.where(upper, parts[i], parts[i + 4]) + pltpu.roll(jnp.where(upper, parts[i + 4], parts[i]), 4, 0)
+        for i in range(4)
+    ]
+    twos = [jnp.where(row % 4 < 2, moved(fours[i], -2), moved(fours[i + 2], 2)) for i in range(2)]
+    return jnp.where(row % 2 < 1, moved(twos[0], -1), moved(twos[1], 1))
 
 
 def store_patch(outs, extended_rows, pick, atoms):
@@ -231,12 +245,10 @@
             outs[x][y * half3 : (y + 1) * half3, atoms : 2 * atoms] = tile[half3:]
 
 
-def select_x_kernel(sides, cur, prev, pos, lists, to_mate, to_other):
-    half3 = cur.shape[0] // 2
-    atoms = cur.shape[1]
-    own = lax.broadcasted_iota(jnp.int32, (1, atoms), 1).astype(jnp.float32)
-    rows = jnp.concatenate([cur[...], prev[...], pos[...], own, jnp.zeros((4, atoms), jnp.float32)], axis=0)
-    emit(sides[0], rows, lists, to_mate, to_other, half3)
+def select_x_kernel(sides, table, to_mate, to_other):
+    rows = table[: table.shape[0] - 8, :]
+    lists = table[table.shape[0] - 8 :, :].astype(jnp.int32)
+    emit(sides[0], rows, lists[0:2], to_mate, to_other, (rows.shape[0] - 8) // 4)
 
 
 def emit(side, rows, lists, to_mate, to_other, half3):
@@ -268,29 +280,37 @@
     )
 
 
-def select_y_kernel(sides, cur, prev, pos, from_mate, from_other, lists, to_mate, to_other, wide):
-    half3 = cur.shape[0] // 2
-    atoms = cur.shape[1]
-    own = lax.broadcasted_iota(jnp.int32, (1, atoms), 1).astype(jnp.float32)
-    rows = jnp.concatenate([cur[...], prev[...], pos[...], own, jnp.zeros((4, atoms), jnp.float32)], axis=0)
-    rows = beside(rows, from_mate[...], from_other[...], sides[0] == 0, float(atoms), half3, lists.shape[1])
-    wide[...] = rows
-    emit(sides[1], rows, lists, to_mate, to_other, half3)
-
-
-def prepare_kernel(nb, count, w_rad, w_vec, w_mix, w_out, dm, valid, rad_t, vec_t, mix_t, out_t):
-    slots, atoms = nb.shape
+def select_y_kernel(sides, table, from_mate, from_other, to_mate, to_other, wide):
+    atoms = table.shape[1]
+    rows = table[: table.shape[0] - 8, :]
+    lists = table[table.shape[0] - 8 :, :].astype(jnp.int32)
+    half3 = (rows.shape[0] - 8) // 4
+    got = beside(rows, from_mate[...], from_other[...], sides[0] == 0, float(atoms), half3, atoms)
+    wide[...] = got
+    emit(sides[1], got, lists[2:4], to_mate, to_other, half3)
+
+
+def prepare_kernel(table, dm, valid, rad, vec, mix, rad_t, vec_t, mix_t, out_t, *, slots, atoms):
     lanes = 2 * atoms
-    difference_matrix(dm, nb[...], dm.shape[0], atoms)
+    basis, channels = rad.shape
+    starts = [0, channels, channels + basis, channels + 2 * basis, channels + 2 * basis + 8]
+    w_mix, w_rad, w_vec = (table[starts[i] : starts[i + 1], :] for i in range(3))
+    w_out = table[starts[3] : starts[4], :]
+    ints = table[starts[4] :, 0:atoms].astype(jnp.int32)
+    nb, count = ints[:slots], ints[slots : slots + 1]
+    difference_matrix(dm, nb, dm.shape[0], atoms)
     lane = lax.broadcasted_iota(jnp.int32, (8, lanes), 1)
     first = jnp.where(lane < atoms, 0, slots // 2)
-    limit = jnp.concatenate([count[...], count[...]], axis=1)
+    limit = jnp.concatenate([count, count], axis=1)
     for j in range(slots // 2):
         valid[:, j * lanes : (j + 1) * lanes] = (first + j < limit).astype(jnp.float32)
-    rad_t[...] = w_rad[...].T
-    vec_t[...] = w_vec[...].T
-    mix_t[...] = w_mix[...].T
-    out_t[...] = jnp.broadcast_to(w_out[...], (8, w_out.shape[1])).T
+    rad[...] = w_rad
+    vec[...] = w_vec
+    mix[...] = w_mix
+    rad_t[...] = w_rad.T
+    vec_t[...] = w_vec.T
+    mix_t[...] = w_mix.T
+    out_t[...] = w_out.T
 
 
 def difference_matrix(dm_ref, nb, extended, atoms):
@@ -351,13 +371,14 @@
         even1 = (slope_k - even_k) * inverse
         even2 = (second - 2.0 * even1) * inverse
 
-        def over(values):
-            return jnp.sum(values, axis=0, keepdims=True)
-
-        first = over(alpha * slope_k)
-        bend_r = over(alpha * second)
-        turn = [over(beta[c] * even1) for c in range(3)]
-        twist = [over(beta[c] * even2) for c in range(3)]
+        sums = stacked_sums(
+            [alpha * slope_k, alpha * second]
+            + [beta[c] * even1 for c in range(3)]
+            + [beta[c] * even2 for c in range(3)]
+        )
+        first, bend_r = sums[0:1], sums[1:2]
+        turn = [sums[2 + c : 3 + c] for c in range(3)]
+        twist = [sums[5 + c : 6 + c] for c in range(3)]
         inv1 = inverse[0:1]
         h1 = [head[c][0:1] for c in range(3)]
         radius = 1.0 / inv1
@@ -367,7 +388,7 @@
         e8[:, at] = jnp.concatenate(h1 + [isotropic, radial] + turn, axis=0)
 
 
-def channel_lift(flow, rad_t, vec_t, mix_t, qs, lanes, atoms):
+def channel_lift(flow, rad_t, vec_t, mix_t, qs, qr, lanes, atoms):
     channels, basis = rad_t.shape
     lower = lax.broadcasted_iota(jnp.int32, (channels, lanes), 1) < atoms
     lift0 = 2.0 * jnp.where(lower, flow[0], flow[2])
@@ -378,34 +399,69 @@
             side = jnp.where(lower, jnp.broadcast_to(rad_t[:, k : k + 1], lower.shape), lift1 * vec_t[:, k : k + 1])
         else:
             side = lift0 * vec_t[:, k : k + 1]
-        qs[:, i * lanes : (i + 1) * lanes] = dot_split(mix_t, side)
-
-
-def descriptor_curvature(vec, u, bend, qs, pmat, rmat, lanes, atoms):
+        lifted = dot_split(mix_t, side)
+        qs[:, i * lanes : (i + 1) * lanes] = lifted
+        qr[:, i * lanes : (i + 1) * lanes] = pltpu.roll(lifted, atoms, 1)
+
+
+def descriptor_curvature(vec, u, bend, qs, qr, bd, both, pmat, rmat, lanes, atoms):
     basis = vec.shape[0]
     pairs = 2 * basis
-    both = [2.0 * dot32(vec * vec[k : k + 1, :], u) for k in range(basis)]
-    low_row = lax.broadcasted_iota(jnp.int32, (1, lanes), 1) < atoms
-    for i in range(pairs):
-        q_i = qs[:, i * lanes : (i + 1) * lanes] * bend
-        for k in range(i + 1):
-            q_k = qs[:, k * lanes : (k + 1) * lanes]
-            straight = jnp.sum(q_i * q_k, axis=0, keepdims=True)
-            crossed = jnp.sum(q_i * pltpu.roll(q_k, atoms, 1), axis=0, keepdims=True)
-            if (i < basis) == (k < basis):
-                extra = both[i % basis][k % basis : k % basis + 1, :]
-                straight = straight + (jnp.where(low_row, 0.0, extra) if i < basis else extra)
-            pmat[i * pairs + k : i * pairs + k + 1, :] = straight
-            rmat[i * pairs + k : i * pairs + k + 1, :] = crossed
-            if k < i:
-                pmat[k * pairs + i : k * pairs + i + 1, :] = straight
-                rmat[k * pairs + i : k * pairs + i + 1, :] = pltpu.roll(crossed, atoms, 1)
+    channels = bend.shape[0]
+    bd[...] = bend
+    low_row = lax.broadcasted_iota(jnp.int32, (basis, lanes), 1) < atoms
+    for k in range(basis):
+        both[k] = 2.0 * dot32(vec * vec[k : k + 1, :], u)
+
+    def block(i, column):
+        accs = None
+        for tile in range(channels // 8):
+            rows = slice(8 * tile, 8 * tile + 8)
+            weight = bd[rows, :]
+            left = [
+                qs[rows, pl.ds(pl.multiple_of((i + d) * lanes, lanes), lanes)] * weight for d in range(2)
+            ]
+            columns = [slice((column + k) * lanes, (column + k + 1) * lanes) for k in range(basis)]
+            right = [ref[rows, at] for ref in (qs, qr) for at in columns]
+            terms = [l * r for l in left for r in right]
+            accs = terms if accs is None else [a + t for a, t in zip(accs, terms)]
+        return [stacked_sums(accs[q * basis : (q + 1) * basis]) for q in range(4)]
+
+    def put(i, column, tiles):
+        for d in range(2):
+            at = pl.ds(pl.multiple_of((i + d) * pairs + column, basis), basis)
+            pmat[at, :] = tiles[2 * d]
+            rmat[at, :] = tiles[2 * d + 1]
+
+    def upper_step(step, carry):
+        i = 2 * step
+        tiles = block(i, 0)
+        for d in range(2):
+            tiles[2 * d] = tiles[2 * d] + jnp.where(low_row, 0.0, both[i + d])
+        put(i, 0, tiles)
+        return carry
+
+    def lower_step(step, carry):
+        i = 2 * step + basis
+        tiles = block(i, 0)
+        put(i, 0, tiles)
+        for d in range(2):
+            pmat[pl.ds(i + d, basis, pairs), :] = tiles[2 * d]
+            rmat[pl.ds(i + d, basis, pairs), :] = pltpu.roll(tiles[2 * d + 1], atoms, 1)
+        tiles = block(i, basis)
+        for d in range(2):
+            tiles[2 * d] = tiles[2 * d] + both[i + d - basis]
+        put(i, basis, tiles)
+        return carry
+
+    lax.fori_loop(0, basis // 2, upper_step, 0)
+    lax.fori_loop(0, basis // 2, lower_step, 0)
 
 
 def first_kernel(
     sides, wide, from_mate, from_other, dm, valid, w_rad, w_vec, w_mix, rad_t, vec_t, mix_t, out_t,
     out_m, out_o, out_x, sums, cext, pext, index, ef, ee, e8, pmat, rmat,
-    mv, eo, xs, sx, cs, f2s, hs, qs,
+    mv, eo, xs, sx, cs, f2s, hs, qs, qr, bd, both,
     *, vectors, atoms, halo,
 ):
     half3 = 3 * vectors // 2
@@ -437,8 +493,8 @@
     alpha = dot32(rad, u)
     beta = [2.0 * dot32(vec, flow[c] * u) for c in range(3)]
     edge_rows(alpha, beta, ef, ee, f2s, hs, e8, lanes)
-    channel_lift(flow, radt, vect, mixt, qs, lanes, atoms)
-    descriptor_curvature(vec, u, bend, qs, pmat, rmat, lanes, atoms)
+    channel_lift(flow, radt, vect, mixt, qs, qr, lanes, atoms)
+    descriptor_curvature(vec, u, bend, qs, qr, bd, both, pmat, rmat, lanes, atoms)
 
     result = apply_operator(None, dm, ef, ee, e8, pmat, rmat, mv, eo, xs, sx, cs, atoms, True)
     store_patch((out_m, out_o, out_x), result, pick_matrix(places, 9 * atoms), atoms)
@@ -522,72 +578,72 @@
     out[...] = jnp.broadcast_to(sent[None], out.shape)
 
 
-def cholesky(matrix):
+def cholesky(matrix, *extra):
     size = matrix.shape[0]
-    rows = lax.broadcasted_iota(jnp.int32, (size, 2 * size), 0)
-    lane = lax.broadcasted_iota(jnp.int32, (size, 2 * size), 1)
-    unit = (lane - size == rows).astype(jnp.float32)
-    work = jnp.concatenate([matrix, jnp.zeros_like(matrix)], axis=1) + unit
-    done = jnp.zeros_like(work)
-    for j in range(size):
-        line = work[j : j + 1, :]
-        pivot = work[j : j + 1, j : j + 1]
-        scale = lax.rsqrt(pivot)
-        scale = scale * (1.5 - 0.5 * pivot * scale * scale)
-        line = line * scale
-        column = work[:, j : j + 1] * scale
-        done = jnp.where(rows == j, line, done)
-        work = work - column * line
-    upper = jnp.where(lane >= rows, done, 0.0)[:, :size]
-    return upper, done[:, size:]
+    rows, cols = rows_and_cols(size)
+    unit = (rows == cols).astype(jnp.float32)
+    work = jnp.concatenate([matrix, unit, *extra], axis=1)
+    columns = [jnp.broadcast_to(matrix[:, k : k + 1], work.shape) for k in range(size)]
+    lines = []
+    for j in range(0, size, 2):
+        first, second = columns[j], columns[j + 1]
+        a, b, d = first[j : j + 1], first[j + 1 : j + 2], second[j + 1 : j + 2]
+        det = a * d - b * b
+        inverse = 1.0 / det
+        ai, bi, di = a * inverse, b * inverse, d * inverse
+        keep = (j + 2) // 8 * 8
+        for k in range(j + 2, size):
+            low = columns[k]
+            x0, x1 = low[j : j + 1], low[j + 1 : j + 2]
+            low = low[keep:] - (first[keep:] * (di * x0 - bi * x1) + second[keep:] * (ai * x1 - bi * x0))
+            columns[k] = jnp.concatenate([columns[k][:keep], low], axis=0) if keep else low
+        r0, r1 = work[j : j + 1], work[j + 1 : j + 2]
+        work = work - (first * (di * r0 - bi * r1) + second * (ai * r1 - bi * r0))
+        lines += [r0 * root_inverse(a), (r1 - (b / a) * r0) * root_inverse(det / a)]
+    done = jnp.concatenate(lines, axis=0)
+    upper = jnp.where(cols >= rows, done[:, :size], 0.0)
+    return [upper] + [done[:, i * size : (i + 1) * size] for i in range(1, 2 + len(extra))]
+
+
+def root_inverse(value):
+    guess = lax.rsqrt(value)
+    return guess * (1.5 - 0.5 * value * guess * guess)
 
 
 def final_kernel(got, sums, rown, yown, cown, blocks, factors, *, vectors, atoms, total_rows):
     devices = got.shape[0]
+    v = vectors
     total = got[0]
     for i in range(1, devices):
         total = total + got[i]
     total = total * (1.0 / total_rows)
-    v = vectors
     count = total.shape[0] // 2
     joined, held = unflatten(total[:count], v), unflatten(total[count:], v)
     rr, ry, yy = from_lower(joined), from_lower(held), from_upper(joined, held)
     shared = sums[...]
-    gram_old = shared[:, : 2 * v]
-    coef1 = shared[:, 2 * v : 3 * v]
-    rows = lax.broadcasted_iota(jnp.int32, (v, v), 0)
-    cols = lax.broadcasted_iota(jnp.int32, (v, v), 1)
+    gram_old, coef1 = shared[:, : 2 * v], shared[:, 2 * v : 3 * v]
+    rows, cols = rows_and_cols(v)
     unit = (rows == cols).astype(jnp.float32)
-
-    upper1, inv1 = cholesky(rr)
     left = coef1 - dot32(gram_old, coef1)
     wr = rr + dot32(coef1, left, TN)
-    coef_x = dot32(dot32(inv1, ry), inv1, NT)
-    coef_c = dot32(wr, inv1, NT)
-    cross = dot32(left[:v], inv1, NT)
-    yy1 = dot32(dot32(inv1, yy), inv1, NT)
-    coef2 = jnp.concatenate([coef_x, coef_c], axis=0)
-    basis = jnp.concatenate(
-        [
-            jnp.concatenate([-unit, cross.T], axis=1),
-            jnp.concatenate([cross, gram_old[:v, :v] - 2.0 * unit], axis=1),
-        ],
-        axis=0,
-    )
-    gram2 = yy1 + dot32(coef2, dot32(basis, coef2), TN)
+    fixed = yy + dot32(wr, dot32(gram_old[:v, :v] - 2.0 * unit, wr), TN)
+
+    upper1, inv1, along, cross = cholesky(rr, ry, left[:v].T)
+    mixed = dot32(cross, wr)
+    gram2 = fixed + dot32(
+        jnp.concatenate([along, mixed], axis=0), jnp.concatenate([mixed - along, along], axis=0), TN
+    )
     upper2, inv2 = cholesky(gram2)
-    by_x = dot32(inv2, coef_x, NT)
-    m_y = dot32(inv2, inv1)
-    m_r = -dot32(by_x, inv1)
-    m_c = -dot32(inv2, coef_c, NT)
-    weights = jnp.concatenate([m_y, m_r, m_c], axis=1)
     factors[0] = upper1.T
-    factors[1] = upper2.T
-    r, y, old = unpack(rown[...], atoms), unpack(yown[...], atoms), cown[...]
+    factors[1] = jnp.where(rows >= cols, dot32(inv1, upper2, NT), 0.0)
+    r, y, old = unpack(rown[...], atoms), unpack(yown[...], atoms), cown[0 : 3 * vectors, :]
+    back = dot32(along, inv1, TN)
+    weights = jnp.concatenate([-back, -wr.T], axis=1)
     for c in range(3):
-        parts = [component(part, c, vectors) for part in (y, r, old)]
-        blocks[0, c] = dot32(inv1, parts[1])
-        blocks[1, c] = dot32(weights, jnp.concatenate(parts, axis=0))
+        parts = [component(part, c, vectors) for part in (r, old)]
+        blocks[0, c] = dot32(inv1, parts[0])
+        rest = component(y, c, vectors) + dot32(weights, jnp.concatenate(parts, axis=0))
+        blocks[1, c] = dot32(inv2, rest)
 
 
 def mates(count):
@@ -600,7 +656,7 @@
     return lax.ppermute(values, axis, [(s, i) for i, s in enumerate(sources)])
 
 
-def vmem_call(kernel, outs, scratch=(), scalars=0, **cost):
+def vmem_call(kernel, outs, scratch=(), scalars=0, flops=1 << 20):
     def call(*operands):
         spaces = [pltpu.SMEM] * scalars + [pltpu.VMEM] * (len(operands) - scalars)
         return pl.pallas_call(
@@ -610,12 +666,20 @@
             out_specs=jax.tree.map(lambda _: pl.BlockSpec(memory_space=pltpu.VMEM), outs),
             scratch_shapes=list(scratch),
             compiler_params=pltpu.CompilerParams(vmem_limit_bytes=VMEM_BYTES),
-            cost_estimate=pl.CostEstimate(
-                flops=cost.get("flops", 1 << 20), bytes_accessed=1 << 16, transcendentals=0
-            ),
+            cost_estimate=pl.CostEstimate(flops=flops, bytes_accessed=1 << 16, transcendentals=0),
         )(*operands)
 
     return call
+
+
+def laid(shape, pieces):
+    total = None
+    for row, piece in pieces:
+        rows, lanes = piece.shape
+        edges = ((row, shape[0] - row - rows), (0, shape[1] - lanes))
+        placed = jnp.pad(piece, edges).astype(jnp.float32)
+        total = placed if total is None else total + placed
+    return total
 
 
 def f32(*shape):
@@ -644,26 +708,54 @@
     cur = block_cur.transpose(1, 0, 2).reshape(vec3, atoms)
     prev = block_prev.transpose(1, 0, 2).reshape(vec3, atoms)
     slab = f32(own_rows, lanes)
-    to_mate, to_other = vmem_call(select_x_kernel, [slab, slab], scalars=1)(
-        sides, cur, prev, positions, x_lists[0]
-    )
+    all_rows = 2 * vec3 + 8
+
+    counting = lax.broadcasted_iota(jnp.float32, (1, atoms), 1)
+    table = laid(
+        (all_rows + 8, atoms),
+        [
+            (0, cur),
+            (vec3, prev),
+            (2 * vec3, positions),
+            (2 * vec3 + 3, counting),
+            (all_rows, x_lists[0]),
+            (all_rows + 2, y_lists[0]),
+        ],
+    )
+    to_mate, to_other = vmem_call(select_x_kernel, [slab, slab], scalars=1)(sides, table)
     mate1 = fetch(to_mate, "gx", mate_x)
     other1 = fetch(to_other, "gx", other_x)
-    dm, valid, rad_t, vec_t, mix_t, out_t = vmem_call(
-        prepare_kernel,
+    after = channels + 2 * basis + 8
+    fixed = laid(
+        (after + slots + 8, channels),
+        [
+            (0, w_mix),
+            (channels, w_radial),
+            (channels + basis, w_vector),
+            (channels + 2 * basis, w_out[None]),
+            (after, neighbours),
+            (after + slots, counts[None]),
+        ],
+    )
+    rad_shape, mix_shape, turned_shape = f32(basis, channels), f32(channels, channels), f32(channels, basis)
+    dm, valid, rad, vec, mix, rad_t, vec_t, mix_t, out_t = vmem_call(
+        functools.partial(prepare_kernel, slots=slots, atoms=atoms),
         [
             jax.ShapeDtypeStruct((extended, edges), jnp.bfloat16),
             f32(8, edges),
-            f32(channels, basis),
-            f32(channels, basis),
-            f32(channels, channels),
+            rad_shape,
+            rad_shape,
+            mix_shape,
+            turned_shape,
+            turned_shape,
+            mix_shape,
             f32(channels, 8),
         ],
         flops=1 << 24,
-    )(neighbours, counts[None], w_radial, w_vector, w_mix, w_out[None])
+    )(fixed)
     to_mate, to_other, wide = vmem_call(
-        select_y_kernel, [slab, slab, f32(2 * vec3 + 8, atoms + 2 * halo)], scalars=1
-    )(sides, cur, prev, positions, mate1, other1, y_lists[0])
+        select_y_kernel, [slab, slab, f32(all_rows, atoms + 2 * halo)], scalars=1
+    )(sides, table, mate1, other1)
     mate2 = fetch(to_mate, "gy", mate_y)
     other2 = fetch(to_other, "gy", other_y)
 
@@ -695,12 +787,15 @@
             pltpu.VMEM((basis, edges), jnp.float32),
             pltpu.VMEM((32, edges), jnp.float32),
             pltpu.VMEM((channels, pairs * lanes), jnp.float32),
+            pltpu.VMEM((channels, pairs * lanes), jnp.float32),
+            pltpu.VMEM((channels, lanes), jnp.float32),
+            pltpu.VMEM((basis, basis, lanes), jnp.float32),
         ],
         scalars=1,
         flops=1 << 31,
     )
     part_m, part_0, part_o, local, cext, pext, index, ef, ee, e8, pmat, rmat = first(
-        sides, wide, mate2, other2, dm, valid, w_radial, w_vector, w_mix, rad_t, vec_t, mix_t, out_t
+        sides, wide, mate2, other2, dm, valid, rad, vec, mix, rad_t, vec_t, mix_t, out_t
     )
 
     back_m = fetch(part_m, "gx", mate_x)
@@ -774,7 +869,7 @@
     blocks, factors = vmem_call(
         functools.partial(final_kernel, vectors=vectors, atoms=atoms, total_rows=total_rows),
         [f32(2, 3, vectors, atoms), f32(2, vectors, vectors)],
-    )(got, shared, rown, yown, cur)
+    )(got, shared, rown, yown, table)
     return blocks.transpose(0, 2, 1, 3), factors
 
 

time: 103 us -> 83.6 us (0.81)
  Pallas kernels: 35.5 us -> 23.7 us
  local copies, waits for them, and re-layouts: 10.1 us -> 0.02 us
  waiting for transfers between devices: 22 us -> 24.7 us
  other arithmetic: 0.24 us -> 2.12 us
  starting transfers between devices: 20.6 us -> 19.3 us
    pallas_call x7, Pallas kernels: 35.5 us -> 23.7 us  [call(): pl.pallas_call(kernel, out_shape=outs, in_specs=[pl.BlockSpec(memory_spac...]
    unnamed x30 -> x0, local copies, waits for them, and re-layouts: 10.1 us -> none
    ppermute x17, waiting for transfers between devices: 22 us -> 24.7 us  [fetch(): return lax.ppermute(values, axis, [(s, i) for i, s in enumerate(sources)])]
    add x0 -> x2, other arithmetic: none -> 1.88 us  [laid(): total = placed if total is None else total + placed]
    ppermute x17, starting transfers between devices: 20.6 us -> 19.3 us  [fetch(): return lax.ppermute(values, axis, [(s, i) for i, s in enumerate(sources)])]
  transfers between devices with their start and end apart: 17 -> 17, of which waited for: 11 -> 12; matrix products, arithmetic and copies ran while one was open for 0% -> 1% of each run, Pallas kernels for 1% -> 1%
where the time goes in v2:
time: 83.6 us; the launch traced here: 83.4 us
  waiting for transfers between devices  24.7 us (30%)
  Pallas kernels  23.7 us (28%)
  starting transfers between devices  19.3 us (23%)
  blocking collectives  12.7 us (15%)
  other arithmetic  2.12 us (3%)
    ppermute x17, waiting for transfers between devices, fetch(): return lax.ppermute(values, axis, [(s, i) for i, s in enumerate(sources)])  24.7 us
    pallas_call x7, Pallas kernels, call(): pl.pallas_call(kernel, out_shape=outs, in_specs=[pl.BlockSpec(memory_spac...  23.7 us
    ppermute x17, starting transfers between devices, fetch(): return lax.ppermute(values, axis, [(s, i) for i, s in enumerate(sources)])  19.3 us
    all_to_all x1, blocking collectives, shards(): got = lax.all_to_all(spread, ('gx', 'gy'), 0, 0)  12.7 us
    add x2, other arithmetic, laid(): total = placed if total is None else total + placed  1.88 us
  transfers between devices with their start and end apart: 17, of which 12 were waited for; matrix products, arithmetic and copies ran while one was open for 1% of the time, Pallas kernels for 1%

profile of v2, /device:TPU:0, one launch (start us, length us, event | category | flops | bytes accessed | tf_op | source)
XLA Modules:
  0.0 83.4 jit_solution(3462197622587428431)
XLA Ops:
  0.6 0.1 pad_add_fusion.1.sides
  0.7 0.9 %convert_add_fusion.table.cown = f32[208,64]{1,0:T(8,128)S(1)} fusion(s32[2,64]{1,0:T(2,128)} %bitcast.19, s32[2,64]{1,0:T(2,128)} %bitcast.20, f32[208,64]{1,0:T(8,128)} %constant.57.clone.1, f32[3,64]{1,0:T(4,128)} %param.11, f32[96,64]{1,0:T(8,128)} %bitcast.17, f32[96,64]{1,0:T(8,128)} %bitcast.18), kind=kLoop, calls=%fused_computation.3 | loop fusion | flops 93184 | bytes 157440 | tf_op jit(solution)/shard_map/add | solution.py:681
  1.7 0.9 %shard_map.122 = (f32[104,128]{1,0:T(8,128)S(1)}, f32[104,128]{1,0:T(8,128)S(1)}) custom-call(s32[2]{0:T(128)S(1)} %pad_add_fusion.1.sides, f32[208,64]{1,0:T(8,128)S(1)} %convert_add_fusion.table.cown), custom_call_target="tpu_custom_call" | custom-call | flops 1048576 | bytes 65536 | tf_op jit(solution)/shard_map/pallas_call | solution.py:662
  2.6 0.5 collective-permute-start
  3.1 4.7 %collective-permute-start.1 = (f32[104,128]{1,0:T(8,128)S(1)}, f32[104,128]{1,0:T(8,128)S(1)}, u32[]{:S(2)}, u32[]{:S(2)}) collective-permute-start(f32[104,128]{1,0:T(8,128)S(1)} %get-tuple-element.38), channel_id=1, source_target_pairs={{28,0},{8,4},{4,8},{16,12},{12,16},{24,20},{20,24},{0,28},{29,1},{... | collective-permute-start | bytes 159752 | tf_op jit(solution)/shard_map/ppermute | solution.py:656
  7.8 0.0 collective-permute-done.from_mate
  7.8 1.9 %collective-permute-done.1.from_other = f32[104,128]{1,0:T(8,128)S(1)} collective-permute-done((f32[104,128]{1,0:T(8,128)S(1)}, f32[104,128]{1,0:T(8,128)S(1)}, u32[]{:S(2)}, u32[]{:S(2)}) %collective-permute-start.1) | collective-permute-done | bytes 53280 | tf_op jit(solution)/shard_map/ppermute | solution.py:656
  9.7 1.0 %shard_map.123 = (f32[104,128]{1,0:T(8,128)S(1)}, f32[104,128]{1,0:T(8,128)S(1)}, f32[200,192]{1,0:T(8,128)S(1)}) custom-call(s32[2]{0:T(128)S(1)} %pad_add_fusion.1.sides, f32[208,64]{1,0:T(8,128)S(1)} %convert_add_fusion.table.cown, f32[104,128]{1,0:T(8,128)S(1)} %collective-permute-done.from_mate, f32[104,128]{1,0:T(8,128)S(1)} %collective-permute-done.1.from_other), custom_call_target="tpu_custom_call" | custom-call | flops 1048576 | bytes 65536 | tf_op jit(solution)/shard_map/pallas_call | solution.py:662
  10.7 1.6 %collective-permute-start.2 = (f32[104,128]{1,0:T(8,128)S(1)}, f32[104,128]{1,0:T(8,128)S(1)}, u32[]{:S(2)}, u32[]{:S(2)}) collective-permute-start(f32[104,128]{1,0:T(8,128)S(1)} %get-tuple-element.40), channel_id=1, source_target_pairs={{1,0},{0,1},{3,2},{2,3},{5,4},{4,5},{7,6},{6,7},{9,8},{8,9},{11,10... | collective-permute-start | bytes 159752 | tf_op jit(solution)/shard_map/ppermute | solution.py:656
  12.2 1.5 %collective-permute-start.3 = (f32[104,128]{1,0:T(8,128)S(1)}, f32[104,128]{1,0:T(8,128)S(1)}, u32[]{:S(2)}, u32[]{:S(2)}) collective-permute-start(f32[104,128]{1,0:T(8,128)S(1)} %get-tuple-element.41), channel_id=1, source_target_pairs={{3,0},{2,1},{1,2},{0,3},{7,4},{6,5},{5,6},{4,7},{11,8},{10,9},{9,1... | collective-permute-start | bytes 159752 | tf_op jit(solution)/shard_map/ppermute | solution.py:656
  13.7 0.9 %convert_add_fusion.1.table = f32[192,128]{1,0:T(8,128)S(1)} fusion(s32[1,64]{1,0:T(1,128)} %bitcast.21, s32[32,64]{1,0:T(8,128)} %param.14, f32[1,128]{1,0:T(1,128)} %bitcast.22, f32[8,128]{1,0:T(8,128)} %param.19, f32[8,128]{1,0:T(8,128)} %param.18, f32[128,128]{1,0:T(8,128)} %param.20), kind=kLoop, calls=%fused_computation.4 | loop fusion | flops 172032 | bytes 180992 | tf_op jit(solution)/shard_map/add | solution.py:681
  14.7 0.7 shard_map.124
  15.4 0.0 collective-permute-done.2.from_mate
  15.4 1.9 %collective-permute-done.3.from_other = f32[104,128]{1,0:T(8,128)S(1)} collective-permute-done((f32[104,128]{1,0:T(8,128)S(1)}, f32[104,128]{1,0:T(8,128)S(1)}, u32[]{:S(2)}, u32[]{:S(2)}) %collective-permute-start.3) | collective-permute-done | bytes 53280 | tf_op jit(solution)/shard_map/ppermute | solution.py:656
  17.3 10.7 %shard_map.125 = (f32[144,128]{1,0:T(8,128)S(1)}, f32[144,128]{1,0:T(8,128)S(1)}, f32[144,128]{1,0:T(8,128)S(1)}, f32[32,128]{1,0:T(8,128)S(1)}, f32[96,320]{1,0...) custom-call(s32[2]{0:T(128)S(1)} %pad_add_fusion.1.sides, ...), custom_call_target="tpu_custom_call" | custom-call | flops 2147483648 | bytes 65536 | tf_op jit(solution)/shard_map/pallas_call | solution.py:662
  28.0 0.0 collective-permute-start.4
  28.0 2.1 %collective-permute-start.5 = (f32[144,128]{1,0:T(8,128)S(1)}, f32[144,128]{1,0:T(8,128)S(1)}, u32[]{:S(2)}, u32[]{:S(2)}) collective-permute-start(f32[144,128]{1,0:T(8,128)S(1)} %get-tuple-element.53), channel_id=1, source_target_pairs={{28,0},{8,4},{4,8},{16,12},{12,16},{24,20},{20,24},{0,28},{29,1},{... | collective-permute-start | bytes 221192 | tf_op jit(solution)/shard_map/ppermute | solution.py:656
  30.1 0.0 collective-permute-start.6
  30.1 4.6 %collective-permute-done.6 = f32[32,128]{1,0:T(8,128)S(1)} collective-permute-done((f32[32,128]{1,0:T(8,128)S(1)}, f32[32,128]{1,0:T(8,128)S(1)}, u32[]{:S(2)}, u32[]{:S(2)}) %collective-permute-start.6) | collective-permute-done | bytes 16416 | tf_op jit(solution)/shard_map/ppermute | solution.py:656
  34.7 0.0 collective-permute-done.4
  34.8 0.0 collective-permute-done.5
  34.8 1.0 %collective-permute-start.7 = (f32[128,128]{1,0:T(8,128)S(1)}, f32[128,128]{1,0:T(8,128)S(1)}, u32[]{:S(2)}, u32[]{:S(2)}) collective-permute-start(f32[128,128]{1,0:T(8,128)S(1)} %get-tuple-element.81), channel_id=1, source_target_pairs={{1,0},{0,1},{3,2},{2,3},{5,4},{4,5},{7,6},{6,7},{9,8},{8,9},{11,10... | collective-permute-start | bytes 196616 | tf_op jit(solution)/shard_map/ppermute | solution.py:656
  35.8 1.1 %collective-permute-start.8 = (f32[128,128]{1,0:T(8,128)S(1)}, f32[128,128]{1,0:T(8,128)S(1)}, u32[]{:S(2)}, u32[]{:S(2)}) collective-permute-start(f32[128,128]{1,0:T(8,128)S(1)} %get-tuple-element.82), channel_id=1, source_target_pairs={{2,0},{3,1},{0,2},{1,3},{6,4},{7,5},{4,6},{5,7},{10,8},{11,9},{8,1... | collective-permute-start | bytes 196616 | tf_op jit(solution)/shard_map/ppermute | solution.py:656
  36.9 1.5 %collective-permute-start.9 = (f32[128,128]{1,0:T(8,128)S(1)}, f32[128,128]{1,0:T(8,128)S(1)}, u32[]{:S(2)}, u32[]{:S(2)}) collective-permute-start(f32[128,128]{1,0:T(8,128)S(1)} %get-tuple-element.83), channel_id=1, source_target_pairs={{3,0},{2,1},{1,2},{0,3},{7,4},{6,5},{5,6},{4,7},{11,8},{10,9},{9,1... | collective-permute-start | bytes 196616 | tf_op jit(solution)/shard_map/ppermute | solution.py:656
  38.4 0.8 collective-permute-done.7
  39.2 0.9 %collective-permute-done.8 = f32[128,128]{1,0:T(8,128)S(1)} collective-permute-done((f32[128,128]{1,0:T(8,128)S(1)}, f32[128,128]{1,0:T(8,128)S(1)}, u32[]{:S(2)}, u32[]{:S(2)}) %collective-permute-start.8) | collective-permute-done | bytes 65568 | tf_op jit(solution)/shard_map/ppermute | solution.py:656
  40.1 2.0 %collective-permute-done.9 = f32[128,128]{1,0:T(8,128)S(1)} collective-permute-done((f32[128,128]{1,0:T(8,128)S(1)}, f32[128,128]{1,0:T(8,128)S(1)}, u32[]{:S(2)}, u32[]{:S(2)}) %collective-permute-start.9) | collective-permute-done | bytes 65568 | tf_op jit(solution)/shard_map/ppermute | solution.py:656
  42.1 1.2 %collective-permute-start.12 = (f32[32,128]{1,0:T(8,128)S(1)}, f32[32,128]{1,0:T(8,128)S(1)}, u32[]{:S(2)}, u32[]{:S(2)}) collective-permute-start(f32[32,128]{1,0:T(8,128)S(1)} %fusion.1), channel_id=1, source_target_pairs={{8,0},{12,4},{16,8},{20,12},{24,16},{28,20},{0,24},{4,28},{9,1},{1... | collective-permute-start | bytes 49160 | tf_op jit(solution)/shard_map/ppermute | solution.py:656
  43.4 0.1 collective-permute-start.11
  43.5 1.1 %collective-permute-start.10 = (f32[176,128]{1,0:T(8,128)S(1)}, f32[176,128]{1,0:T(8,128)S(1)}, u32[]{:S(2)}, u32[]{:S(2)}) collective-permute-start(f32[176,128]{1,0:T(8,128)S(1)} %pad_maximum_fusion.3.own), channel_id=1, source_target_pairs={{4,0},{0,4},{12,8},{8,12},{20,16},{16,20},{28,24},{24,28},{5,1},{1... | collective-permute-start | bytes 270344 | tf_op jit(solution)/shard_map/ppermute | solution.py:656
  44.6 0.1 pad_add_fusion.order
  44.7 1.4 %collective-permute-done.12.far = f32[32,128]{1,0:T(8,128)S(1)} collective-permute-done((f32[32,128]{1,0:T(8,128)S(1)}, f32[32,128]{1,0:T(8,128)S(1)}, u32[]{:S(2)}, u32[]{:S(2)}) %collective-permute-start.12) | collective-permute-done | bytes 16416 | tf_op jit(solution)/shard_map/ppermute | solution.py:656
  46.1 3.1 %collective-permute-done.11.other = f32[176,128]{1,0:T(8,128)S(1)} collective-permute-done((f32[176,128]{1,0:T(8,128)S(1)}, f32[176,128]{1,0:T(8,128)S(1)}, u32[]{:S(2)}, u32[]{:S(2)}) %collective-permute-start.11) | collective-permute-done | bytes 90144 | tf_op jit(solution)/shard_map/ppermute | solution.py:656
  49.2 0.0 collective-permute-done.10.mate
  49.2 6.2 %shard_map.126 = (f32[144,128]{1,0:T(8,128)S(1)}, f32[144,128]{1,0:T(8,128)S(1)}, f32[144,128]{1,0:T(8,128)S(1)}, f32[64,128]{1,0:T(8,128)S(1)}, f32[48,128]{1,0:T(8,128)S(1)}) custom-call(s32[4]{0:T(128)S(1)} %pad_add_fusion.order, f32[176,128]{1,0:T(8,128)S(1)} %pad_maximum_fusion.3.own, f32[176,128]{1,0:T(8,128)S(1)} %collective-permute-done.10.mate, ...), custom_call_target="tpu_custom_call" | custom-call | flops 1073741824 | bytes 65536 | tf_op jit(solution)/shard_map/pallas_call | solution.py:662
  55.4 0.1 collective-permute-start.13
  55.5 0.8 collective-permute-start.14
  56.3 0.4 collective-permute-done.13
  56.7 4.4 %collective-permute-done.14 = f32[144,128]{1,0:T(8,128)S(1)} collective-permute-done((f32[144,128]{1,0:T(8,128)S(1)}, f32[144,128]{1,0:T(8,128)S(1)}, u32[]{:S(2)}, u32[]{:S(2)}) %collective-permute-start.14) | collective-permute-done | bytes 73760 | tf_op jit(solution)/shard_map/ppermute | solution.py:656
  61.2 1.5 %collective-permute-start.16 = (f32[48,128]{1,0:T(8,128)S(1)}, f32[48,128]{1,0:T(8,128)S(1)}, u32[]{:S(2)}, u32[]{:S(2)}) collective-permute-start(f32[48,128]{1,0:T(8,128)S(1)} %get-tuple-element.75), channel_id=1, source_target_pairs={{3,0},{2,1},{1,2},{0,3},{7,4},{6,5},{5,6},{4,7},{11,8},{10,9},{9,1... | collective-permute-start | bytes 73736 | tf_op jit(solution)/shard_map/ppermute | solution.py:656
  62.6 0.6 collective-permute-start.15
  63.2 2.7 %collective-permute-done.16.yo = f32[48,128]{1,0:T(8,128)S(1)} collective-permute-done((f32[48,128]{1,0:T(8,128)S(1)}, f32[48,128]{1,0:T(8,128)S(1)}, u32[]{:S(2)}, u32[]{:S(2)}) %collective-permute-start.16) | collective-permute-done | bytes 24608 | tf_op jit(solution)/shard_map/ppermute | solution.py:656
  66.0 0.5 collective-permute-done.15.ym
  66.5 0.4 shard_map.127
  66.9 12.7 %all_to_all.5.got = f32[32,16,128]{2,1,0:T(8,128)S(1)} all-to-all(f32[32,16,128]{2,1,0:T(8,128)S(1)} %get-tuple-element.67), channel_id=1, replica_groups=mesh['gx'=8,'gy'=4] {'gx','gy'}, dimensions={0} | all-to-all | bytes 524288 | tf_op jit(solution)/shard_map/all_to_all | solution.py:868
  79.5 3.9 %shard_map.128 = (f32[2,3,32,64]{3,2,1,0:T(8,128)}, f32[2,32,32]{2,1,0:T(8,128)}) custom-call(f32[32,16,128]{2,1,0:T(8,128)S(1)} %all_to_all.5.got, f32[64,128]{1,0:T(8,128)S(1)} %get-tuple-element.68.sums, f32[48,128]{1,0:T(8,128)S(1)} %get-tuple-element.63.rown, f32[48,128]{1,0:T(8,128)S(1)} %get-tuple-element.69.yown, ...), custom_call_target="tpu_custom_call" | custom-call | flops 1048576 | bytes 65536 | tf_op jit(solution)/shard_map/pallas_call | solution.py:662
  (10 shorter events, 0.1 us)
Async XLA Ops:
  2.6 5.2 %collective-permute-start = (f32[104,128]{1,0:T(8,128)S(1)}, f32[104,128]{1,0:T(8,128)S(1)}, u32[]{:S(2)}, u32[]{:S(2)}) collective-permute-start(f32[104,128]{1,0:T(8,128)S(1)} %get-tuple-element.37), channel_id=1, source_target_pairs={{4,0},{0,4},{12,8},{8,12},{20,16},{16,20},{28,24},{24,28},{5,1},{1... | collective-permute-start | bytes 159752 | tf_op jit(solution)/shard_map/ppermute | solution.py:656
  3.1 6.6 %collective-permute-start.1 = (f32[104,128]{1,0:T(8,128)S(1)}, f32[104,128]{1,0:T(8,128)S(1)}, u32[]{:S(2)}, u32[]{:S(2)}) collective-permute-start(f32[104,128]{1,0:T(8,128)S(1)} %get-tuple-element.38), channel_id=1, source_target_pairs={{28,0},{8,4},{4,8},{16,12},{12,16},{24,20},{20,24},{0,28},{29,1},{... | collective-permute-start | bytes 159752 | tf_op jit(solution)/shard_map/ppermute | solution.py:656
  10.7 4.7 %collective-permute-start.2 = (f32[104,128]{1,0:T(8,128)S(1)}, f32[104,128]{1,0:T(8,128)S(1)}, u32[]{:S(2)}, u32[]{:S(2)}) collective-permute-start(f32[104,128]{1,0:T(8,128)S(1)} %get-tuple-element.40), channel_id=1, source_target_pairs={{1,0},{0,1},{3,2},{2,3},{5,4},{4,5},{7,6},{6,7},{9,8},{8,9},{11,10... | collective-permute-start | bytes 159752 | tf_op jit(solution)/shard_map/ppermute | solution.py:656
  12.2 5.0 %collective-permute-start.3 = (f32[104,128]{1,0:T(8,128)S(1)}, f32[104,128]{1,0:T(8,128)S(1)}, u32[]{:S(2)}, u32[]{:S(2)}) collective-permute-start(f32[104,128]{1,0:T(8,128)S(1)} %get-tuple-element.41), channel_id=1, source_target_pairs={{3,0},{2,1},{1,2},{0,3},{7,4},{6,5},{5,6},{4,7},{11,8},{10,9},{9,1... | collective-permute-start | bytes 159752 | tf_op jit(solution)/shard_map/ppermute | solution.py:656
  28.0 6.8 %collective-permute-start.4 = (f32[144,128]{1,0:T(8,128)S(1)}, f32[144,128]{1,0:T(8,128)S(1)}, u32[]{:S(2)}, u32[]{:S(2)}) collective-permute-start(f32[144,128]{1,0:T(8,128)S(1)} %get-tuple-element.52), channel_id=1, source_target_pairs={{4,0},{0,4},{12,8},{8,12},{20,16},{16,20},{28,24},{24,28},{5,1},{1... | collective-permute-start | bytes 221192 | tf_op jit(solution)/shard_map/ppermute | solution.py:656
  28.0 6.7 %collective-permute-start.5 = (f32[144,128]{1,0:T(8,128)S(1)}, f32[144,128]{1,0:T(8,128)S(1)}, u32[]{:S(2)}, u32[]{:S(2)}) collective-permute-start(f32[144,128]{1,0:T(8,128)S(1)} %get-tuple-element.53), channel_id=1, source_target_pairs={{28,0},{8,4},{4,8},{16,12},{12,16},{24,20},{20,24},{0,28},{29,1},{... | collective-permute-start | bytes 221192 | tf_op jit(solution)/shard_map/ppermute | solution.py:656
  30.1 4.6 %collective-permute-start.6 = (f32[32,128]{1,0:T(8,128)S(1)}, f32[32,128]{1,0:T(8,128)S(1)}, u32[]{:S(2)}, u32[]{:S(2)}) collective-permute-start(f32[32,128]{1,0:T(8,128)S(1)} %get-tuple-element.54), channel_id=1, source_target_pairs={{16,0},{20,4},{24,8},{28,12},{0,16},{4,20},{8,24},{12,28},{17,1},{... | collective-permute-start | bytes 49160 | tf_op jit(solution)/shard_map/ppermute | solution.py:656
  34.8 4.3 %collective-permute-start.7 = (f32[128,128]{1,0:T(8,128)S(1)}, f32[128,128]{1,0:T(8,128)S(1)}, u32[]{:S(2)}, u32[]{:S(2)}) collective-permute-start(f32[128,128]{1,0:T(8,128)S(1)} %get-tuple-element.81), channel_id=1, source_target_pairs={{1,0},{0,1},{3,2},{2,3},{5,4},{4,5},{7,6},{6,7},{9,8},{8,9},{11,10... | collective-permute-start | bytes 196616 | tf_op jit(solution)/shard_map/ppermute | solution.py:656
  35.8 4.3 %collective-permute-start.8 = (f32[128,128]{1,0:T(8,128)S(1)}, f32[128,128]{1,0:T(8,128)S(1)}, u32[]{:S(2)}, u32[]{:S(2)}) collective-permute-start(f32[128,128]{1,0:T(8,128)S(1)} %get-tuple-element.82), channel_id=1, source_target_pairs={{2,0},{3,1},{0,2},{1,3},{6,4},{7,5},{4,6},{5,7},{10,8},{11,9},{8,1... | collective-permute-start | bytes 196616 | tf_op jit(solution)/shard_map/ppermute | solution.py:656
  36.9 5.2 %collective-permute-start.9 = (f32[128,128]{1,0:T(8,128)S(1)}, f32[128,128]{1,0:T(8,128)S(1)}, u32[]{:S(2)}, u32[]{:S(2)}) collective-permute-start(f32[128,128]{1,0:T(8,128)S(1)} %get-tuple-element.83), channel_id=1, source_target_pairs={{3,0},{2,1},{1,2},{0,3},{7,4},{6,5},{5,6},{4,7},{11,8},{10,9},{9,1... | collective-permute-start | bytes 196616 | tf_op jit(solution)/shard_map/ppermute | solution.py:656
  42.1 4.0 %collective-permute-start.12 = (f32[32,128]{1,0:T(8,128)S(1)}, f32[32,128]{1,0:T(8,128)S(1)}, u32[]{:S(2)}, u32[]{:S(2)}) collective-permute-start(f32[32,128]{1,0:T(8,128)S(1)} %fusion.1), channel_id=1, source_target_pairs={{8,0},{12,4},{16,8},{20,12},{24,16},{28,20},{0,24},{4,28},{9,1},{1... | collective-permute-start | bytes 49160 | tf_op jit(solution)/shard_map/ppermute | solution.py:656
  43.4 5.8 %collective-permute-start.11 = (f32[176,128]{1,0:T(8,128)S(1)}, f32[176,128]{1,0:T(8,128)S(1)}, u32[]{:S(2)}, u32[]{:S(2)}) collective-permute-start(f32[176,128]{1,0:T(8,128)S(1)} %pad_maximum_fusion.3.own), channel_id=1, source_target_pairs={{28,0},{8,4},{4,8},{16,12},{12,16},{24,20},{20,24},{0,28},{29,1},{... | collective-permute-start | bytes 270344 | tf_op jit(solution)/shard_map/ppermute | solution.py:656
  43.5 5.7 %collective-permute-start.10 = (f32[176,128]{1,0:T(8,128)S(1)}, f32[176,128]{1,0:T(8,128)S(1)}, u32[]{:S(2)}, u32[]{:S(2)}) collective-permute-start(f32[176,128]{1,0:T(8,128)S(1)} %pad_maximum_fusion.3.own), channel_id=1, source_target_pairs={{4,0},{0,4},{12,8},{8,12},{20,16},{16,20},{28,24},{24,28},{5,1},{1... | collective-permute-start | bytes 270344 | tf_op jit(solution)/shard_map/ppermute | solution.py:656
  55.4 1.3 %collective-permute-start.13 = (f32[144,128]{1,0:T(8,128)S(1)}, f32[144,128]{1,0:T(8,128)S(1)}, u32[]{:S(2)}, u32[]{:S(2)}) collective-permute-start(f32[144,128]{1,0:T(8,128)S(1)} %get-tuple-element.65), channel_id=1, source_target_pairs={{4,0},{0,4},{12,8},{8,12},{20,16},{16,20},{28,24},{24,28},{5,1},{1... | collective-permute-start | bytes 221192 | tf_op jit(solution)/shard_map/ppermute | solution.py:656
  55.5 5.6 %collective-permute-start.14 = (f32[144,128]{1,0:T(8,128)S(1)}, f32[144,128]{1,0:T(8,128)S(1)}, u32[]{:S(2)}, u32[]{:S(2)}) collective-permute-start(f32[144,128]{1,0:T(8,128)S(1)} %get-tuple-element.66), channel_id=1, source_target_pairs={{28,0},{8,4},{4,8},{16,12},{12,16},{24,20},{20,24},{0,28},{29,1},{... | collective-permute-start | bytes 221192 | tf_op jit(solution)/shard_map/ppermute | solution.py:656
  61.2 4.8 %collective-permute-start.16 = (f32[48,128]{1,0:T(8,128)S(1)}, f32[48,128]{1,0:T(8,128)S(1)}, u32[]{:S(2)}, u32[]{:S(2)}) collective-permute-start(f32[48,128]{1,0:T(8,128)S(1)} %get-tuple-element.75), channel_id=1, source_target_pairs={{3,0},{2,1},{1,2},{0,3},{7,4},{6,5},{5,6},{4,7},{11,8},{10,9},{9,1... | collective-permute-start | bytes 73736 | tf_op jit(solution)/shard_map/ppermute | solution.py:656
  62.6 3.8 %collective-permute-start.15 = (f32[48,128]{1,0:T(8,128)S(1)}, f32[48,128]{1,0:T(8,128)S(1)}, u32[]{:S(2)}, u32[]{:S(2)}) collective-permute-start(f32[48,128]{1,0:T(8,128)S(1)} %get-tuple-element.76), channel_id=1, source_target_pairs={{1,0},{0,1},{3,2},{2,3},{5,4},{4,5},{7,6},{6,7},{9,8},{8,9},{11,10... | collective-permute-start | bytes 73736 | tf_op jit(solution)/shard_map/ppermute | solution.py:656

commit v3 on v2

--- a/solution.py
+++ b/solution.py
@@ -67,8 +67,8 @@
     return (rows == index_row).astype(jnp.float32).astype(jnp.bfloat16)
 
 
-def select(rows, first, second):
-    picks = jnp.concatenate([first, second], axis=1)
+def select(rows, *names):
+    picks = jnp.concatenate(names, axis=1)
     hits = lax.broadcasted_iota(jnp.int32, (rows.shape[1], picks.shape[1]), 0) == picks
     got = dot16(split(rows, 3), hits.astype(jnp.float32).astype(jnp.bfloat16))
     count = rows.shape[0]
@@ -121,53 +121,47 @@
     )
 
 
-def apply_operator(parts16, dm_ref, ef_ref, ee_ref, e8_ref, p_ref, r_ref, mv_ref, eo_ref, xs_ref, sx_ref, cs_ref, atoms, moved_ready=False):
+def rows_of(tile, comp, vectors):
+    return slice(comp * vectors + tile * 8, comp * vectors + tile * 8 + 8)
+
+
+def contract(mv_ref, ef_ref, ee_ref, head_of, xs_ref, sx_ref, atoms):
     lanes = 2 * atoms
-    edges = dm_ref.shape[1]
-    groups = edges // lanes
-    basis = ef_ref.shape[0]
-    vec3 = mv_ref.shape[0]
-    vectors = vec3 // 3
+    basis, edges = ef_ref.shape
+    vectors = mv_ref.shape[0] // 3
     pairs = 2 * basis
-    tiles = vec3 // 24
     lower = lax.broadcasted_iota(jnp.int32, (8, lanes), 1) < atoms
-
-    def rows_of(tile, comp):
-        return comp * vectors + tile * 8
-
-    if not moved_ready:
-        wide = 2 * lanes
-        for j in range(edges // wide):
-            got = dot16(parts16, dm_ref[:, j * wide : (j + 1) * wide])
-            mv_ref[:, j * wide : (j + 1) * wide] = got[:vec3] + got[vec3 : 2 * vec3]
-
-    for tile in range(tiles):
-
-        def gather_step(j, acc, tile=tile):
-            at = pl.ds(pl.multiple_of(j * lanes, lanes), lanes)
-            m = [mv_ref[rows_of(tile, c) : rows_of(tile, c) + 8, at] for c in range(3)]
-            head = [e8_ref[c : c + 1, at] for c in range(3)]
+    for tile in range(vectors // 8):
+        acc = [jnp.zeros((8, lanes), jnp.float32)] * (4 * basis)
+        for j in range(edges // lanes):
+            at = slice(j * lanes, (j + 1) * lanes)
+            m = [mv_ref[rows_of(tile, c, vectors), at] for c in range(3)]
+            head = [head_of(c, at) for c in range(3)]
             u = head[0] * m[0] + head[1] * m[1] + head[2] * m[2]
             along = [head[c] * u for c in range(3)]
             across = [m[c] - along[c] for c in range(3)]
-            new = list(acc)
             for k in range(basis):
                 slope = ef_ref[k : k + 1, at]
                 even = ee_ref[k : k + 1, at]
-                new[k] = new[k] + slope * u
+                acc[k] = acc[k] + slope * u
                 for c in range(3):
                     i = (c + 1) * basis + k
-                    new[i] = new[i] + (slope * along[c] + even * across[c])
-            return tuple(new)
-
-        zero = jnp.zeros((8, lanes), jnp.float32)
-        acc = lax.fori_loop(0, groups, gather_step, (zero,) * (4 * basis), unroll=groups)
+                    acc[i] = acc[i] + (slope * along[c] + even * across[c])
         for i in range(pairs):
             a, b = acc[i], acc[i + pairs]
             x = jnp.where(lower, a, b) + pltpu.roll(jnp.where(lower, b, a), atoms, 1)
             xs_ref[i, tile * 8 : tile * 8 + 8, :] = x
             sx_ref[i, tile * 8 : tile * 8 + 8, :] = pltpu.roll(x, atoms, 1)
 
+
+def spread(dm_ref, ef_ref, ee_ref, e8_ref, p_ref, r_ref, mv_ref, eo_ref, xs_ref, sx_ref, cs_ref, atoms):
+    lanes = 2 * atoms
+    basis, edges = ef_ref.shape
+    groups = edges // lanes
+    vec3 = mv_ref.shape[0]
+    vectors = vec3 // 3
+    pairs = 2 * basis
+    tiles = vectors // 8
     wide_lower = lax.broadcasted_iota(jnp.int32, (8 * tiles, lanes), 1) < atoms
 
     def mix_step(kappa, carry):
@@ -189,7 +183,7 @@
 
         def spread_step(j, carry, tile=tile, coeff=coeff):
             at = pl.ds(pl.multiple_of(j * lanes, lanes), lanes)
-            m = [mv_ref[rows_of(tile, c) : rows_of(tile, c) + 8, at] for c in range(3)]
+            m = [mv_ref[rows_of(tile, c, vectors), at] for c in range(3)]
             row = [e8_ref[i : i + 1, at] for i in range(8)]
             head, turn = row[0:3], row[5:8]
             u = head[0] * m[0] + head[1] * m[1] + head[2] * m[2]
@@ -208,13 +202,13 @@
                 radial = radial + head[c] * (sums[c] - evens[c])
             for c in range(3):
                 out = evens[c] + head[c] * radial + (row[3] * m[c] + turn[c] * u)
-                eo_ref[rows_of(tile, c) : rows_of(tile, c) + 8, at] = out
+                eo_ref[rows_of(tile, c, vectors), at] = out
             return carry
 
         lax.fori_loop(0, groups, spread_step, 0, unroll=groups)
 
-    spread = dot16(split(eo_ref[...], 2), dm_ref[...], NT)
-    return spread[:vec3] + spread[vec3:]
+    both = dot16(split(eo_ref[...], 2), dm_ref[...], NT)
+    return both[:vec3] + both[vec3:]
 
 
 def stacked_sums(parts):
@@ -245,49 +239,56 @@
             outs[x][y * half3 : (y + 1) * half3, atoms : 2 * atoms] = tile[half3:]
 
 
-def select_x_kernel(sides, table, to_mate, to_other):
-    rows = table[: table.shape[0] - 8, :]
-    lists = table[table.shape[0] - 8 :, :].astype(jnp.int32)
-    emit(sides[0], rows, lists[0:2], to_mate, to_other, (rows.shape[0] - 8) // 4)
-
-
-def emit(side, rows, lists, to_mate, to_other, half3):
-    even = side == 0
-    low, high = lists[0:1, :], lists[1:2, :]
+def emit(even, rows, lists, to_mate, to_other):
+    low, high = lists
     got = select(rows, jnp.where(even, low, high), jnp.where(even, high, low))
     halo = low.shape[1]
+    vec3 = (rows.shape[0] - 8) // 2
     for which, out in enumerate((to_mate, to_other)):
         part = got[:, which * halo : (which + 1) * halo]
-        out[0:half3, :] = pack(part[0 : 2 * half3])
-        out[half3 : 2 * half3, :] = pack(part[2 * half3 : 4 * half3])
-        out[2 * half3 :, 0:halo] = part[4 * half3 :]
-        out[2 * half3 :, halo:] = jnp.zeros_like(part[4 * half3 :])
-
-
-def unpack_rows(block, half3, halo):
-    return jnp.concatenate(
-        [unpack(block[0:half3], halo), unpack(block[half3 : 2 * half3], halo), block[2 * half3 :, 0:halo]],
-        axis=0,
-    )
-
-
-def beside(rows, mate, other, even, step, half3, halo):
+        out[0:vec3, :] = jnp.concatenate([part[0:vec3], part[vec3 : 2 * vec3]], axis=1)
+        out[vec3:, :] = jnp.concatenate([part[2 * vec3 :], jnp.zeros_like(part[2 * vec3 :])], axis=1)
+
+
+def unpack_rows(block, width):
+    vec3 = block.shape[0] - 8
+    return jnp.concatenate([block[:vec3, 0:width], block[:vec3, width : 2 * width], block[vec3:, 0:width]], axis=0)
+
+
+def table_rows(table, atoms):
+    rows = unpack_rows(table, atoms)
+    count = rows.shape[0]
+    number = lax.broadcasted_iota(jnp.int32, (8, atoms), 1).astype(jnp.float32)
+    line = lax.broadcasted_iota(jnp.int32, (8, atoms), 0)
+    last = jnp.where(line < 3, rows[count - 8 :], jnp.where(line == 3, number, 0.0))
+    return jnp.concatenate([rows[: count - 8], last], axis=0)
+
+
+def table_lists(table, line, halo):
+    base = table.shape[0] - 8 + line
+    rows = table[base : base + 2, 0:halo].astype(jnp.int32)
+    return rows[0:1], rows[1:2]
+
+
+def beside(rows, mate, other, even, step):
     line = rows.shape[0] - 5
     at = (lax.broadcasted_iota(jnp.int32, (rows.shape[0], 1), 0) == line).astype(jnp.float32) * step
-    mate, other = unpack_rows(mate, half3, halo), unpack_rows(other, half3, halo) + 2.0 * at
+    other = other + 2.0 * at
     return jnp.concatenate(
         [rows + at, jnp.where(even, other, mate), jnp.where(even, mate, other)], axis=1
     )
 
 
-def select_y_kernel(sides, table, from_mate, from_other, to_mate, to_other, wide):
-    atoms = table.shape[1]
-    rows = table[: table.shape[0] - 8, :]
-    lists = table[table.shape[0] - 8 :, :].astype(jnp.int32)
-    half3 = (rows.shape[0] - 8) // 4
-    got = beside(rows, from_mate[...], from_other[...], sides[0] == 0, float(atoms), half3, atoms)
+def select_kernel(sides, table, from_mate, from_other, to_mate, to_other, wide, *, atoms, halo):
+    even = sides[0] == 0
+    picked = []
+    for ref, flip in ((from_mate[...], False), (from_other[...], True)):
+        low, high = table_lists(ref, 3, halo)
+        names = jnp.where(even, low, high) if flip else jnp.where(even, high, low)
+        picked.append(select(table_rows(ref, atoms), names))
+    got = beside(table_rows(table[...], atoms), *picked, even, float(atoms))
     wide[...] = got
-    emit(sides[1], got, lists[2:4], to_mate, to_other, half3)
+    emit(sides[1] == 0, got, table_lists(table[...], 5, halo), to_mate, to_other)
 
 
 def prepare_kernel(table, dm, valid, rad, vec, mix, rad_t, vec_t, mix_t, out_t, *, slots, atoms):
@@ -460,14 +461,20 @@
 
 def first_kernel(
     sides, wide, from_mate, from_other, dm, valid, w_rad, w_vec, w_mix, rad_t, vec_t, mix_t, out_t,
-    out_m, out_o, out_x, sums, cext, pext, index, ef, ee, e8, pmat, rmat,
+    out_m, out_o, out_x, partial, cext, pext, index, ef, ee, e8, pmat, rmat,
     mv, eo, xs, sx, cs, f2s, hs, qs, qr, bd, both,
     *, vectors, atoms, halo,
 ):
     half3 = 3 * vectors // 2
     vec3 = 2 * half3
     lanes = 2 * atoms
-    rows = beside(wide[...], from_mate[...], from_other[...], sides[1] == 0, 3.0 * atoms, half3, halo)
+    rows = beside(
+        wide[...],
+        unpack_rows(from_mate[...], halo),
+        unpack_rows(from_other[...], halo),
+        sides[1] == 0,
+        3.0 * atoms,
+    )
     cext[...] = rows[:vec3]
     pext[...] = rows[vec3 : 2 * vec3]
     base = 2 * vec3
@@ -493,41 +500,54 @@
     alpha = dot32(rad, u)
     beta = [2.0 * dot32(vec, flow[c] * u) for c in range(3)]
     edge_rows(alpha, beta, ef, ee, f2s, hs, e8, lanes)
+    contract(mv, ef, ee, lambda c, at: hs[8 * c : 8 * c + 8, at], xs, sx, atoms)
     channel_lift(flow, radt, vect, mixt, qs, qr, lanes, atoms)
     descriptor_curvature(vec, u, bend, qs, qr, bd, both, pmat, rmat, lanes, atoms)
 
-    result = apply_operator(None, dm, ef, ee, e8, pmat, rmat, mv, eo, xs, sx, cs, atoms, True)
+    result = spread(dm, ef, ee, e8, pmat, rmat, mv, eo, xs, sx, cs, atoms)
+    partial[...] = result
     store_patch((out_m, out_o, out_x), result, pick_matrix(places, 9 * atoms), atoms)
 
-    def gram(left, right, width):
-        total = jnp.zeros((vectors, vectors), jnp.float32)
-        for c in range(3):
-            total = total + dot_split(
-                component(left, c, vectors)[:, :width], component(right, c, vectors)[:, :width], NT
-            )
-        return total
-
-    old_c, old_p = rows[:vec3], rows[vec3 : 2 * vec3]
-    extended = rows.shape[1]
-    cw, pw = gram(old_c, result, extended), gram(old_p, result, extended)
-    cc, cp, pp = gram(old_c, old_c, atoms), gram(old_c, old_p, atoms), gram(old_p, old_p, atoms)
-    sums[...] = jnp.concatenate([with_diagonal(cw, pp), pw, cp, join_triangles(cc, pp)], axis=1)
-
-
-def second_kernel(
-    order, own, mate, other, far, cext, pext, index, dm, ef, ee, e8, pmat, rmat,
-    out_m, out_o, out_x, shared, rown,
-    mv, eo, xs, sx, cs, patch, ring,
-    *, vectors, atoms, total_rows,
-):
+
+def product(left, right, vectors):
+    total = jnp.zeros((vectors, vectors), jnp.float32)
+    for c in range(3):
+        total = total + dot_split(component(left, c, vectors), component(right, c, vectors), NT)
+    return total
+
+
+def sums_kernel(cext, pext, partial, out, *, vectors, atoms):
+    old_c, old_p, new = cext[...], pext[...], partial[...]
+    cw, pw = product(old_c, new, vectors), product(old_p, new, vectors)
+    own_c, own_p = old_c[:, :atoms], old_p[:, :atoms]
+    cc, cp, pp = (product(*pair, vectors) for pair in ((own_c, own_c), (own_c, own_p), (own_p, own_p)))
+    out[...] = jnp.concatenate([with_diagonal(cw, pp), pw, cp, join_triangles(cc, pp)], axis=1)
+
+
+def pair_kernel(resid, partial, out, *, vectors, atoms):
+    r = resid[...]
+    own = r[:, :atoms]
+    lanes = out.shape[1]
+    rr, ry = product(own, own, vectors), product(r, partial[...], vectors)
+    out[...] = jnp.concatenate([flatten(rr, lanes), flatten(ry, lanes)], axis=0)
+
+
+def second_kernel(order, own, mate, other, *rest, vectors, atoms, total_rows, chips):
+    far, rest = rest[: chips - 2], rest[chips - 2 :]
+    cext, pext, index, dm, ef, ee, e8, pmat, rmat, out_m, out_o, out_x, shared, rown, rext, partial = rest[:16]
+    mv, eo, xs, sx, cs, patch, ring = rest[16:]
     half3 = 3 * vectors // 2
     vec3 = 2 * half3
     tail = 3 * half3
     pick = pick_matrix(index[0:1, :], 9 * atoms)
-    for i, part in enumerate((own, mate, other)):
-        ring[order[i]] = part[tail:, :]
-    ring[order[3]] = far[...]
-    total = ((ring[0] + ring[1]) + (ring[2] + ring[3])) * (1.0 / total_rows)
+    ring[order[0]] = own[tail:, :]
+    ring[order[1]] = other[tail:, :]
+    for i, part in enumerate(far):
+        ring[order[2 + i]] = part[...]
+    total = ring[0]
+    for i in range(1, chips):
+        total = total + ring[i]
+    total = total * (1.0 / total_rows)
     v = vectors
     held, pw, cp, joined = (total[:, i * v : (i + 1) * v] for i in range(4))
     coef = jnp.concatenate([from_lower(held), pw], axis=0)
@@ -557,25 +577,53 @@
         axis=0,
     )
     rown[...] = pack(resid[:, :atoms])
-    rows = apply_operator(split(resid, 2), dm, ef, ee, e8, pmat, rmat, mv, eo, xs, sx, cs, atoms)
+    rext[...] = resid
+    parts16 = split(resid, 2)
+    wide = 4 * atoms
+    for j in range(dm.shape[1] // wide):
+        at = slice(j * wide, (j + 1) * wide)
+        got = dot16(parts16, dm[:, at])
+        mv[:, at] = got[:vec3] + got[vec3:]
+    contract(mv, ef, ee, lambda c, at: e8[c : c + 1, at], xs, sx, atoms)
+    rows = spread(dm, ef, ee, e8, pmat, rmat, mv, eo, xs, sx, cs, atoms)
+    partial[...] = rows
     store_patch((out_m, out_o, out_x), rows, pick, atoms)
 
 
-def gram_kernel(rown, y0, ym, yo, out, yown, *, vectors, atoms):
+def send_sums(pairs, yy, out):
+    count, lanes = pairs.shape[0] // 2, pairs.shape[1]
+    size = yy.shape[0]
+    rr, ry = unflatten(pairs[:count], size), unflatten(pairs[count:], size)
+    sent = jnp.concatenate(
+        [flatten(join_triangles(rr, yy), lanes), flatten(with_diagonal(ry, yy), lanes)], axis=0
+    )
+    out[...] = jnp.broadcast_to(sent[None], out.shape)
+
+
+def gram_kernel(pairs, y0, ym, yo, out, yown, *, vectors, atoms):
     work = y0[...] + ym[...] + yo[...]
     yown[...] = work
-    r, y = unpack(rown[...], atoms), unpack(work, atoms)
-    gram = jnp.zeros((2 * vectors, 2 * vectors), jnp.float32)
-    for c in range(3):
-        stacked = jnp.concatenate([component(r, c, vectors), component(y, c, vectors)], axis=0)
-        gram = gram + dot_split(stacked, stacked, NT)
-    v = vectors
-    rr, ry, yy = gram[:v, :v], gram[:v, v:], gram[v:, v:]
-    lanes = out.shape[2]
-    sent = jnp.concatenate(
-        [flatten(join_triangles(rr, yy), lanes), flatten(with_diagonal(ry, yy), lanes)], axis=0
-    )
-    out[...] = jnp.broadcast_to(sent[None], out.shape)
+    y = unpack(work, atoms)
+    send_sums(pairs[...], product(y, y, vectors), out)
+
+
+def column_gram_kernel(order, own, mate, other, far, out, yown, held, *, vectors, atoms):
+    half3 = 3 * vectors // 2
+
+    def part(ref, which):
+        return ref[which * half3 : (which + 1) * half3, :]
+
+    m, zero, o = 0, 1, 2
+    mine = part(own, zero) + part(mate, m) + part(other, o)
+    yown[...] = mine
+    held[order[0]] = mine
+    held[order[1]] = part(mate, zero) + part(own, m) + part(far, o)
+    held[order[2]] = part(other, zero) + part(far, m) + part(own, o)
+    held[order[3]] = part(far, zero) + part(other, m) + part(mate, o)
+    y = jnp.concatenate([unpack(held[i], atoms) for i in range(4)], axis=1)
+    tail = 3 * half3
+    pairs = (own[tail:, :] + mate[tail:, :]) + (other[tail:, :] + far[tail:, :])
+    send_sums(pairs, product(y, y, vectors), out)
 
 
 def cholesky(matrix, *extra):
@@ -636,7 +684,7 @@
     upper2, inv2 = cholesky(gram2)
     factors[0] = upper1.T
     factors[1] = jnp.where(rows >= cols, dot32(inv1, upper2, NT), 0.0)
-    r, y, old = unpack(rown[...], atoms), unpack(yown[...], atoms), cown[0 : 3 * vectors, :]
+    r, y, old = unpack(rown[...], atoms), unpack(yown[...], atoms), cown[0 : 3 * vectors, 0:atoms]
     back = dot32(along, inv1, TN)
     weights = jnp.concatenate([-back, -wr.T], axis=1)
     for c in range(3):
@@ -674,9 +722,9 @@
 
 def laid(shape, pieces):
     total = None
-    for row, piece in pieces:
+    for row, lane, piece in pieces:
         rows, lanes = piece.shape
-        edges = ((row, shape[0] - row - rows), (0, shape[1] - lanes))
+        edges = ((row, shape[0] - row - rows), (lane, shape[1] - lane - lanes))
         placed = jnp.pad(piece, edges).astype(jnp.float32)
         total = placed if total is None else total + placed
     return total
@@ -703,38 +751,35 @@
     mate_y, other_y = mates(n_y)
     at_x, at_y = lax.axis_index("gx"), lax.axis_index("gy")
     sides = jnp.stack([at_x % 2, at_y % 2]).astype(jnp.int32)
-    own_rows = 2 * half3 + 8
+    own_rows = vec3 + 8
 
     cur = block_cur.transpose(1, 0, 2).reshape(vec3, atoms)
     prev = block_prev.transpose(1, 0, 2).reshape(vec3, atoms)
     slab = f32(own_rows, lanes)
     all_rows = 2 * vec3 + 8
 
-    counting = lax.broadcasted_iota(jnp.float32, (1, atoms), 1)
     table = laid(
-        (all_rows + 8, atoms),
+        (own_rows, lanes),
         [
-            (0, cur),
-            (vec3, prev),
-            (2 * vec3, positions),
-            (2 * vec3 + 3, counting),
-            (all_rows, x_lists[0]),
-            (all_rows + 2, y_lists[0]),
+            (0, 0, cur),
+            (0, atoms, prev),
+            (vec3, 0, positions),
+            (vec3 + 3, 0, x_lists[0]),
+            (vec3 + 5, 0, y_lists[0]),
         ],
     )
-    to_mate, to_other = vmem_call(select_x_kernel, [slab, slab], scalars=1)(sides, table)
-    mate1 = fetch(to_mate, "gx", mate_x)
-    other1 = fetch(to_other, "gx", other_x)
+    mate1 = fetch(table, "gx", mate_x)
+    other1 = fetch(table, "gx", other_x)
     after = channels + 2 * basis + 8
     fixed = laid(
         (after + slots + 8, channels),
         [
-            (0, w_mix),
-            (channels, w_radial),
-            (channels + basis, w_vector),
-            (channels + 2 * basis, w_out[None]),
-            (after, neighbours),
-            (after + slots, counts[None]),
+            (0, 0, w_mix),
+            (channels, 0, w_radial),
+            (channels + basis, 0, w_vector),
+            (channels + 2 * basis, 0, w_out[None]),
+            (after, 0, neighbours),
+            (after + slots, 0, counts[None]),
         ],
     )
     rad_shape, mix_shape, turned_shape = f32(basis, channels), f32(channels, channels), f32(channels, basis)
@@ -754,7 +799,9 @@
         flops=1 << 24,
     )(fixed)
     to_mate, to_other, wide = vmem_call(
-        select_y_kernel, [slab, slab, f32(all_rows, atoms + 2 * halo)], scalars=1
+        functools.partial(select_kernel, atoms=atoms, halo=halo),
+        [slab, slab, f32(all_rows, atoms + 2 * halo)],
+        scalars=1,
     )(sides, table, mate1, other1)
     mate2 = fetch(to_mate, "gy", mate_y)
     other2 = fetch(to_other, "gy", other_y)
@@ -772,7 +819,7 @@
             f32(3 * half3, lanes),
             f32(3 * half3, lanes),
             f32(3 * half3, lanes),
-            f32(vectors, lanes),
+            f32(vec3, extended),
             f32(vec3, extended),
             f32(vec3, extended),
             jax.ShapeDtypeStruct((8, extended), jnp.int32),
@@ -794,19 +841,16 @@
         scalars=1,
         flops=1 << 31,
     )
-    part_m, part_0, part_o, local, cext, pext, index, ef, ee, e8, pmat, rmat = first(
+    part_m, part_0, part_o, partial, cext, pext, index, ef, ee, e8, pmat, rmat = first(
         sides, wide, mate2, other2, dm, valid, rad, vec, mix, rad_t, vec_t, mix_t, out_t
     )
 
     back_m = fetch(part_m, "gx", mate_x)
     back_o = fetch(part_o, "gx", other_x)
-    strided = [local] + [
-        fetch(local, "gx", [(i + d) % n_x for i in range(n_x)]) for d in range(4, n_x, 4)
-    ]
-    if len(strided) == 2:
-        local = strided[0] + strided[1]
-    else:
-        local = jnp.sum(jnp.roll(jnp.stack(strided), at_x // 4, axis=0), axis=0)
+    local = vmem_call(
+        functools.partial(sums_kernel, vectors=vectors, atoms=atoms), f32(vectors, lanes), flops=1 << 25
+    )(cext, pext, partial)
+    local = local + fetch(local, "gx", mate_x)
     folded = part_0 + back_m + back_o
     f_m, f_0, f_o = folded[:half3], folded[half3 : 2 * half3], folded[2 * half3 :]
 
@@ -832,40 +876,62 @@
 
     col_m = fetch(column, "gx", mate_x)
     col_o = fetch(column, "gx", other_x)
-    far = fetch(sums, "gx", [(i + 2) % n_x for i in range(n_x)])
-    order = jnp.stack(
-        [at_x % 4, (at_x ^ 1) % 4, (at_x - 1 + 2 * (at_x % 2)) % 4, (at_x + 2) % 4]
-    ).astype(jnp.int32)
+    pairs_x = n_x // 2
+    steps = [d for d in range(1, pairs_x - 1)]
+    far = [
+        fetch(sums, "gx", [(i + 2 * d) % n_x if i % 2 == 0 else (i - 2 * d) % n_x for i in range(n_x)])
+        for d in steps
+    ]
+    chip, way = at_x // 2, 1 - 2 * (at_x % 2)
+    order = jnp.stack([(chip + d * way) % pairs_x for d in [0, -1] + steps]).astype(jnp.int32)
 
     second = vmem_call(
-        functools.partial(second_kernel, vectors=vectors, atoms=atoms, total_rows=total_rows),
+        functools.partial(second_kernel, vectors=vectors, atoms=atoms, total_rows=total_rows, chips=pairs_x),
         [
             f32(3 * half3, lanes),
             f32(3 * half3, lanes),
             f32(3 * half3, lanes),
             f32(2 * vectors, lanes),
             f32(half3, lanes),
+            f32(vec3, extended),
+            f32(vec3, extended),
         ],
         work_scratch
-        + [pltpu.VMEM((vec3, 9 * atoms), jnp.float32), pltpu.VMEM((4, vectors, lanes), jnp.float32)],
+        + [pltpu.VMEM((vec3, 9 * atoms), jnp.float32), pltpu.VMEM((pairs_x, vectors, lanes), jnp.float32)],
         scalars=1,
         flops=1 << 30,
     )
-    part_m, part_0, part_o, shared, rown = second(
-        order, column, col_m, col_o, far, cext, pext, index, dm, ef, ee, e8, pmat, rmat
+    part_m, part_0, part_o, shared, rown, rext, partial = second(
+        order, column, col_m, col_o, *far, cext, pext, index, dm, ef, ee, e8, pmat, rmat
     )
     back_m = fetch(part_m, "gx", mate_x)
     back_o = fetch(part_o, "gx", other_x)
+    sent_rows = 2 * vectors * vectors // lanes
+    pairs_rr = vmem_call(
+        functools.partial(pair_kernel, vectors=vectors, atoms=atoms), f32(sent_rows, lanes), flops=1 << 25
+    )(rext, partial)
     folded = part_0 + back_m + back_o
-    y_m = fetch(folded[:half3], "gy", mate_y)
-    y_o = fetch(folded[2 * half3 :], "gy", other_y)
-
-    sent_rows = 2 * vectors * vectors // lanes
-    spread, yown = vmem_call(
-        functools.partial(gram_kernel, vectors=vectors, atoms=atoms),
-        [f32(n_x * n_y, sent_rows, lanes), f32(half3, lanes)],
-    )(rown, folded[half3 : 2 * half3], y_m, y_o)
-    got = lax.all_to_all(spread, ("gx", "gy"), 0, 0)
+    if far_m == far_o:
+        share = jnp.concatenate([folded, pairs_rr])
+        got_m = fetch(share, "gy", mate_y)
+        got_o = fetch(share, "gy", other_y)
+        got_2 = fetch(share, "gy", far_m)
+        order = jnp.stack([at_y, at_y ^ 1, (at_y - 1 + 2 * (at_y % 2)) % 4, (at_y + 2) % 4])
+        spread_sums, yown = vmem_call(
+            functools.partial(column_gram_kernel, vectors=vectors, atoms=atoms),
+            [f32(n_x, sent_rows, lanes), f32(half3, lanes)],
+            [pltpu.VMEM((4, half3, lanes), jnp.float32)],
+            scalars=1,
+        )(order.astype(jnp.int32), share, got_m, got_o, got_2)
+        got = lax.all_to_all(spread_sums, "gx", 0, 0)
+    else:
+        y_m = fetch(folded[:half3], "gy", mate_y)
+        y_o = fetch(folded[2 * half3 :], "gy", other_y)
+        spread_sums, yown = vmem_call(
+            functools.partial(gram_kernel, vectors=vectors, atoms=atoms),
+            [f32(n_x * n_y, sent_rows, lanes), f32(half3, lanes)],
+        )(pairs_rr, folded[half3 : 2 * half3], y_m, y_o)
+        got = lax.all_to_all(spread_sums, ("gx", "gy"), 0, 0)
     blocks, factors = vmem_call(
         functools.partial(final_kernel, vectors=vectors, atoms=atoms, total_rows=total_rows),
         [f32(2, 3, vectors, atoms), f32(2, vectors, vectors)],

time: 83.6 us -> 79.5 us (0.951)
  blocking collectives: 12.7 us -> 8.28 us
  starting transfers between devices: 19.3 us -> 21.1 us
  waiting for transfers between devices: 24.7 us -> 23.7 us
    all_to_all x1, blocking collectives: 12.7 us -> 8.28 us  [shards(): got = lax.all_to_all(spread_sums, 'gx', 0, 0)]
    ppermute x17 -> x19, starting transfers between devices: 19.3 us -> 21.1 us  [fetch(): return lax.ppermute(values, axis, [(s, i) for i, s in enumerate(sources)])]
    ppermute x17 -> x19, waiting for transfers between devices: 24.7 us -> 23.7 us  [fetch(): return lax.ppermute(values, axis, [(s, i) for i, s in enumerate(sources)])]
    pallas_call x7 -> x8, Pallas kernels: 23.7 us -> 23.2 us  [call(): pl.pallas_call(kernel, out_shape=outs, in_specs=[pl.BlockSpec(memory_spac...]
  transfers between devices with their start and end apart: 17 -> 19, of which waited for: 12 -> 13; matrix products, arithmetic and copies ran while one was open for 1% -> 1% of each run, Pallas kernels for 1% -> 2%
where the time goes in v3:
time: 79.5 us; the launch traced here: 79.3 us
  waiting for transfers between devices  23.7 us (30%)
  Pallas kernels  23.2 us (29%)
  starting transfers between devices  21.1 us (27%)
  blocking collectives  8.28 us (10%)
  other arithmetic  2.2 us (3%)
    ppermute x19, waiting for transfers between devices, fetch(): return lax.ppermute(values, axis, [(s, i) for i, s in enumerate(sources)])  23.7 us
    pallas_call x8, Pallas kernels, call(): pl.pallas_call(kernel, out_shape=outs, in_specs=[pl.BlockSpec(memory_spac...  23.2 us
    ppermute x19, starting transfers between devices, fetch(): return lax.ppermute(values, axis, [(s, i) for i, s in enumerate(sources)])  21.1 us
    all_to_all x1, blocking collectives, shards(): got = lax.all_to_all(spread_sums, 'gx', 0, 0)  8.28 us
    add x2, other arithmetic, laid(): total = placed if total is None else total + placed  1.88 us
  transfers between devices with their start and end apart: 19, of which 13 were waited for; matrix products, arithmetic and copies ran while one was open for 1% of the time, Pallas kernels for 2%

profile of v3, /device:TPU:0, one launch (start us, length us, event | category | flops | bytes accessed | tf_op | source)
XLA Modules:
  0.0 79.3 jit_solution(1083571170938646429)
XLA Ops:
  0.6 1.0 %convert_add_fusion.1.table.cown = f32[104,128]{1,0:T(8,128)S(1)} fusion(s32[2,64]{1,0:T(2,128)} %bitcast.23, s32[2,64]{1,0:T(2,128)} %bitcast.24, f32[3,64]{1,0:T(4,128)} %param.11, f32[96,64]{1,0:T(8,128)} %bitcast.21, f32[96,64]{1,0:T(8,128)} %bitcast.22), kind=kLoop, calls=%fused_computation.8 | loop fusion | flops 79872 | bytes 104192 | tf_op jit(solution)/shard_map/add | solution.py:729
  1.6 4.6 %collective-permute-start.1 = (f32[104,128]{1,0:T(8,128)S(1)}, f32[104,128]{1,0:T(8,128)S(1)}, u32[]{:S(2)}, u32[]{:S(2)}) collective-permute-start(f32[104,128]{1,0:T(8,128)S(1)} %convert_add_fusion.1.table.cown), channel_id=1, source_target_pairs={{28,0},{8,4},{4,8},{16,12},{12,16},{24,20},{20,24},{0,28},{29,1},{... | collective-permute-start | bytes 159752 | tf_op jit(solution)/shard_map/ppermute | solution.py:704
  6.1 0.0 collective-permute-start
  6.1 0.1 pad_add_fusion.2.sides
  6.2 1.8 %collective-permute-done.1.from_other = f32[104,128]{1,0:T(8,128)S(1)} collective-permute-done((f32[104,128]{1,0:T(8,128)S(1)}, f32[104,128]{1,0:T(8,128)S(1)}, u32[]{:S(2)}, u32[]{:S(2)}) %collective-permute-start.1) | collective-permute-done | bytes 53280 | tf_op jit(solution)/shard_map/ppermute | solution.py:704
  8.1 1.2 %shard_map.122 = (f32[104,128]{1,0:T(8,128)S(1)}, f32[104,128]{1,0:T(8,128)S(1)}, f32[200,192]{1,0:T(8,128)S(1)}) custom-call(s32[2]{0:T(128)S(1)} %pad_add_fusion.2.sides, f32[104,128]{1,0:T(8,128)S(1)} %convert_add_fusion.1.table.cown, f32[104,128]{1,0:T(8,128)S(1)} %collective-permute-done.from_mate, f32[104,128]{1,0:T(8,128)S(1)} %collective-permute-done.1.from_other), custom_call_target="tpu_custom_call" | custom-call | flops 1048576 | bytes 65536 | tf_op jit(solution)/shard_map/pallas_call | solution.py:710
  9.2 2.2 %collective-permute-start.2 = (f32[104,128]{1,0:T(8,128)S(1)}, f32[104,128]{1,0:T(8,128)S(1)}, u32[]{:S(2)}, u32[]{:S(2)}) collective-permute-start(f32[104,128]{1,0:T(8,128)S(1)} %get-tuple-element.38), channel_id=1, source_target_pairs={{1,0},{0,1},{3,2},{2,3},{5,4},{4,5},{7,6},{6,7},{9,8},{8,9},{11,10... | collective-permute-start | bytes 159752 | tf_op jit(solution)/shard_map/ppermute | solution.py:704
  11.5 1.5 %collective-permute-start.3 = (f32[104,128]{1,0:T(8,128)S(1)}, f32[104,128]{1,0:T(8,128)S(1)}, u32[]{:S(2)}, u32[]{:S(2)}) collective-permute-start(f32[104,128]{1,0:T(8,128)S(1)} %get-tuple-element.39), channel_id=1, source_target_pairs={{3,0},{2,1},{1,2},{0,3},{7,4},{6,5},{5,6},{4,7},{11,8},{10,9},{9,1... | collective-permute-start | bytes 159752 | tf_op jit(solution)/shard_map/ppermute | solution.py:704
  13.0 0.9 %convert_add_fusion.table = f32[192,128]{1,0:T(8,128)S(1)} fusion(s32[1,64]{1,0:T(1,128)} %bitcast.25, s32[32,64]{1,0:T(8,128)} %param.14, f32[1,128]{1,0:T(1,128)} %bitcast.26, f32[8,128]{1,0:T(8,128)} %param.19, f32[8,128]{1,0:T(8,128)} %param.18, f32[128,128]{1,0:T(8,128)} %param.20), kind=kLoop, calls=%fused_computation.3 | loop fusion | flops 172032 | bytes 180992 | tf_op jit(solution)/shard_map/add | solution.py:729
  13.9 0.7 shard_map.123
  14.7 0.0 collective-permute-done.2.from_mate
  14.7 1.8 %collective-permute-done.3.from_other = f32[104,128]{1,0:T(8,128)S(1)} collective-permute-done((f32[104,128]{1,0:T(8,128)S(1)}, f32[104,128]{1,0:T(8,128)S(1)}, u32[]{:S(2)}, u32[]{:S(2)}) %collective-permute-start.3) | collective-permute-done | bytes 53280 | tf_op jit(solution)/shard_map/ppermute | solution.py:704
  16.5 9.5 %shard_map.124 = (f32[144,128]{1,0:T(8,128)S(1)}, f32[144,128]{1,0:T(8,128)S(1)}, f32[144,128]{1,0:T(8,128)S(1)}, f32[96,320]{1,0:T(8,128)S(1)}, f32[96,320]{1,0...) custom-call(s32[2]{0:T(128)S(1)} %pad_add_fusion.2.sides, ...), custom_call_target="tpu_custom_call" | custom-call | flops 2147483648 | bytes 65536 | tf_op jit(solution)/shard_map/pallas_call | solution.py:710
  26.1 0.1 collective-permute-start.4
  26.1 1.9 %collective-permute-start.5 = (f32[144,128]{1,0:T(8,128)S(1)}, f32[144,128]{1,0:T(8,128)S(1)}, u32[]{:S(2)}, u32[]{:S(2)}) collective-permute-start(f32[144,128]{1,0:T(8,128)S(1)} %get-tuple-element.51), channel_id=1, source_target_pairs={{28,0},{8,4},{4,8},{16,12},{12,16},{24,20},{20,24},{0,28},{29,1},{... | collective-permute-start | bytes 221192 | tf_op jit(solution)/shard_map/ppermute | solution.py:704
  28.0 0.5 shard_map.125
  28.5 0.1 collective-permute-start.6
  28.5 1.2 %collective-permute-done.6 = f32[32,128]{1,0:T(8,128)S(1)} collective-permute-done((f32[32,128]{1,0:T(8,128)S(1)}, f32[32,128]{1,0:T(8,128)S(1)}, u32[]{:S(2)}, u32[]{:S(2)}) %collective-permute-start.6) | collective-permute-done | bytes 16416 | tf_op jit(solution)/shard_map/ppermute | solution.py:704
  29.7 2.1 %collective-permute-done.5 = f32[144,128]{1,0:T(8,128)S(1)} collective-permute-done((f32[144,128]{1,0:T(8,128)S(1)}, f32[144,128]{1,0:T(8,128)S(1)}, u32[]{:S(2)}, u32[]{:S(2)}) %collective-permute-start.5) | collective-permute-done | bytes 73760 | tf_op jit(solution)/shard_map/ppermute | solution.py:704
  31.9 0.7 collective-permute-start.7
  32.6 1.4 %collective-permute-start.8 = (f32[128,128]{1,0:T(8,128)S(1)}, f32[128,128]{1,0:T(8,128)S(1)}, u32[]{:S(2)}, u32[]{:S(2)}) collective-permute-start(f32[128,128]{1,0:T(8,128)S(1)} %get-tuple-element.79), channel_id=1, source_target_pairs={{2,0},{3,1},{0,2},{1,3},{6,4},{7,5},{4,6},{5,7},{10,8},{11,9},{8,1... | collective-permute-start | bytes 196616 | tf_op jit(solution)/shard_map/ppermute | solution.py:704
  34.0 1.4 %collective-permute-start.9 = (f32[128,128]{1,0:T(8,128)S(1)}, f32[128,128]{1,0:T(8,128)S(1)}, u32[]{:S(2)}, u32[]{:S(2)}) collective-permute-start(f32[128,128]{1,0:T(8,128)S(1)} %get-tuple-element.80), channel_id=1, source_target_pairs={{3,0},{2,1},{1,2},{0,3},{7,4},{6,5},{5,6},{4,7},{11,8},{10,9},{9,1... | collective-permute-start | bytes 196616 | tf_op jit(solution)/shard_map/ppermute | solution.py:704
  35.4 0.8 collective-permute-done.7
  36.2 0.8 collective-permute-done.8
  37.0 2.2 %collective-permute-done.9 = f32[128,128]{1,0:T(8,128)S(1)} collective-permute-done((f32[128,128]{1,0:T(8,128)S(1)}, f32[128,128]{1,0:T(8,128)S(1)}, u32[]{:S(2)}, u32[]{:S(2)}) %collective-permute-start.9) | collective-permute-done | bytes 65568 | tf_op jit(solution)/shard_map/ppermute | solution.py:704
  39.2 0.1 collective-permute-start.13
  39.2 0.9 %collective-permute-start.12 = (f32[32,128]{1,0:T(8,128)S(1)}, f32[32,128]{1,0:T(8,128)S(1)}, u32[]{:S(2)}, u32[]{:S(2)}) collective-permute-start(f32[32,128]{1,0:T(8,128)S(1)} %fusion.1), channel_id=1, source_target_pairs={{8,0},{28,4},{16,8},{4,12},{24,16},{12,20},{0,24},{20,28},{9,1},{2... | collective-permute-start | bytes 49160 | tf_op jit(solution)/shard_map/ppermute | solution.py:704
  40.1 0.1 collective-permute-start.11
  40.2 1.5 %collective-permute-start.10 = (f32[176,128]{1,0:T(8,128)S(1)}, f32[176,128]{1,0:T(8,128)S(1)}, u32[]{:S(2)}, u32[]{:S(2)}) collective-permute-start(f32[176,128]{1,0:T(8,128)S(1)} %pad_maximum_fusion.3.own), channel_id=1, source_target_pairs={{4,0},{0,4},{12,8},{8,12},{20,16},{16,20},{28,24},{24,28},{5,1},{1... | collective-permute-start | bytes 270344 | tf_op jit(solution)/shard_map/ppermute | solution.py:704
  41.7 0.1 pad_add_fusion.1.order
  41.8 2.2 %collective-permute-done.13.rest_1_ = f32[32,128]{1,0:T(8,128)S(1)} collective-permute-done((f32[32,128]{1,0:T(8,128)S(1)}, f32[32,128]{1,0:T(8,128)S(1)}, u32[]{:S(2)}, u32[]{:S(2)}) %collective-permute-start.13) | collective-permute-done | bytes 16416 | tf_op jit(solution)/shard_map/ppermute | solution.py:704
  44.0 0.0 collective-permute-done.12.rest_0_
  44.0 2.8 %collective-permute-done.11.other = f32[176,128]{1,0:T(8,128)S(1)} collective-permute-done((f32[176,128]{1,0:T(8,128)S(1)}, f32[176,128]{1,0:T(8,128)S(1)}, u32[]{:S(2)}, u32[]{:S(2)}) %collective-permute-start.11) | collective-permute-done | bytes 90144 | tf_op jit(solution)/shard_map/ppermute | solution.py:704
  46.8 6.2 %shard_map.126 = (f32[144,128]{1,0:T(8,128)S(1)}, f32[144,128]{1,0:T(8,128)S(1)}, f32[144,128]{1,0:T(8,128)S(1)}, f32[64,128]{1,0:T(8,128)S(1)}, f32[48,128]{1,0...) custom-call(s32[4]{0:T(128)S(1)} %pad_add_fusion.1.order, f32[176,128]{1,0:T(8,128)S(1)} %pad_maximum_fusion.3.own, ...), custom_call_target="tpu_custom_call" | custom-call | flops 1073741824 | bytes 65536 | tf_op jit(solution)/shard_map/pallas_call | solution.py:710
  53.0 0.1 collective-permute-start.14
  53.1 1.1 %collective-permute-start.15 = (f32[144,128]{1,0:T(8,128)S(1)}, f32[144,128]{1,0:T(8,128)S(1)}, u32[]{:S(2)}, u32[]{:S(2)}) collective-permute-start(f32[144,128]{1,0:T(8,128)S(1)} %get-tuple-element.63), channel_id=1, source_target_pairs={{28,0},{8,4},{4,8},{16,12},{12,16},{24,20},{20,24},{0,28},{29,1},{... | collective-permute-start | bytes 221192 | tf_op jit(solution)/shard_map/ppermute | solution.py:704
  54.1 0.3 shard_map.127
  54.4 4.3 %collective-permute-done.15 = f32[144,128]{1,0:T(8,128)S(1)} collective-permute-done((f32[144,128]{1,0:T(8,128)S(1)}, f32[144,128]{1,0:T(8,128)S(1)}, u32[]{:S(2)}, u32[]{:S(2)}) %collective-permute-start.15) | collective-permute-done | bytes 73760 | tf_op jit(solution)/shard_map/ppermute | solution.py:704
  58.7 1.2 %collective-permute-start.18 = (f32[160,128]{1,0:T(8,128)S(1)}, f32[160,128]{1,0:T(8,128)S(1)}, u32[]{:S(2)}, u32[]{:S(2)}) collective-permute-start(f32[160,128]{1,0:T(8,128)S(1)} %pad_maximum_fusion.4.own), channel_id=1, source_target_pairs={{2,0},{3,1},{0,2},{1,3},{6,4},{7,5},{4,6},{5,7},{10,8},{11,9},{8,1... | collective-permute-start | bytes 245768 | tf_op jit(solution)/shard_map/ppermute | solution.py:704
  59.9 1.8 %collective-permute-start.17 = (f32[160,128]{1,0:T(8,128)S(1)}, f32[160,128]{1,0:T(8,128)S(1)}, u32[]{:S(2)}, u32[]{:S(2)}) collective-permute-start(f32[160,128]{1,0:T(8,128)S(1)} %pad_maximum_fusion.4.own), channel_id=1, source_target_pairs={{3,0},{2,1},{1,2},{0,3},{7,4},{6,5},{5,6},{4,7},{11,8},{10,9},{9,1... | collective-permute-start | bytes 245768 | tf_op jit(solution)/shard_map/ppermute | solution.py:704
  61.8 0.5 collective-permute-start.16
  62.3 0.1 pad_add_fusion.order
  62.4 1.1 %collective-permute-done.18.far = f32[160,128]{1,0:T(8,128)S(1)} collective-permute-done((f32[160,128]{1,0:T(8,128)S(1)}, f32[160,128]{1,0:T(8,128)S(1)}, u32[]{:S(2)}, u32[]{:S(2)}) %collective-permute-start.18) | collective-permute-done | bytes 81952 | tf_op jit(solution)/shard_map/ppermute | solution.py:704
  63.5 1.7 %collective-permute-done.17.other = f32[160,128]{1,0:T(8,128)S(1)} collective-permute-done((f32[160,128]{1,0:T(8,128)S(1)}, f32[160,128]{1,0:T(8,128)S(1)}, u32[]{:S(2)}, u32[]{:S(2)}) %collective-permute-start.17) | collective-permute-done | bytes 81952 | tf_op jit(solution)/shard_map/ppermute | solution.py:704
  65.2 1.0 %collective-permute-done.16.mate = f32[160,128]{1,0:T(8,128)S(1)} collective-permute-done((f32[160,128]{1,0:T(8,128)S(1)}, f32[160,128]{1,0:T(8,128)S(1)}, u32[]{:S(2)}, u32[]{:S(2)}) %collective-permute-start.16) | collective-permute-done | bytes 81952 | tf_op jit(solution)/shard_map/ppermute | solution.py:704
  66.2 0.9 %shard_map.128 = (f32[8,16,128]{2,1,0:T(8,128)S(1)}, f32[48,128]{1,0:T(8,128)S(1)}) custom-call(s32[4]{0:T(128)S(1)} %pad_add_fusion.order, f32[160,128]{1,0:T(8,128)S(1)} %pad_maximum_fusion.4.own, f32[160,128]{1,0:T(8,128)S(1)} %collective-permute-done.16.mate, f32[160,128]{1,0:T(8,128)S(1)} %collective-permute-done.17.other, ...), custom_call_target="tpu_custom_call" | custom-call | flops 1048576 | bytes 65536 | tf_op jit(solution)/shard_map/pallas_call | solution.py:710
  67.1 8.3 %all_to_all.5.got = f32[8,16,128]{2,1,0:T(8,128)S(1)} all-to-all(f32[8,16,128]{2,1,0:T(8,128)S(1)} %get-tuple-element.66), channel_id=1, replica_groups=mesh['gx'=8,'gy'=4] {'gx'}, dimensions={0} | all-to-all | bytes 131072 | tf_op jit(solution)/shard_map/all_to_all | solution.py:926
  75.4 3.9 %shard_map.129 = (f32[2,3,32,64]{3,2,1,0:T(8,128)}, f32[2,32,32]{2,1,0:T(8,128)}) custom-call(f32[8,16,128]{2,1,0:T(8,128)S(1)} %all_to_all.5.got, f32[64,128]{1,0:T(8,128)S(1)} %get-tuple-element.67.sums, f32[48,128]{1,0:T(8,128)S(1)} %get-tuple-element.68.rown, f32[48,128]{1,0:T(8,128)S(1)} %get-tuple-element.69.yown, ...), custom_call_target="tpu_custom_call" | custom-call | flops 1048576 | bytes 65536 | tf_op jit(solution)/shard_map/pallas_call | solution.py:710
  (14 shorter events, 0.1 us)
Async XLA Ops:
  1.6 6.5 %collective-permute-start.1 = (f32[104,128]{1,0:T(8,128)S(1)}, f32[104,128]{1,0:T(8,128)S(1)}, u32[]{:S(2)}, u32[]{:S(2)}) collective-permute-start(f32[104,128]{1,0:T(8,128)S(1)} %convert_add_fusion.1.table.cown), channel_id=1, source_target_pairs={{28,0},{8,4},{4,8},{16,12},{12,16},{24,20},{20,24},{0,28},{29,1},{... | collective-permute-start | bytes 159752 | tf_op jit(solution)/shard_map/ppermute | solution.py:704
  6.1 1.9 %collective-permute-start = (f32[104,128]{1,0:T(8,128)S(1)}, f32[104,128]{1,0:T(8,128)S(1)}, u32[]{:S(2)}, u32[]{:S(2)}) collective-permute-start(f32[104,128]{1,0:T(8,128)S(1)} %convert_add_fusion.1.table.cown), channel_id=1, source_target_pairs={{4,0},{0,4},{12,8},{8,12},{20,16},{16,20},{28,24},{24,28},{5,1},{1... | collective-permute-start | bytes 159752 | tf_op jit(solution)/shard_map/ppermute | solution.py:704
  9.2 5.4 %collective-permute-start.2 = (f32[104,128]{1,0:T(8,128)S(1)}, f32[104,128]{1,0:T(8,128)S(1)}, u32[]{:S(2)}, u32[]{:S(2)}) collective-permute-start(f32[104,128]{1,0:T(8,128)S(1)} %get-tuple-element.38), channel_id=1, source_target_pairs={{1,0},{0,1},{3,2},{2,3},{5,4},{4,5},{7,6},{6,7},{9,8},{8,9},{11,10... | collective-permute-start | bytes 159752 | tf_op jit(solution)/shard_map/ppermute | solution.py:704
  11.5 5.0 %collective-permute-start.3 = (f32[104,128]{1,0:T(8,128)S(1)}, f32[104,128]{1,0:T(8,128)S(1)}, u32[]{:S(2)}, u32[]{:S(2)}) collective-permute-start(f32[104,128]{1,0:T(8,128)S(1)} %get-tuple-element.39), channel_id=1, source_target_pairs={{3,0},{2,1},{1,2},{0,3},{7,4},{6,5},{5,6},{4,7},{11,8},{10,9},{9,1... | collective-permute-start | bytes 159752 | tf_op jit(solution)/shard_map/ppermute | solution.py:704
  26.1 3.7 %collective-permute-start.4 = (f32[144,128]{1,0:T(8,128)S(1)}, f32[144,128]{1,0:T(8,128)S(1)}, u32[]{:S(2)}, u32[]{:S(2)}) collective-permute-start(f32[144,128]{1,0:T(8,128)S(1)} %get-tuple-element.50), channel_id=1, source_target_pairs={{4,0},{0,4},{12,8},{8,12},{20,16},{16,20},{28,24},{24,28},{5,1},{1... | collective-permute-start | bytes 221192 | tf_op jit(solution)/shard_map/ppermute | solution.py:704
  26.1 5.6 %collective-permute-start.5 = (f32[144,128]{1,0:T(8,128)S(1)}, f32[144,128]{1,0:T(8,128)S(1)}, u32[]{:S(2)}, u32[]{:S(2)}) collective-permute-start(f32[144,128]{1,0:T(8,128)S(1)} %get-tuple-element.51), channel_id=1, source_target_pairs={{28,0},{8,4},{4,8},{16,12},{12,16},{24,20},{20,24},{0,28},{29,1},{... | collective-permute-start | bytes 221192 | tf_op jit(solution)/shard_map/ppermute | solution.py:704
  28.5 1.2 %collective-permute-start.6 = (f32[32,128]{1,0:T(8,128)S(1)}, f32[32,128]{1,0:T(8,128)S(1)}, u32[]{:S(2)}, u32[]{:S(2)}) collective-permute-start(f32[32,128]{1,0:T(8,128)S(1)} %shard_map.125), channel_id=1, source_target_pairs={{4,0},{0,4},{12,8},{8,12},{20,16},{16,20},{28,24},{24,28},{5,1},{1... | collective-permute-start | bytes 49160 | tf_op jit(solution)/shard_map/ppermute | solution.py:704
  31.9 4.3 %collective-permute-start.7 = (f32[128,128]{1,0:T(8,128)S(1)}, f32[128,128]{1,0:T(8,128)S(1)}, u32[]{:S(2)}, u32[]{:S(2)}) collective-permute-start(f32[128,128]{1,0:T(8,128)S(1)} %get-tuple-element.78), channel_id=1, source_target_pairs={{1,0},{0,1},{3,2},{2,3},{5,4},{4,5},{7,6},{6,7},{9,8},{8,9},{11,10... | collective-permute-start | bytes 196616 | tf_op jit(solution)/shard_map/ppermute | solution.py:704
  32.6 4.4 %collective-permute-start.8 = (f32[128,128]{1,0:T(8,128)S(1)}, f32[128,128]{1,0:T(8,128)S(1)}, u32[]{:S(2)}, u32[]{:S(2)}) collective-permute-start(f32[128,128]{1,0:T(8,128)S(1)} %get-tuple-element.79), channel_id=1, source_target_pairs={{2,0},{3,1},{0,2},{1,3},{6,4},{7,5},{4,6},{5,7},{10,8},{11,9},{8,1... | collective-permute-start | bytes 196616 | tf_op jit(solution)/shard_map/ppermute | solution.py:704
  34.0 5.2 %collective-permute-start.9 = (f32[128,128]{1,0:T(8,128)S(1)}, f32[128,128]{1,0:T(8,128)S(1)}, u32[]{:S(2)}, u32[]{:S(2)}) collective-permute-start(f32[128,128]{1,0:T(8,128)S(1)} %get-tuple-element.80), channel_id=1, source_target_pairs={{3,0},{2,1},{1,2},{0,3},{7,4},{6,5},{5,6},{4,7},{11,8},{10,9},{9,1... | collective-permute-start | bytes 196616 | tf_op jit(solution)/shard_map/ppermute | solution.py:704
  39.2 4.8 %collective-permute-start.13 = (f32[32,128]{1,0:T(8,128)S(1)}, f32[32,128]{1,0:T(8,128)S(1)}, u32[]{:S(2)}, u32[]{:S(2)}) collective-permute-start(f32[32,128]{1,0:T(8,128)S(1)} %fusion.1), channel_id=1, source_target_pairs={{16,0},{20,4},{24,8},{28,12},{0,16},{4,20},{8,24},{12,28},{17,1},{... | collective-permute-start | bytes 49160 | tf_op jit(solution)/shard_map/ppermute | solution.py:704
  39.2 4.7 %collective-permute-start.12 = (f32[32,128]{1,0:T(8,128)S(1)}, f32[32,128]{1,0:T(8,128)S(1)}, u32[]{:S(2)}, u32[]{:S(2)}) collective-permute-start(f32[32,128]{1,0:T(8,128)S(1)} %fusion.1), channel_id=1, source_target_pairs={{8,0},{28,4},{16,8},{4,12},{24,16},{12,20},{0,24},{20,28},{9,1},{2... | collective-permute-start | bytes 49160 | tf_op jit(solution)/shard_map/ppermute | solution.py:704
  40.1 6.6 %collective-permute-start.11 = (f32[176,128]{1,0:T(8,128)S(1)}, f32[176,128]{1,0:T(8,128)S(1)}, u32[]{:S(2)}, u32[]{:S(2)}) collective-permute-start(f32[176,128]{1,0:T(8,128)S(1)} %pad_maximum_fusion.3.own), channel_id=1, source_target_pairs={{28,0},{8,4},{4,8},{16,12},{12,16},{24,20},{20,24},{0,28},{29,1},{... | collective-permute-start | bytes 270344 | tf_op jit(solution)/shard_map/ppermute | solution.py:704
  40.2 6.5 %collective-permute-start.10 = (f32[176,128]{1,0:T(8,128)S(1)}, f32[176,128]{1,0:T(8,128)S(1)}, u32[]{:S(2)}, u32[]{:S(2)}) collective-permute-start(f32[176,128]{1,0:T(8,128)S(1)} %pad_maximum_fusion.3.own), channel_id=1, source_target_pairs={{4,0},{0,4},{12,8},{8,12},{20,16},{16,20},{28,24},{24,28},{5,1},{1... | collective-permute-start | bytes 270344 | tf_op jit(solution)/shard_map/ppermute | solution.py:704
  53.0 1.5 %collective-permute-start.14 = (f32[144,128]{1,0:T(8,128)S(1)}, f32[144,128]{1,0:T(8,128)S(1)}, u32[]{:S(2)}, u32[]{:S(2)}) collective-permute-start(f32[144,128]{1,0:T(8,128)S(1)} %get-tuple-element.62), channel_id=1, source_target_pairs={{4,0},{0,4},{12,8},{8,12},{20,16},{16,20},{28,24},{24,28},{5,1},{1... | collective-permute-start | bytes 221192 | tf_op jit(solution)/shard_map/ppermute | solution.py:704
  53.1 5.6 %collective-permute-start.15 = (f32[144,128]{1,0:T(8,128)S(1)}, f32[144,128]{1,0:T(8,128)S(1)}, u32[]{:S(2)}, u32[]{:S(2)}) collective-permute-start(f32[144,128]{1,0:T(8,128)S(1)} %get-tuple-element.63), channel_id=1, source_target_pairs={{28,0},{8,4},{4,8},{16,12},{12,16},{24,20},{20,24},{0,28},{29,1},{... | collective-permute-start | bytes 221192 | tf_op jit(solution)/shard_map/ppermute | solution.py:704
  58.7 4.8 %collective-permute-start.18 = (f32[160,128]{1,0:T(8,128)S(1)}, f32[160,128]{1,0:T(8,128)S(1)}, u32[]{:S(2)}, u32[]{:S(2)}) collective-permute-start(f32[160,128]{1,0:T(8,128)S(1)} %pad_maximum_fusion.4.own), channel_id=1, source_target_pairs={{2,0},{3,1},{0,2},{1,3},{6,4},{7,5},{4,6},{5,7},{10,8},{11,9},{8,1... | collective-permute-start | bytes 245768 | tf_op jit(solution)/shard_map/ppermute | solution.py:704
  59.9 5.3 %collective-permute-start.17 = (f32[160,128]{1,0:T(8,128)S(1)}, f32[160,128]{1,0:T(8,128)S(1)}, u32[]{:S(2)}, u32[]{:S(2)}) collective-permute-start(f32[160,128]{1,0:T(8,128)S(1)} %pad_maximum_fusion.4.own), channel_id=1, source_target_pairs={{3,0},{2,1},{1,2},{0,3},{7,4},{6,5},{5,6},{4,7},{11,8},{10,9},{9,1... | collective-permute-start | bytes 245768 | tf_op jit(solution)/shard_map/ppermute | solution.py:704
  61.8 4.4 %collective-permute-start.16 = (f32[160,128]{1,0:T(8,128)S(1)}, f32[160,128]{1,0:T(8,128)S(1)}, u32[]{:S(2)}, u32[]{:S(2)}) collective-permute-start(f32[160,128]{1,0:T(8,128)S(1)} %pad_maximum_fusion.4.own), channel_id=1, source_target_pairs={{1,0},{0,1},{3,2},{2,3},{5,4},{4,5},{7,6},{6,7},{9,8},{8,9},{11,10... | collective-permute-start | bytes 245768 | tf_op jit(solution)/shard_map/ppermute | solution.py:704

commit v4 on v3

--- a/solution.py
+++ b/solution.py
@@ -176,39 +176,41 @@
         cs_ref[kappa + pairs] = jnp.where(wide_lower, turned, y)
         return carry
 
-    lax.fori_loop(0, pairs, mix_step, 0, unroll=4)
-
-    for tile in range(tiles):
-        coeff = [cs_ref[i, tile * 8 : tile * 8 + 8, :] for i in range(4 * basis)]
-
-        def spread_step(j, carry, tile=tile, coeff=coeff):
-            at = pl.ds(pl.multiple_of(j * lanes, lanes), lanes)
-            m = [mv_ref[rows_of(tile, c, vectors), at] for c in range(3)]
-            row = [e8_ref[i : i + 1, at] for i in range(8)]
-            head, turn = row[0:3], row[5:8]
-            u = head[0] * m[0] + head[1] * m[1] + head[2] * m[2]
-            radial = row[4] * u + (turn[0] * m[0] + turn[1] * m[1] + turn[2] * m[2])
-            sums, evens = [None] * 3, [None] * 3
-            for k in range(basis):
-                slope = ef_ref[k : k + 1, at]
-                even = ee_ref[k : k + 1, at]
-                radial = radial + slope * coeff[k]
+    lax.fori_loop(0, pairs, mix_step, 0, unroll=8)
+
+    total = None
+    step = max(groups // 4, 1)
+    for first in range(0, groups, step):
+        for tile in range(tiles):
+            coeff = [cs_ref[i, tile * 8 : tile * 8 + 8, :] for i in range(4 * basis)]
+            for j in range(first, first + step):
+                at = slice(j * lanes, (j + 1) * lanes)
+                m = [mv_ref[rows_of(tile, c, vectors), at] for c in range(3)]
+                row = [e8_ref[i : i + 1, at] for i in range(8)]
+                head, turn = row[0:3], row[5:8]
+                u = head[0] * m[0] + head[1] * m[1] + head[2] * m[2]
+                radial = row[4] * u + (turn[0] * m[0] + turn[1] * m[1] + turn[2] * m[2])
+                sums, evens = [None] * 3, [None] * 3
+                for k in range(basis):
+                    slope = ef_ref[k : k + 1, at]
+                    even = ee_ref[k : k + 1, at]
+                    radial = radial + slope * coeff[k]
+                    for c in range(3):
+                        i = (c + 1) * basis + k
+                        more, plus = slope * coeff[i], even * coeff[i]
+                        sums[c] = more if k == 0 else sums[c] + more
+                        evens[c] = plus if k == 0 else evens[c] + plus
                 for c in range(3):
-                    i = (c + 1) * basis + k
-                    more, plus = slope * coeff[i], even * coeff[i]
-                    sums[c] = more if k == 0 else sums[c] + more
-                    evens[c] = plus if k == 0 else evens[c] + plus
-            for c in range(3):
-                radial = radial + head[c] * (sums[c] - evens[c])
-            for c in range(3):
-                out = evens[c] + head[c] * radial + (row[3] * m[c] + turn[c] * u)
-                eo_ref[rows_of(tile, c, vectors), at] = out
-            return carry
-
-        lax.fori_loop(0, groups, spread_step, 0, unroll=groups)
-
-    both = dot16(split(eo_ref[...], 2), dm_ref[...], NT)
-    return both[:vec3] + both[vec3:]
+                    radial = radial + head[c] * (sums[c] - evens[c])
+                for c in range(3):
+                    eo_ref[rows_of(tile, c, vectors), at] = (
+                        evens[c] + head[c] * radial + (row[3] * m[c] + turn[c] * u)
+                    )
+        at = slice(first * lanes, (first + step) * lanes)
+        both = dot16(split(eo_ref[:, at], 2), dm_ref[:, at], NT)
+        part = both[:vec3] + both[vec3:]
+        total = part if total is None else total + part
+    return total
 
 
 def stacked_sums(parts):
@@ -455,8 +457,8 @@
         put(i, basis, tiles)
         return carry
 
-    lax.fori_loop(0, basis // 2, upper_step, 0)
-    lax.fori_loop(0, basis // 2, lower_step, 0)
+    lax.fori_loop(0, basis // 2, upper_step, 0, unroll=True)
+    lax.fori_loop(0, basis // 2, lower_step, 0, unroll=True)
 
 
 def first_kernel(

time: 79.5 us -> 78.5 us (0.987)
  Pallas kernels: 23.2 us -> 22.2 us
    pallas_call x8, Pallas kernels: 23.2 us -> 22.2 us  [call(): pl.pallas_call(kernel, out_shape=outs, in_specs=[pl.BlockSpec(memory_spac...]
  transfers between devices with their start and end apart: 19 -> 19, of which waited for: 13 -> 13; matrix products, arithmetic and copies ran while one was open for 1% -> 2% of each run, Pallas kernels for 2% -> 2%
where the time goes in v4:
time: 78.5 us; the launch traced here: 78.3 us
  waiting for transfers between devices  23.7 us (30%)
  Pallas kernels  22.2 us (28%)
  starting transfers between devices  21.1 us (27%)
  blocking collectives  8.28 us (11%)
  other arithmetic  2.2 us (3%)
  between operations  0.79 us (1%)
    ppermute x19, waiting for transfers between devices, fetch(): return lax.ppermute(values, axis, [(s, i) for i, s in enumerate(sources)])  23.7 us
    pallas_call x8, Pallas kernels, call(): pl.pallas_call(kernel, out_shape=outs, in_specs=[pl.BlockSpec(memory_spac...  22.2 us
    ppermute x19, starting transfers between devices, fetch(): return lax.ppermute(values, axis, [(s, i) for i, s in enumerate(sources)])  21.1 us
    all_to_all x1, blocking collectives, shards(): got = lax.all_to_all(spread_sums, 'gx', 0, 0)  8.28 us
    add x2, other arithmetic, laid(): total = placed if total is None else total + placed  1.88 us
  transfers between devices with their start and end apart: 19, of which 13 were waited for; matrix products, arithmetic and copies ran while one was open for 2% of the time, Pallas kernels for 2%

profile of v4, /device:TPU:0, one launch (start us, length us, event | category | flops | bytes accessed | tf_op | source)
XLA Modules:
  0.0 78.3 jit_solution(8081449429930499100)
XLA Ops:
  0.6 1.0 %convert_add_fusion.1.table.cown = f32[104,128]{1,0:T(8,128)S(1)} fusion(s32[2,64]{1,0:T(2,128)} %bitcast.23, s32[2,64]{1,0:T(2,128)} %bitcast.24, f32[3,64]{1,0:T(4,128)} %param.11, f32[96,64]{1,0:T(8,128)} %bitcast.21, f32[96,64]{1,0:T(8,128)} %bitcast.22), kind=kLoop, calls=%fused_computation.8 | loop fusion | flops 79872 | bytes 104192 | tf_op jit(solution)/shard_map/add | solution.py:731
  1.6 4.6 %collective-permute-start.1 = (f32[104,128]{1,0:T(8,128)S(1)}, f32[104,128]{1,0:T(8,128)S(1)}, u32[]{:S(2)}, u32[]{:S(2)}) collective-permute-start(f32[104,128]{1,0:T(8,128)S(1)} %convert_add_fusion.1.table.cown), channel_id=1, source_target_pairs={{28,0},{8,4},{4,8},{16,12},{12,16},{24,20},{20,24},{0,28},{29,1},{... | collective-permute-start | bytes 159752 | tf_op jit(solution)/shard_map/ppermute | solution.py:706
  6.1 0.0 collective-permute-start
  6.1 0.1 pad_add_fusion.2.sides
  6.2 1.8 %collective-permute-done.1.from_other = f32[104,128]{1,0:T(8,128)S(1)} collective-permute-done((f32[104,128]{1,0:T(8,128)S(1)}, f32[104,128]{1,0:T(8,128)S(1)}, u32[]{:S(2)}, u32[]{:S(2)}) %collective-permute-start.1) | collective-permute-done | bytes 53280 | tf_op jit(solution)/shard_map/ppermute | solution.py:706
  8.1 1.2 %shard_map.122 = (f32[104,128]{1,0:T(8,128)S(1)}, f32[104,128]{1,0:T(8,128)S(1)}, f32[200,192]{1,0:T(8,128)S(1)}) custom-call(s32[2]{0:T(128)S(1)} %pad_add_fusion.2.sides, f32[104,128]{1,0:T(8,128)S(1)} %convert_add_fusion.1.table.cown, f32[104,128]{1,0:T(8,128)S(1)} %collective-permute-done.from_mate, f32[104,128]{1,0:T(8,128)S(1)} %collective-permute-done.1.from_other), custom_call_target="tpu_custom_call" | custom-call | flops 1048576 | bytes 65536 | tf_op jit(solution)/shard_map/pallas_call | solution.py:712
  9.2 2.2 %collective-permute-start.2 = (f32[104,128]{1,0:T(8,128)S(1)}, f32[104,128]{1,0:T(8,128)S(1)}, u32[]{:S(2)}, u32[]{:S(2)}) collective-permute-start(f32[104,128]{1,0:T(8,128)S(1)} %get-tuple-element.38), channel_id=1, source_target_pairs={{1,0},{0,1},{3,2},{2,3},{5,4},{4,5},{7,6},{6,7},{9,8},{8,9},{11,10... | collective-permute-start | bytes 159752 | tf_op jit(solution)/shard_map/ppermute | solution.py:706
  11.5 1.5 %collective-permute-start.3 = (f32[104,128]{1,0:T(8,128)S(1)}, f32[104,128]{1,0:T(8,128)S(1)}, u32[]{:S(2)}, u32[]{:S(2)}) collective-permute-start(f32[104,128]{1,0:T(8,128)S(1)} %get-tuple-element.39), channel_id=1, source_target_pairs={{3,0},{2,1},{1,2},{0,3},{7,4},{6,5},{5,6},{4,7},{11,8},{10,9},{9,1... | collective-permute-start | bytes 159752 | tf_op jit(solution)/shard_map/ppermute | solution.py:706
  13.0 0.9 %convert_add_fusion.table = f32[192,128]{1,0:T(8,128)S(1)} fusion(s32[1,64]{1,0:T(1,128)} %bitcast.25, s32[32,64]{1,0:T(8,128)} %param.14, f32[1,128]{1,0:T(1,128)} %bitcast.26, f32[8,128]{1,0:T(8,128)} %param.19, f32[8,128]{1,0:T(8,128)} %param.18, f32[128,128]{1,0:T(8,128)} %param.20), kind=kLoop, calls=%fused_computation.3 | loop fusion | flops 172032 | bytes 180992 | tf_op jit(solution)/shard_map/add | solution.py:731
  13.9 0.7 shard_map.123
  14.7 0.0 collective-permute-done.2.from_mate
  14.7 1.8 %collective-permute-done.3.from_other = f32[104,128]{1,0:T(8,128)S(1)} collective-permute-done((f32[104,128]{1,0:T(8,128)S(1)}, f32[104,128]{1,0:T(8,128)S(1)}, u32[]{:S(2)}, u32[]{:S(2)}) %collective-permute-start.3) | collective-permute-done | bytes 53280 | tf_op jit(solution)/shard_map/ppermute | solution.py:706
  16.5 8.6 %shard_map.124 = (f32[144,128]{1,0:T(8,128)S(1)}, f32[144,128]{1,0:T(8,128)S(1)}, f32[144,128]{1,0:T(8,128)S(1)}, f32[96,320]{1,0:T(8,128)S(1)}, f32[96,320]{1,0...) custom-call(s32[2]{0:T(128)S(1)} %pad_add_fusion.2.sides, ...), custom_call_target="tpu_custom_call" | custom-call | flops 2147483648 | bytes 65536 | tf_op jit(solution)/shard_map/pallas_call | solution.py:712
  25.1 0.1 collective-permute-start.4
  25.2 1.9 %collective-permute-start.5 = (f32[144,128]{1,0:T(8,128)S(1)}, f32[144,128]{1,0:T(8,128)S(1)}, u32[]{:S(2)}, u32[]{:S(2)}) collective-permute-start(f32[144,128]{1,0:T(8,128)S(1)} %get-tuple-element.51), channel_id=1, source_target_pairs={{28,0},{8,4},{4,8},{16,12},{12,16},{24,20},{20,24},{0,28},{29,1},{... | collective-permute-start | bytes 221192 | tf_op jit(solution)/shard_map/ppermute | solution.py:706
  27.1 0.5 shard_map.125
  27.5 0.1 collective-permute-start.6
  27.6 1.2 %collective-permute-done.6 = f32[32,128]{1,0:T(8,128)S(1)} collective-permute-done((f32[32,128]{1,0:T(8,128)S(1)}, f32[32,128]{1,0:T(8,128)S(1)}, u32[]{:S(2)}, u32[]{:S(2)}) %collective-permute-start.6) | collective-permute-done | bytes 16416 | tf_op jit(solution)/shard_map/ppermute | solution.py:706
  28.8 2.1 %collective-permute-done.5 = f32[144,128]{1,0:T(8,128)S(1)} collective-permute-done((f32[144,128]{1,0:T(8,128)S(1)}, f32[144,128]{1,0:T(8,128)S(1)}, u32[]{:S(2)}, u32[]{:S(2)}) %collective-permute-start.5) | collective-permute-done | bytes 73760 | tf_op jit(solution)/shard_map/ppermute | solution.py:706
  30.9 0.7 collective-permute-start.7
  31.6 1.4 %collective-permute-start.8 = (f32[128,128]{1,0:T(8,128)S(1)}, f32[128,128]{1,0:T(8,128)S(1)}, u32[]{:S(2)}, u32[]{:S(2)}) collective-permute-start(f32[128,128]{1,0:T(8,128)S(1)} %get-tuple-element.79), channel_id=1, source_target_pairs={{2,0},{3,1},{0,2},{1,3},{6,4},{7,5},{4,6},{5,7},{10,8},{11,9},{8,1... | collective-permute-start | bytes 196616 | tf_op jit(solution)/shard_map/ppermute | solution.py:706
  33.0 1.4 %collective-permute-start.9 = (f32[128,128]{1,0:T(8,128)S(1)}, f32[128,128]{1,0:T(8,128)S(1)}, u32[]{:S(2)}, u32[]{:S(2)}) collective-permute-start(f32[128,128]{1,0:T(8,128)S(1)} %get-tuple-element.80), channel_id=1, source_target_pairs={{3,0},{2,1},{1,2},{0,3},{7,4},{6,5},{5,6},{4,7},{11,8},{10,9},{9,1... | collective-permute-start | bytes 196616 | tf_op jit(solution)/shard_map/ppermute | solution.py:706
  34.5 0.8 collective-permute-done.7
  35.2 0.8 collective-permute-done.8
  36.0 2.2 %collective-permute-done.9 = f32[128,128]{1,0:T(8,128)S(1)} collective-permute-done((f32[128,128]{1,0:T(8,128)S(1)}, f32[128,128]{1,0:T(8,128)S(1)}, u32[]{:S(2)}, u32[]{:S(2)}) %collective-permute-start.9) | collective-permute-done | bytes 65568 | tf_op jit(solution)/shard_map/ppermute | solution.py:706
  38.2 0.1 collective-permute-start.13
  38.3 0.9 %collective-permute-start.12 = (f32[32,128]{1,0:T(8,128)S(1)}, f32[32,128]{1,0:T(8,128)S(1)}, u32[]{:S(2)}, u32[]{:S(2)}) collective-permute-start(f32[32,128]{1,0:T(8,128)S(1)} %fusion.1), channel_id=1, source_target_pairs={{8,0},{28,4},{16,8},{4,12},{24,16},{12,20},{0,24},{20,28},{9,1},{2... | collective-permute-start | bytes 49160 | tf_op jit(solution)/shard_map/ppermute | solution.py:706
  39.2 0.1 collective-permute-start.11
  39.3 1.5 %collective-permute-start.10 = (f32[176,128]{1,0:T(8,128)S(1)}, f32[176,128]{1,0:T(8,128)S(1)}, u32[]{:S(2)}, u32[]{:S(2)}) collective-permute-start(f32[176,128]{1,0:T(8,128)S(1)} %pad_maximum_fusion.3.own), channel_id=1, source_target_pairs={{4,0},{0,4},{12,8},{8,12},{20,16},{16,20},{28,24},{24,28},{5,1},{1... | collective-permute-start | bytes 270344 | tf_op jit(solution)/shard_map/ppermute | solution.py:706
  40.8 0.1 pad_add_fusion.1.order
  40.9 2.1 %collective-permute-done.13.rest_1_ = f32[32,128]{1,0:T(8,128)S(1)} collective-permute-done((f32[32,128]{1,0:T(8,128)S(1)}, f32[32,128]{1,0:T(8,128)S(1)}, u32[]{:S(2)}, u32[]{:S(2)}) %collective-permute-start.13) | collective-permute-done | bytes 16416 | tf_op jit(solution)/shard_map/ppermute | solution.py:706
  43.0 0.0 collective-permute-done.12.rest_0_
  43.0 2.8 %collective-permute-done.11.other = f32[176,128]{1,0:T(8,128)S(1)} collective-permute-done((f32[176,128]{1,0:T(8,128)S(1)}, f32[176,128]{1,0:T(8,128)S(1)}, u32[]{:S(2)}, u32[]{:S(2)}) %collective-permute-start.11) | collective-permute-done | bytes 90144 | tf_op jit(solution)/shard_map/ppermute | solution.py:706
  45.8 6.2 %shard_map.126 = (f32[144,128]{1,0:T(8,128)S(1)}, f32[144,128]{1,0:T(8,128)S(1)}, f32[144,128]{1,0:T(8,128)S(1)}, f32[64,128]{1,0:T(8,128)S(1)}, f32[48,128]{1,0...) custom-call(s32[4]{0:T(128)S(1)} %pad_add_fusion.1.order, f32[176,128]{1,0:T(8,128)S(1)} %pad_maximum_fusion.3.own, ...), custom_call_target="tpu_custom_call" | custom-call | flops 1073741824 | bytes 65536 | tf_op jit(solution)/shard_map/pallas_call | solution.py:712
  52.0 0.1 collective-permute-start.14
  52.1 1.1 %collective-permute-start.15 = (f32[144,128]{1,0:T(8,128)S(1)}, f32[144,128]{1,0:T(8,128)S(1)}, u32[]{:S(2)}, u32[]{:S(2)}) collective-permute-start(f32[144,128]{1,0:T(8,128)S(1)} %get-tuple-element.63), channel_id=1, source_target_pairs={{28,0},{8,4},{4,8},{16,12},{12,16},{24,20},{20,24},{0,28},{29,1},{... | collective-permute-start | bytes 221192 | tf_op jit(solution)/shard_map/ppermute | solution.py:706
  53.1 0.3 shard_map.127
  53.4 4.3 %collective-permute-done.15 = f32[144,128]{1,0:T(8,128)S(1)} collective-permute-done((f32[144,128]{1,0:T(8,128)S(1)}, f32[144,128]{1,0:T(8,128)S(1)}, u32[]{:S(2)}, u32[]{:S(2)}) %collective-permute-start.15) | collective-permute-done | bytes 73760 | tf_op jit(solution)/shard_map/ppermute | solution.py:706
  57.8 1.2 %collective-permute-start.18 = (f32[160,128]{1,0:T(8,128)S(1)}, f32[160,128]{1,0:T(8,128)S(1)}, u32[]{:S(2)}, u32[]{:S(2)}) collective-permute-start(f32[160,128]{1,0:T(8,128)S(1)} %pad_maximum_fusion.4.own), channel_id=1, source_target_pairs={{2,0},{3,1},{0,2},{1,3},{6,4},{7,5},{4,6},{5,7},{10,8},{11,9},{8,1... | collective-permute-start | bytes 245768 | tf_op jit(solution)/shard_map/ppermute | solution.py:706
  58.9 1.8 %collective-permute-start.17 = (f32[160,128]{1,0:T(8,128)S(1)}, f32[160,128]{1,0:T(8,128)S(1)}, u32[]{:S(2)}, u32[]{:S(2)}) collective-permute-start(f32[160,128]{1,0:T(8,128)S(1)} %pad_maximum_fusion.4.own), channel_id=1, source_target_pairs={{3,0},{2,1},{1,2},{0,3},{7,4},{6,5},{5,6},{4,7},{11,8},{10,9},{9,1... | collective-permute-start | bytes 245768 | tf_op jit(solution)/shard_map/ppermute | solution.py:706
  60.8 0.5 collective-permute-start.16
  61.3 0.1 pad_add_fusion.order
  61.4 1.1 %collective-permute-done.18.far = f32[160,128]{1,0:T(8,128)S(1)} collective-permute-done((f32[160,128]{1,0:T(8,128)S(1)}, f32[160,128]{1,0:T(8,128)S(1)}, u32[]{:S(2)}, u32[]{:S(2)}) %collective-permute-start.18) | collective-permute-done | bytes 81952 | tf_op jit(solution)/shard_map/ppermute | solution.py:706
  62.5 1.7 %collective-permute-done.17.other = f32[160,128]{1,0:T(8,128)S(1)} collective-permute-done((f32[160,128]{1,0:T(8,128)S(1)}, f32[160,128]{1,0:T(8,128)S(1)}, u32[]{:S(2)}, u32[]{:S(2)}) %collective-permute-start.17) | collective-permute-done | bytes 81952 | tf_op jit(solution)/shard_map/ppermute | solution.py:706
  64.3 0.9 %collective-permute-done.16.mate = f32[160,128]{1,0:T(8,128)S(1)} collective-permute-done((f32[160,128]{1,0:T(8,128)S(1)}, f32[160,128]{1,0:T(8,128)S(1)}, u32[]{:S(2)}, u32[]{:S(2)}) %collective-permute-start.16) | collective-permute-done | bytes 81952 | tf_op jit(solution)/shard_map/ppermute | solution.py:706
  65.2 0.9 %shard_map.128 = (f32[8,16,128]{2,1,0:T(8,128)S(1)}, f32[48,128]{1,0:T(8,128)S(1)}) custom-call(s32[4]{0:T(128)S(1)} %pad_add_fusion.order, f32[160,128]{1,0:T(8,128)S(1)} %pad_maximum_fusion.4.own, f32[160,128]{1,0:T(8,128)S(1)} %collective-permute-done.16.mate, f32[160,128]{1,0:T(8,128)S(1)} %collective-permute-done.17.other, ...), custom_call_target="tpu_custom_call" | custom-call | flops 1048576 | bytes 65536 | tf_op jit(solution)/shard_map/pallas_call | solution.py:712
  66.1 8.3 %all_to_all.5.got = f32[8,16,128]{2,1,0:T(8,128)S(1)} all-to-all(f32[8,16,128]{2,1,0:T(8,128)S(1)} %get-tuple-element.66), channel_id=1, replica_groups=mesh['gx'=8,'gy'=4] {'gx'}, dimensions={0} | all-to-all | bytes 131072 | tf_op jit(solution)/shard_map/all_to_all | solution.py:928
  74.4 3.9 %shard_map.129 = (f32[2,3,32,64]{3,2,1,0:T(8,128)}, f32[2,32,32]{2,1,0:T(8,128)}) custom-call(f32[8,16,128]{2,1,0:T(8,128)S(1)} %all_to_all.5.got, f32[64,128]{1,0:T(8,128)S(1)} %get-tuple-element.67.sums, f32[48,128]{1,0:T(8,128)S(1)} %get-tuple-element.68.rown, f32[48,128]{1,0:T(8,128)S(1)} %get-tuple-element.69.yown, ...), custom_call_target="tpu_custom_call" | custom-call | flops 1048576 | bytes 65536 | tf_op jit(solution)/shard_map/pallas_call | solution.py:712
  (14 shorter events, 0.1 us)
Async XLA Ops:
  1.6 6.5 %collective-permute-start.1 = (f32[104,128]{1,0:T(8,128)S(1)}, f32[104,128]{1,0:T(8,128)S(1)}, u32[]{:S(2)}, u32[]{:S(2)}) collective-permute-start(f32[104,128]{1,0:T(8,128)S(1)} %convert_add_fusion.1.table.cown), channel_id=1, source_target_pairs={{28,0},{8,4},{4,8},{16,12},{12,16},{24,20},{20,24},{0,28},{29,1},{... | collective-permute-start | bytes 159752 | tf_op jit(solution)/shard_map/ppermute | solution.py:706
  6.1 1.9 %collective-permute-start = (f32[104,128]{1,0:T(8,128)S(1)}, f32[104,128]{1,0:T(8,128)S(1)}, u32[]{:S(2)}, u32[]{:S(2)}) collective-permute-start(f32[104,128]{1,0:T(8,128)S(1)} %convert_add_fusion.1.table.cown), channel_id=1, source_target_pairs={{4,0},{0,4},{12,8},{8,12},{20,16},{16,20},{28,24},{24,28},{5,1},{1... | collective-permute-start | bytes 159752 | tf_op jit(solution)/shard_map/ppermute | solution.py:706
  9.2 5.4 %collective-permute-start.2 = (f32[104,128]{1,0:T(8,128)S(1)}, f32[104,128]{1,0:T(8,128)S(1)}, u32[]{:S(2)}, u32[]{:S(2)}) collective-permute-start(f32[104,128]{1,0:T(8,128)S(1)} %get-tuple-element.38), channel_id=1, source_target_pairs={{1,0},{0,1},{3,2},{2,3},{5,4},{4,5},{7,6},{6,7},{9,8},{8,9},{11,10... | collective-permute-start | bytes 159752 | tf_op jit(solution)/shard_map/ppermute | solution.py:706
  11.5 5.0 %collective-permute-start.3 = (f32[104,128]{1,0:T(8,128)S(1)}, f32[104,128]{1,0:T(8,128)S(1)}, u32[]{:S(2)}, u32[]{:S(2)}) collective-permute-start(f32[104,128]{1,0:T(8,128)S(1)} %get-tuple-element.39), channel_id=1, source_target_pairs={{3,0},{2,1},{1,2},{0,3},{7,4},{6,5},{5,6},{4,7},{11,8},{10,9},{9,1... | collective-permute-start | bytes 159752 | tf_op jit(solution)/shard_map/ppermute | solution.py:706
  25.1 3.7 %collective-permute-start.4 = (f32[144,128]{1,0:T(8,128)S(1)}, f32[144,128]{1,0:T(8,128)S(1)}, u32[]{:S(2)}, u32[]{:S(2)}) collective-permute-start(f32[144,128]{1,0:T(8,128)S(1)} %get-tuple-element.50), channel_id=1, source_target_pairs={{4,0},{0,4},{12,8},{8,12},{20,16},{16,20},{28,24},{24,28},{5,1},{1... | collective-permute-start | bytes 221192 | tf_op jit(solution)/shard_map/ppermute | solution.py:706
  25.2 5.6 %collective-permute-start.5 = (f32[144,128]{1,0:T(8,128)S(1)}, f32[144,128]{1,0:T(8,128)S(1)}, u32[]{:S(2)}, u32[]{:S(2)}) collective-permute-start(f32[144,128]{1,0:T(8,128)S(1)} %get-tuple-element.51), channel_id=1, source_target_pairs={{28,0},{8,4},{4,8},{16,12},{12,16},{24,20},{20,24},{0,28},{29,1},{... | collective-permute-start | bytes 221192 | tf_op jit(solution)/shard_map/ppermute | solution.py:706
  27.5 1.2 %collective-permute-start.6 = (f32[32,128]{1,0:T(8,128)S(1)}, f32[32,128]{1,0:T(8,128)S(1)}, u32[]{:S(2)}, u32[]{:S(2)}) collective-permute-start(f32[32,128]{1,0:T(8,128)S(1)} %shard_map.125), channel_id=1, source_target_pairs={{4,0},{0,4},{12,8},{8,12},{20,16},{16,20},{28,24},{24,28},{5,1},{1... | collective-permute-start | bytes 49160 | tf_op jit(solution)/shard_map/ppermute | solution.py:706
  30.9 4.3 %collective-permute-start.7 = (f32[128,128]{1,0:T(8,128)S(1)}, f32[128,128]{1,0:T(8,128)S(1)}, u32[]{:S(2)}, u32[]{:S(2)}) collective-permute-start(f32[128,128]{1,0:T(8,128)S(1)} %get-tuple-element.78), channel_id=1, source_target_pairs={{1,0},{0,1},{3,2},{2,3},{5,4},{4,5},{7,6},{6,7},{9,8},{8,9},{11,10... | collective-permute-start | bytes 196616 | tf_op jit(solution)/shard_map/ppermute | solution.py:706
  31.6 4.4 %collective-permute-start.8 = (f32[128,128]{1,0:T(8,128)S(1)}, f32[128,128]{1,0:T(8,128)S(1)}, u32[]{:S(2)}, u32[]{:S(2)}) collective-permute-start(f32[128,128]{1,0:T(8,128)S(1)} %get-tuple-element.79), channel_id=1, source_target_pairs={{2,0},{3,1},{0,2},{1,3},{6,4},{7,5},{4,6},{5,7},{10,8},{11,9},{8,1... | collective-permute-start | bytes 196616 | tf_op jit(solution)/shard_map/ppermute | solution.py:706
  33.0 5.2 %collective-permute-start.9 = (f32[128,128]{1,0:T(8,128)S(1)}, f32[128,128]{1,0:T(8,128)S(1)}, u32[]{:S(2)}, u32[]{:S(2)}) collective-permute-start(f32[128,128]{1,0:T(8,128)S(1)} %get-tuple-element.80), channel_id=1, source_target_pairs={{3,0},{2,1},{1,2},{0,3},{7,4},{6,5},{5,6},{4,7},{11,8},{10,9},{9,1... | collective-permute-start | bytes 196616 | tf_op jit(solution)/shard_map/ppermute | solution.py:706
  38.2 4.8 %collective-permute-start.13 = (f32[32,128]{1,0:T(8,128)S(1)}, f32[32,128]{1,0:T(8,128)S(1)}, u32[]{:S(2)}, u32[]{:S(2)}) collective-permute-start(f32[32,128]{1,0:T(8,128)S(1)} %fusion.1), channel_id=1, source_target_pairs={{16,0},{20,4},{24,8},{28,12},{0,16},{4,20},{8,24},{12,28},{17,1},{... | collective-permute-start | bytes 49160 | tf_op jit(solution)/shard_map/ppermute | solution.py:706
  38.3 4.7 %collective-permute-start.12 = (f32[32,128]{1,0:T(8,128)S(1)}, f32[32,128]{1,0:T(8,128)S(1)}, u32[]{:S(2)}, u32[]{:S(2)}) collective-permute-start(f32[32,128]{1,0:T(8,128)S(1)} %fusion.1), channel_id=1, source_target_pairs={{8,0},{28,4},{16,8},{4,12},{24,16},{12,20},{0,24},{20,28},{9,1},{2... | collective-permute-start | bytes 49160 | tf_op jit(solution)/shard_map/ppermute | solution.py:706
  39.2 6.6 %collective-permute-start.11 = (f32[176,128]{1,0:T(8,128)S(1)}, f32[176,128]{1,0:T(8,128)S(1)}, u32[]{:S(2)}, u32[]{:S(2)}) collective-permute-start(f32[176,128]{1,0:T(8,128)S(1)} %pad_maximum_fusion.3.own), channel_id=1, source_target_pairs={{28,0},{8,4},{4,8},{16,12},{12,16},{24,20},{20,24},{0,28},{29,1},{... | collective-permute-start | bytes 270344 | tf_op jit(solution)/shard_map/ppermute | solution.py:706
  39.3 6.5 %collective-permute-start.10 = (f32[176,128]{1,0:T(8,128)S(1)}, f32[176,128]{1,0:T(8,128)S(1)}, u32[]{:S(2)}, u32[]{:S(2)}) collective-permute-start(f32[176,128]{1,0:T(8,128)S(1)} %pad_maximum_fusion.3.own), channel_id=1, source_target_pairs={{4,0},{0,4},{12,8},{8,12},{20,16},{16,20},{28,24},{24,28},{5,1},{1... | collective-permute-start | bytes 270344 | tf_op jit(solution)/shard_map/ppermute | solution.py:706
  52.0 1.4 %collective-permute-start.14 = (f32[144,128]{1,0:T(8,128)S(1)}, f32[144,128]{1,0:T(8,128)S(1)}, u32[]{:S(2)}, u32[]{:S(2)}) collective-permute-start(f32[144,128]{1,0:T(8,128)S(1)} %get-tuple-element.62), channel_id=1, source_target_pairs={{4,0},{0,4},{12,8},{8,12},{20,16},{16,20},{28,24},{24,28},{5,1},{1... | collective-permute-start | bytes 221192 | tf_op jit(solution)/shard_map/ppermute | solution.py:706
  52.1 5.6 %collective-permute-start.15 = (f32[144,128]{1,0:T(8,128)S(1)}, f32[144,128]{1,0:T(8,128)S(1)}, u32[]{:S(2)}, u32[]{:S(2)}) collective-permute-start(f32[144,128]{1,0:T(8,128)S(1)} %get-tuple-element.63), channel_id=1, source_target_pairs={{28,0},{8,4},{4,8},{16,12},{12,16},{24,20},{20,24},{0,28},{29,1},{... | collective-permute-start | bytes 221192 | tf_op jit(solution)/shard_map/ppermute | solution.py:706
  57.8 4.8 %collective-permute-start.18 = (f32[160,128]{1,0:T(8,128)S(1)}, f32[160,128]{1,0:T(8,128)S(1)}, u32[]{:S(2)}, u32[]{:S(2)}) collective-permute-start(f32[160,128]{1,0:T(8,128)S(1)} %pad_maximum_fusion.4.own), channel_id=1, source_target_pairs={{2,0},{3,1},{0,2},{1,3},{6,4},{7,5},{4,6},{5,7},{10,8},{11,9},{8,1... | collective-permute-start | bytes 245768 | tf_op jit(solution)/shard_map/ppermute | solution.py:706
  58.9 5.3 %collective-permute-start.17 = (f32[160,128]{1,0:T(8,128)S(1)}, f32[160,128]{1,0:T(8,128)S(1)}, u32[]{:S(2)}, u32[]{:S(2)}) collective-permute-start(f32[160,128]{1,0:T(8,128)S(1)} %pad_maximum_fusion.4.own), channel_id=1, source_target_pairs={{3,0},{2,1},{1,2},{0,3},{7,4},{6,5},{5,6},{4,7},{11,8},{10,9},{9,1... | collective-permute-start | bytes 245768 | tf_op jit(solution)/shard_map/ppermute | solution.py:706
  60.8 4.4 %collective-permute-start.16 = (f32[160,128]{1,0:T(8,128)S(1)}, f32[160,128]{1,0:T(8,128)S(1)}, u32[]{:S(2)}, u32[]{:S(2)}) collective-permute-start(f32[160,128]{1,0:T(8,128)S(1)} %pad_maximum_fusion.4.own), channel_id=1, source_target_pairs={{1,0},{0,1},{3,2},{2,3},{5,4},{4,5},{7,6},{6,7},{9,8},{8,9},{11,10... | collective-permute-start | bytes 245768 | tf_op jit(solution)/shard_map/ppermute | solution.py:706

commit v5 on v4

--- a/solution.py
+++ b/solution.py
@@ -339,8 +339,8 @@
         got = dot16(parts16, dm[:, at])
         mv[:, at] = got[:vec3] + got[vec3 : 2 * vec3]
         third = 2 * vec3
-        delta = got[third : third + 24] + got[third + 32 : third + 56] + got[third + 64 : third + 88]
-        d = [delta[8 * c : 8 * c + 8] for c in range(3)]
+        delta = got[third : third + 8] + got[third + 16 : third + 24] + got[third + 32 : third + 40]
+        d = [jnp.broadcast_to(delta[c : c + 1], delta.shape) for c in range(3)]
         squared = d[0] * d[0] + d[1] * d[1] + d[2] * d[2] + SOFTEN
         radius = jnp.sqrt(squared)
         inverse = 1.0 / radius
@@ -483,12 +483,10 @@
     places = jnp.round(rows[base + 3 : base + 4]).astype(jnp.int32)
     index[...] = jnp.broadcast_to(places, index.shape)
     shape = (8, rows.shape[1])
-    place = jnp.concatenate(
-        [jnp.broadcast_to(rows[base + c : base + c + 1], shape) for c in range(3)] + [jnp.zeros(shape, jnp.float32)],
-        axis=0,
-    )
+    place = jnp.concatenate([rows[base : base + 8], jnp.zeros(shape, jnp.float32)], axis=0)
     parts16 = jnp.concatenate([split(rows[:vec3], 2), split(place, 3)], axis=0)
     descr = gather_edges(parts16, dm, valid, mv, ef, ee, f2s, hs, vec3, lanes)
+    contract(mv, ef, ee, lambda c, at: hs[8 * c : 8 * c + 8, at], xs, sx, atoms)
 
     rad, vec, mix = w_rad[...], w_vec[...], w_mix[...]
     radt, vect, mixt, outt = rad_t[...], vec_t[...], mix_t[...], out_t[:, 0:1]
@@ -502,7 +500,6 @@
     alpha = dot32(rad, u)
     beta = [2.0 * dot32(vec, flow[c] * u) for c in range(3)]
     edge_rows(alpha, beta, ef, ee, f2s, hs, e8, lanes)
-    contract(mv, ef, ee, lambda c, at: hs[8 * c : 8 * c + 8, at], xs, sx, atoms)
     channel_lift(flow, radt, vect, mixt, qs, qr, lanes, atoms)
     descriptor_curvature(vec, u, bend, qs, qr, bd, both, pmat, rmat, lanes, atoms)
 
@@ -628,12 +625,12 @@
     send_sums(pairs, product(y, y, vectors), out)
 
 
-def cholesky(matrix, *extra):
+def cholesky(matrix, lower, *extra):
     size = matrix.shape[0]
     rows, cols = rows_and_cols(size)
     unit = (rows == cols).astype(jnp.float32)
     work = jnp.concatenate([matrix, unit, *extra], axis=1)
-    columns = [jnp.broadcast_to(matrix[:, k : k + 1], work.shape) for k in range(size)]
+    columns = [jnp.broadcast_to(lower[:, k : k + 1], work.shape) for k in range(size)]
     lines = []
     for j in range(0, size, 2):
         first, second = columns[j], columns[j + 1]
@@ -643,9 +640,8 @@
         ai, bi, di = a * inverse, b * inverse, d * inverse
         keep = (j + 2) // 8 * 8
         for k in range(j + 2, size):
-            low = columns[k]
-            x0, x1 = low[j : j + 1], low[j + 1 : j + 2]
-            low = low[keep:] - (first[keep:] * (di * x0 - bi * x1) + second[keep:] * (ai * x1 - bi * x0))
+            x0, x1 = first[k : k + 1], second[k : k + 1]
+            low = columns[k][keep:] - (first[keep:] * (di * x0 - bi * x1) + second[keep:] * (ai * x1 - bi * x0))
             columns[k] = jnp.concatenate([columns[k][:keep], low], axis=0) if keep else low
         r0, r1 = work[j : j + 1], work[j + 1 : j + 2]
         work = work - (first * (di * r0 - bi * r1) + second * (ai * r1 - bi * r0))
@@ -678,12 +674,12 @@
     wr = rr + dot32(coef1, left, TN)
     fixed = yy + dot32(wr, dot32(gram_old[:v, :v] - 2.0 * unit, wr), TN)
 
-    upper1, inv1, along, cross = cholesky(rr, ry, left[:v].T)
+    upper1, inv1, along, cross = cholesky(rr, joined, ry, left[:v].T)
     mixed = dot32(cross, wr)
     gram2 = fixed + dot32(
         jnp.concatenate([along, mixed], axis=0), jnp.concatenate([mixed - along, along], axis=0), TN
     )
-    upper2, inv2 = cholesky(gram2)
+    upper2, inv2 = cholesky(gram2, gram2)
     factors[0] = upper1.T
     factors[1] = jnp.where(rows >= cols, dot32(inv1, upper2, NT), 0.0)
     r, y, old = unpack(rown[...], atoms), unpack(yown[...], atoms), cown[0 : 3 * vectors, 0:atoms]

time: 78.5 us -> 78.3 us (level)
  no operation moved by 1% of the time
where the time goes in v5:
time: 78.3 us; the launch traced here: 78 us
  waiting for transfers between devices  23.7 us (30%)
  Pallas kernels  21.9 us (28%)
  starting transfers between devices  21.1 us (27%)
  blocking collectives  8.28 us (11%)
  other arithmetic  2.2 us (3%)
  between operations  0.79 us (1%)
    ppermute x19, waiting for transfers between devices, fetch(): return lax.ppermute(values, axis, [(s, i) for i, s in enumerate(sources)])  23.7 us
    pallas_call x8, Pallas kernels, call(): pl.pallas_call(kernel, out_shape=outs, in_specs=[pl.BlockSpec(memory_spac...  21.9 us
    ppermute x19, starting transfers between devices, fetch(): return lax.ppermute(values, axis, [(s, i) for i, s in enumerate(sources)])  21.1 us
    all_to_all x1, blocking collectives, shards(): got = lax.all_to_all(spread_sums, 'gx', 0, 0)  8.28 us
    add x2, other arithmetic, laid(): total = placed if total is None else total + placed  1.88 us
  transfers between devices with their start and end apart: 19, of which 13 were waited for; matrix products, arithmetic and copies ran while one was open for 2% of the time, Pallas kernels for 2%

profile of v5, /device:TPU:0, one launch (start us, length us, event | category | flops | bytes accessed | tf_op | source)
XLA Modules:
  0.0 78.0 jit_solution(5769144193303688942)
XLA Ops:
  0.6 1.0 %convert_add_fusion.1.table.cown = f32[104,128]{1,0:T(8,128)S(1)} fusion(s32[2,64]{1,0:T(2,128)} %bitcast.23, s32[2,64]{1,0:T(2,128)} %bitcast.24, f32[3,64]{1,0:T(4,128)} %param.11, f32[96,64]{1,0:T(8,128)} %bitcast.21, f32[96,64]{1,0:T(8,128)} %bitcast.22), kind=kLoop, calls=%fused_computation.8 | loop fusion | flops 79872 | bytes 104192 | tf_op jit(solution)/shard_map/add | solution.py:727
  1.6 4.6 %collective-permute-start.1 = (f32[104,128]{1,0:T(8,128)S(1)}, f32[104,128]{1,0:T(8,128)S(1)}, u32[]{:S(2)}, u32[]{:S(2)}) collective-permute-start(f32[104,128]{1,0:T(8,128)S(1)} %convert_add_fusion.1.table.cown), channel_id=1, source_target_pairs={{28,0},{8,4},{4,8},{16,12},{12,16},{24,20},{20,24},{0,28},{29,1},{... | collective-permute-start | bytes 159752 | tf_op jit(solution)/shard_map/ppermute | solution.py:702
  6.1 0.0 collective-permute-start
  6.1 0.1 pad_add_fusion.2.sides
  6.2 1.8 %collective-permute-done.1.from_other = f32[104,128]{1,0:T(8,128)S(1)} collective-permute-done((f32[104,128]{1,0:T(8,128)S(1)}, f32[104,128]{1,0:T(8,128)S(1)}, u32[]{:S(2)}, u32[]{:S(2)}) %collective-permute-start.1) | collective-permute-done | bytes 53280 | tf_op jit(solution)/shard_map/ppermute | solution.py:702
  8.1 1.2 %shard_map.122 = (f32[104,128]{1,0:T(8,128)S(1)}, f32[104,128]{1,0:T(8,128)S(1)}, f32[200,192]{1,0:T(8,128)S(1)}) custom-call(s32[2]{0:T(128)S(1)} %pad_add_fusion.2.sides, f32[104,128]{1,0:T(8,128)S(1)} %convert_add_fusion.1.table.cown, f32[104,128]{1,0:T(8,128)S(1)} %collective-permute-done.from_mate, f32[104,128]{1,0:T(8,128)S(1)} %collective-permute-done.1.from_other), custom_call_target="tpu_custom_call" | custom-call | flops 1048576 | bytes 65536 | tf_op jit(solution)/shard_map/pallas_call | solution.py:708
  9.2 2.2 %collective-permute-start.2 = (f32[104,128]{1,0:T(8,128)S(1)}, f32[104,128]{1,0:T(8,128)S(1)}, u32[]{:S(2)}, u32[]{:S(2)}) collective-permute-start(f32[104,128]{1,0:T(8,128)S(1)} %get-tuple-element.38), channel_id=1, source_target_pairs={{1,0},{0,1},{3,2},{2,3},{5,4},{4,5},{7,6},{6,7},{9,8},{8,9},{11,10... | collective-permute-start | bytes 159752 | tf_op jit(solution)/shard_map/ppermute | solution.py:702
  11.5 1.5 %collective-permute-start.3 = (f32[104,128]{1,0:T(8,128)S(1)}, f32[104,128]{1,0:T(8,128)S(1)}, u32[]{:S(2)}, u32[]{:S(2)}) collective-permute-start(f32[104,128]{1,0:T(8,128)S(1)} %get-tuple-element.39), channel_id=1, source_target_pairs={{3,0},{2,1},{1,2},{0,3},{7,4},{6,5},{5,6},{4,7},{11,8},{10,9},{9,1... | collective-permute-start | bytes 159752 | tf_op jit(solution)/shard_map/ppermute | solution.py:702
  13.0 0.9 %convert_add_fusion.table = f32[192,128]{1,0:T(8,128)S(1)} fusion(s32[1,64]{1,0:T(1,128)} %bitcast.25, s32[32,64]{1,0:T(8,128)} %param.14, f32[1,128]{1,0:T(1,128)} %bitcast.26, f32[8,128]{1,0:T(8,128)} %param.19, f32[8,128]{1,0:T(8,128)} %param.18, f32[128,128]{1,0:T(8,128)} %param.20), kind=kLoop, calls=%fused_computation.3 | loop fusion | flops 172032 | bytes 180992 | tf_op jit(solution)/shard_map/add | solution.py:727
  13.9 0.7 shard_map.123
  14.7 0.0 collective-permute-done.2.from_mate
  14.7 1.8 %collective-permute-done.3.from_other = f32[104,128]{1,0:T(8,128)S(1)} collective-permute-done((f32[104,128]{1,0:T(8,128)S(1)}, f32[104,128]{1,0:T(8,128)S(1)}, u32[]{:S(2)}, u32[]{:S(2)}) %collective-permute-start.3) | collective-permute-done | bytes 53280 | tf_op jit(solution)/shard_map/ppermute | solution.py:702
  16.5 8.6 %shard_map.124 = (f32[144,128]{1,0:T(8,128)S(1)}, f32[144,128]{1,0:T(8,128)S(1)}, f32[144,128]{1,0:T(8,128)S(1)}, f32[96,320]{1,0:T(8,128)S(1)}, f32[96,320]{1,0...) custom-call(s32[2]{0:T(128)S(1)} %pad_add_fusion.2.sides, ...), custom_call_target="tpu_custom_call" | custom-call | flops 2147483648 | bytes 65536 | tf_op jit(solution)/shard_map/pallas_call | solution.py:708
  25.1 0.1 collective-permute-start.4
  25.2 1.9 %collective-permute-start.5 = (f32[144,128]{1,0:T(8,128)S(1)}, f32[144,128]{1,0:T(8,128)S(1)}, u32[]{:S(2)}, u32[]{:S(2)}) collective-permute-start(f32[144,128]{1,0:T(8,128)S(1)} %get-tuple-element.51), channel_id=1, source_target_pairs={{28,0},{8,4},{4,8},{16,12},{12,16},{24,20},{20,24},{0,28},{29,1},{... | collective-permute-start | bytes 221192 | tf_op jit(solution)/shard_map/ppermute | solution.py:702
  27.1 0.5 shard_map.125
  27.6 0.1 collective-permute-start.6
  27.6 1.2 %collective-permute-done.6 = f32[32,128]{1,0:T(8,128)S(1)} collective-permute-done((f32[32,128]{1,0:T(8,128)S(1)}, f32[32,128]{1,0:T(8,128)S(1)}, u32[]{:S(2)}, u32[]{:S(2)}) %collective-permute-start.6) | collective-permute-done | bytes 16416 | tf_op jit(solution)/shard_map/ppermute | solution.py:702
  28.8 2.1 %collective-permute-done.5 = f32[144,128]{1,0:T(8,128)S(1)} collective-permute-done((f32[144,128]{1,0:T(8,128)S(1)}, f32[144,128]{1,0:T(8,128)S(1)}, u32[]{:S(2)}, u32[]{:S(2)}) %collective-permute-start.5) | collective-permute-done | bytes 73760 | tf_op jit(solution)/shard_map/ppermute | solution.py:702
  30.9 0.7 collective-permute-start.7
  31.6 1.4 %collective-permute-start.8 = (f32[128,128]{1,0:T(8,128)S(1)}, f32[128,128]{1,0:T(8,128)S(1)}, u32[]{:S(2)}, u32[]{:S(2)}) collective-permute-start(f32[128,128]{1,0:T(8,128)S(1)} %get-tuple-element.79), channel_id=1, source_target_pairs={{2,0},{3,1},{0,2},{1,3},{6,4},{7,5},{4,6},{5,7},{10,8},{11,9},{8,1... | collective-permute-start | bytes 196616 | tf_op jit(solution)/shard_map/ppermute | solution.py:702
  33.1 1.4 %collective-permute-start.9 = (f32[128,128]{1,0:T(8,128)S(1)}, f32[128,128]{1,0:T(8,128)S(1)}, u32[]{:S(2)}, u32[]{:S(2)}) collective-permute-start(f32[128,128]{1,0:T(8,128)S(1)} %get-tuple-element.80), channel_id=1, source_target_pairs={{3,0},{2,1},{1,2},{0,3},{7,4},{6,5},{5,6},{4,7},{11,8},{10,9},{9,1... | collective-permute-start | bytes 196616 | tf_op jit(solution)/shard_map/ppermute | solution.py:702
  34.5 0.8 collective-permute-done.7
  35.3 0.8 collective-permute-done.8
  36.0 2.2 %collective-permute-done.9 = f32[128,128]{1,0:T(8,128)S(1)} collective-permute-done((f32[128,128]{1,0:T(8,128)S(1)}, f32[128,128]{1,0:T(8,128)S(1)}, u32[]{:S(2)}, u32[]{:S(2)}) %collective-permute-start.9) | collective-permute-done | bytes 65568 | tf_op jit(solution)/shard_map/ppermute | solution.py:702
  38.2 0.1 collective-permute-start.13
  38.3 0.9 %collective-permute-start.12 = (f32[32,128]{1,0:T(8,128)S(1)}, f32[32,128]{1,0:T(8,128)S(1)}, u32[]{:S(2)}, u32[]{:S(2)}) collective-permute-start(f32[32,128]{1,0:T(8,128)S(1)} %fusion.1), channel_id=1, source_target_pairs={{8,0},{28,4},{16,8},{4,12},{24,16},{12,20},{0,24},{20,28},{9,1},{2... | collective-permute-start | bytes 49160 | tf_op jit(solution)/shard_map/ppermute | solution.py:702
  39.2 0.1 collective-permute-start.11
  39.3 1.5 %collective-permute-start.10 = (f32[176,128]{1,0:T(8,128)S(1)}, f32[176,128]{1,0:T(8,128)S(1)}, u32[]{:S(2)}, u32[]{:S(2)}) collective-permute-start(f32[176,128]{1,0:T(8,128)S(1)} %pad_maximum_fusion.3.own), channel_id=1, source_target_pairs={{4,0},{0,4},{12,8},{8,12},{20,16},{16,20},{28,24},{24,28},{5,1},{1... | collective-permute-start | bytes 270344 | tf_op jit(solution)/shard_map/ppermute | solution.py:702
  40.8 0.1 pad_add_fusion.1.order
  40.9 2.1 %collective-permute-done.13.rest_1_ = f32[32,128]{1,0:T(8,128)S(1)} collective-permute-done((f32[32,128]{1,0:T(8,128)S(1)}, f32[32,128]{1,0:T(8,128)S(1)}, u32[]{:S(2)}, u32[]{:S(2)}) %collective-permute-start.13) | collective-permute-done | bytes 16416 | tf_op jit(solution)/shard_map/ppermute | solution.py:702
  43.0 2.8 %collective-permute-done.11.other = f32[176,128]{1,0:T(8,128)S(1)} collective-permute-done((f32[176,128]{1,0:T(8,128)S(1)}, f32[176,128]{1,0:T(8,128)S(1)}, u32[]{:S(2)}, u32[]{:S(2)}) %collective-permute-start.11) | collective-permute-done | bytes 90144 | tf_op jit(solution)/shard_map/ppermute | solution.py:702
  45.8 0.0 collective-permute-done.10.mate
  45.8 6.2 %shard_map.126 = (f32[144,128]{1,0:T(8,128)S(1)}, f32[144,128]{1,0:T(8,128)S(1)}, f32[144,128]{1,0:T(8,128)S(1)}, f32[64,128]{1,0:T(8,128)S(1)}, f32[48,128]{1,0...) custom-call(s32[4]{0:T(128)S(1)} %pad_add_fusion.1.order, f32[176,128]{1,0:T(8,128)S(1)} %pad_maximum_fusion.3.own, ...), custom_call_target="tpu_custom_call" | custom-call | flops 1073741824 | bytes 65536 | tf_op jit(solution)/shard_map/pallas_call | solution.py:708
  52.0 0.1 collective-permute-start.14
  52.1 1.1 %collective-permute-start.15 = (f32[144,128]{1,0:T(8,128)S(1)}, f32[144,128]{1,0:T(8,128)S(1)}, u32[]{:S(2)}, u32[]{:S(2)}) collective-permute-start(f32[144,128]{1,0:T(8,128)S(1)} %get-tuple-element.63), channel_id=1, source_target_pairs={{28,0},{8,4},{4,8},{16,12},{12,16},{24,20},{20,24},{0,28},{29,1},{... | collective-permute-start | bytes 221192 | tf_op jit(solution)/shard_map/ppermute | solution.py:702
  53.2 0.3 shard_map.127
  53.5 4.3 %collective-permute-done.15 = f32[144,128]{1,0:T(8,128)S(1)} collective-permute-done((f32[144,128]{1,0:T(8,128)S(1)}, f32[144,128]{1,0:T(8,128)S(1)}, u32[]{:S(2)}, u32[]{:S(2)}) %collective-permute-start.15) | collective-permute-done | bytes 73760 | tf_op jit(solution)/shard_map/ppermute | solution.py:702
  57.8 1.2 %collective-permute-start.18 = (f32[160,128]{1,0:T(8,128)S(1)}, f32[160,128]{1,0:T(8,128)S(1)}, u32[]{:S(2)}, u32[]{:S(2)}) collective-permute-start(f32[160,128]{1,0:T(8,128)S(1)} %pad_maximum_fusion.4.own), channel_id=1, source_target_pairs={{2,0},{3,1},{0,2},{1,3},{6,4},{7,5},{4,6},{5,7},{10,8},{11,9},{8,1... | collective-permute-start | bytes 245768 | tf_op jit(solution)/shard_map/ppermute | solution.py:702
  58.9 1.9 %collective-permute-start.17 = (f32[160,128]{1,0:T(8,128)S(1)}, f32[160,128]{1,0:T(8,128)S(1)}, u32[]{:S(2)}, u32[]{:S(2)}) collective-permute-start(f32[160,128]{1,0:T(8,128)S(1)} %pad_maximum_fusion.4.own), channel_id=1, source_target_pairs={{3,0},{2,1},{1,2},{0,3},{7,4},{6,5},{5,6},{4,7},{11,8},{10,9},{9,1... | collective-permute-start | bytes 245768 | tf_op jit(solution)/shard_map/ppermute | solution.py:702
  60.8 0.5 collective-permute-start.16
  61.3 0.1 pad_add_fusion.order
  61.4 1.1 %collective-permute-done.18.far = f32[160,128]{1,0:T(8,128)S(1)} collective-permute-done((f32[160,128]{1,0:T(8,128)S(1)}, f32[160,128]{1,0:T(8,128)S(1)}, u32[]{:S(2)}, u32[]{:S(2)}) %collective-permute-start.18) | collective-permute-done | bytes 81952 | tf_op jit(solution)/shard_map/ppermute | solution.py:702
  62.5 1.7 %collective-permute-done.17.other = f32[160,128]{1,0:T(8,128)S(1)} collective-permute-done((f32[160,128]{1,0:T(8,128)S(1)}, f32[160,128]{1,0:T(8,128)S(1)}, u32[]{:S(2)}, u32[]{:S(2)}) %collective-permute-start.17) | collective-permute-done | bytes 81952 | tf_op jit(solution)/shard_map/ppermute | solution.py:702
  64.3 1.0 %collective-permute-done.16.mate = f32[160,128]{1,0:T(8,128)S(1)} collective-permute-done((f32[160,128]{1,0:T(8,128)S(1)}, f32[160,128]{1,0:T(8,128)S(1)}, u32[]{:S(2)}, u32[]{:S(2)}) %collective-permute-start.16) | collective-permute-done | bytes 81952 | tf_op jit(solution)/shard_map/ppermute | solution.py:702
  65.2 0.9 %shard_map.128 = (f32[8,16,128]{2,1,0:T(8,128)S(1)}, f32[48,128]{1,0:T(8,128)S(1)}) custom-call(s32[4]{0:T(128)S(1)} %pad_add_fusion.order, f32[160,128]{1,0:T(8,128)S(1)} %pad_maximum_fusion.4.own, f32[160,128]{1,0:T(8,128)S(1)} %collective-permute-done.16.mate, f32[160,128]{1,0:T(8,128)S(1)} %collective-permute-done.17.other, ...), custom_call_target="tpu_custom_call" | custom-call | flops 1048576 | bytes 65536 | tf_op jit(solution)/shard_map/pallas_call | solution.py:708
  66.2 8.3 %all_to_all.5.got = f32[8,16,128]{2,1,0:T(8,128)S(1)} all-to-all(f32[8,16,128]{2,1,0:T(8,128)S(1)} %get-tuple-element.66), channel_id=1, replica_groups=mesh['gx'=8,'gy'=4] {'gx'}, dimensions={0} | all-to-all | bytes 131072 | tf_op jit(solution)/shard_map/all_to_all | solution.py:924
  74.5 3.5 %shard_map.129 = (f32[2,3,32,64]{3,2,1,0:T(8,128)}, f32[2,32,32]{2,1,0:T(8,128)}) custom-call(f32[8,16,128]{2,1,0:T(8,128)S(1)} %all_to_all.5.got, f32[64,128]{1,0:T(8,128)S(1)} %get-tuple-element.67.sums, f32[48,128]{1,0:T(8,128)S(1)} %get-tuple-element.68.rown, f32[48,128]{1,0:T(8,128)S(1)} %get-tuple-element.69.yown, ...), custom_call_target="tpu_custom_call" | custom-call | flops 1048576 | bytes 65536 | tf_op jit(solution)/shard_map/pallas_call | solution.py:708
  (14 shorter events, 0.1 us)
Async XLA Ops:
  1.6 6.5 %collective-permute-start.1 = (f32[104,128]{1,0:T(8,128)S(1)}, f32[104,128]{1,0:T(8,128)S(1)}, u32[]{:S(2)}, u32[]{:S(2)}) collective-permute-start(f32[104,128]{1,0:T(8,128)S(1)} %convert_add_fusion.1.table.cown), channel_id=1, source_target_pairs={{28,0},{8,4},{4,8},{16,12},{12,16},{24,20},{20,24},{0,28},{29,1},{... | collective-permute-start | bytes 159752 | tf_op jit(solution)/shard_map/ppermute | solution.py:702
  6.1 1.9 %collective-permute-start = (f32[104,128]{1,0:T(8,128)S(1)}, f32[104,128]{1,0:T(8,128)S(1)}, u32[]{:S(2)}, u32[]{:S(2)}) collective-permute-start(f32[104,128]{1,0:T(8,128)S(1)} %convert_add_fusion.1.table.cown), channel_id=1, source_target_pairs={{4,0},{0,4},{12,8},{8,12},{20,16},{16,20},{28,24},{24,28},{5,1},{1... | collective-permute-start | bytes 159752 | tf_op jit(solution)/shard_map/ppermute | solution.py:702
  9.2 5.4 %collective-permute-start.2 = (f32[104,128]{1,0:T(8,128)S(1)}, f32[104,128]{1,0:T(8,128)S(1)}, u32[]{:S(2)}, u32[]{:S(2)}) collective-permute-start(f32[104,128]{1,0:T(8,128)S(1)} %get-tuple-element.38), channel_id=1, source_target_pairs={{1,0},{0,1},{3,2},{2,3},{5,4},{4,5},{7,6},{6,7},{9,8},{8,9},{11,10... | collective-permute-start | bytes 159752 | tf_op jit(solution)/shard_map/ppermute | solution.py:702
  11.5 5.0 %collective-permute-start.3 = (f32[104,128]{1,0:T(8,128)S(1)}, f32[104,128]{1,0:T(8,128)S(1)}, u32[]{:S(2)}, u32[]{:S(2)}) collective-permute-start(f32[104,128]{1,0:T(8,128)S(1)} %get-tuple-element.39), channel_id=1, source_target_pairs={{3,0},{2,1},{1,2},{0,3},{7,4},{6,5},{5,6},{4,7},{11,8},{10,9},{9,1... | collective-permute-start | bytes 159752 | tf_op jit(solution)/shard_map/ppermute | solution.py:702
  25.1 3.7 %collective-permute-start.4 = (f32[144,128]{1,0:T(8,128)S(1)}, f32[144,128]{1,0:T(8,128)S(1)}, u32[]{:S(2)}, u32[]{:S(2)}) collective-permute-start(f32[144,128]{1,0:T(8,128)S(1)} %get-tuple-element.50), channel_id=1, source_target_pairs={{4,0},{0,4},{12,8},{8,12},{20,16},{16,20},{28,24},{24,28},{5,1},{1... | collective-permute-start | bytes 221192 | tf_op jit(solution)/shard_map/ppermute | solution.py:702
  25.2 5.6 %collective-permute-start.5 = (f32[144,128]{1,0:T(8,128)S(1)}, f32[144,128]{1,0:T(8,128)S(1)}, u32[]{:S(2)}, u32[]{:S(2)}) collective-permute-start(f32[144,128]{1,0:T(8,128)S(1)} %get-tuple-element.51), channel_id=1, source_target_pairs={{28,0},{8,4},{4,8},{16,12},{12,16},{24,20},{20,24},{0,28},{29,1},{... | collective-permute-start | bytes 221192 | tf_op jit(solution)/shard_map/ppermute | solution.py:702
  27.6 1.2 %collective-permute-start.6 = (f32[32,128]{1,0:T(8,128)S(1)}, f32[32,128]{1,0:T(8,128)S(1)}, u32[]{:S(2)}, u32[]{:S(2)}) collective-permute-start(f32[32,128]{1,0:T(8,128)S(1)} %shard_map.125), channel_id=1, source_target_pairs={{4,0},{0,4},{12,8},{8,12},{20,16},{16,20},{28,24},{24,28},{5,1},{1... | collective-permute-start | bytes 49160 | tf_op jit(solution)/shard_map/ppermute | solution.py:702
  30.9 4.3 %collective-permute-start.7 = (f32[128,128]{1,0:T(8,128)S(1)}, f32[128,128]{1,0:T(8,128)S(1)}, u32[]{:S(2)}, u32[]{:S(2)}) collective-permute-start(f32[128,128]{1,0:T(8,128)S(1)} %get-tuple-element.78), channel_id=1, source_target_pairs={{1,0},{0,1},{3,2},{2,3},{5,4},{4,5},{7,6},{6,7},{9,8},{8,9},{11,10... | collective-permute-start | bytes 196616 | tf_op jit(solution)/shard_map/ppermute | solution.py:702
  31.6 4.4 %collective-permute-start.8 = (f32[128,128]{1,0:T(8,128)S(1)}, f32[128,128]{1,0:T(8,128)S(1)}, u32[]{:S(2)}, u32[]{:S(2)}) collective-permute-start(f32[128,128]{1,0:T(8,128)S(1)} %get-tuple-element.79), channel_id=1, source_target_pairs={{2,0},{3,1},{0,2},{1,3},{6,4},{7,5},{4,6},{5,7},{10,8},{11,9},{8,1... | collective-permute-start | bytes 196616 | tf_op jit(solution)/shard_map/ppermute | solution.py:702
  33.1 5.2 %collective-permute-start.9 = (f32[128,128]{1,0:T(8,128)S(1)}, f32[128,128]{1,0:T(8,128)S(1)}, u32[]{:S(2)}, u32[]{:S(2)}) collective-permute-start(f32[128,128]{1,0:T(8,128)S(1)} %get-tuple-element.80), channel_id=1, source_target_pairs={{3,0},{2,1},{1,2},{0,3},{7,4},{6,5},{5,6},{4,7},{11,8},{10,9},{9,1... | collective-permute-start | bytes 196616 | tf_op jit(solution)/shard_map/ppermute | solution.py:702
  38.2 4.8 %collective-permute-start.13 = (f32[32,128]{1,0:T(8,128)S(1)}, f32[32,128]{1,0:T(8,128)S(1)}, u32[]{:S(2)}, u32[]{:S(2)}) collective-permute-start(f32[32,128]{1,0:T(8,128)S(1)} %fusion.1), channel_id=1, source_target_pairs={{16,0},{20,4},{24,8},{28,12},{0,16},{4,20},{8,24},{12,28},{17,1},{... | collective-permute-start | bytes 49160 | tf_op jit(solution)/shard_map/ppermute | solution.py:702
  38.3 4.7 %collective-permute-start.12 = (f32[32,128]{1,0:T(8,128)S(1)}, f32[32,128]{1,0:T(8,128)S(1)}, u32[]{:S(2)}, u32[]{:S(2)}) collective-permute-start(f32[32,128]{1,0:T(8,128)S(1)} %fusion.1), channel_id=1, source_target_pairs={{8,0},{28,4},{16,8},{4,12},{24,16},{12,20},{0,24},{20,28},{9,1},{2... | collective-permute-start | bytes 49160 | tf_op jit(solution)/shard_map/ppermute | solution.py:702
  39.2 6.6 %collective-permute-start.11 = (f32[176,128]{1,0:T(8,128)S(1)}, f32[176,128]{1,0:T(8,128)S(1)}, u32[]{:S(2)}, u32[]{:S(2)}) collective-permute-start(f32[176,128]{1,0:T(8,128)S(1)} %pad_maximum_fusion.3.own), channel_id=1, source_target_pairs={{28,0},{8,4},{4,8},{16,12},{12,16},{24,20},{20,24},{0,28},{29,1},{... | collective-permute-start | bytes 270344 | tf_op jit(solution)/shard_map/ppermute | solution.py:702
  39.3 6.5 %collective-permute-start.10 = (f32[176,128]{1,0:T(8,128)S(1)}, f32[176,128]{1,0:T(8,128)S(1)}, u32[]{:S(2)}, u32[]{:S(2)}) collective-permute-start(f32[176,128]{1,0:T(8,128)S(1)} %pad_maximum_fusion.3.own), channel_id=1, source_target_pairs={{4,0},{0,4},{12,8},{8,12},{20,16},{16,20},{28,24},{24,28},{5,1},{1... | collective-permute-start | bytes 270344 | tf_op jit(solution)/shard_map/ppermute | solution.py:702
  52.0 1.4 %collective-permute-start.14 = (f32[144,128]{1,0:T(8,128)S(1)}, f32[144,128]{1,0:T(8,128)S(1)}, u32[]{:S(2)}, u32[]{:S(2)}) collective-permute-start(f32[144,128]{1,0:T(8,128)S(1)} %get-tuple-element.62), channel_id=1, source_target_pairs={{4,0},{0,4},{12,8},{8,12},{20,16},{16,20},{28,24},{24,28},{5,1},{1... | collective-permute-start | bytes 221192 | tf_op jit(solution)/shard_map/ppermute | solution.py:702
  52.1 5.6 %collective-permute-start.15 = (f32[144,128]{1,0:T(8,128)S(1)}, f32[144,128]{1,0:T(8,128)S(1)}, u32[]{:S(2)}, u32[]{:S(2)}) collective-permute-start(f32[144,128]{1,0:T(8,128)S(1)} %get-tuple-element.63), channel_id=1, source_target_pairs={{28,0},{8,4},{4,8},{16,12},{12,16},{24,20},{20,24},{0,28},{29,1},{... | collective-permute-start | bytes 221192 | tf_op jit(solution)/shard_map/ppermute | solution.py:702
  57.8 4.8 %collective-permute-start.18 = (f32[160,128]{1,0:T(8,128)S(1)}, f32[160,128]{1,0:T(8,128)S(1)}, u32[]{:S(2)}, u32[]{:S(2)}) collective-permute-start(f32[160,128]{1,0:T(8,128)S(1)} %pad_maximum_fusion.4.own), channel_id=1, source_target_pairs={{2,0},{3,1},{0,2},{1,3},{6,4},{7,5},{4,6},{5,7},{10,8},{11,9},{8,1... | collective-permute-start | bytes 245768 | tf_op jit(solution)/shard_map/ppermute | solution.py:702
  58.9 5.3 %collective-permute-start.17 = (f32[160,128]{1,0:T(8,128)S(1)}, f32[160,128]{1,0:T(8,128)S(1)}, u32[]{:S(2)}, u32[]{:S(2)}) collective-permute-start(f32[160,128]{1,0:T(8,128)S(1)} %pad_maximum_fusion.4.own), channel_id=1, source_target_pairs={{3,0},{2,1},{1,2},{0,3},{7,4},{6,5},{5,6},{4,7},{11,8},{10,9},{9,1... | collective-permute-start | bytes 245768 | tf_op jit(solution)/shard_map/ppermute | solution.py:702
  60.8 4.4 %collective-permute-start.16 = (f32[160,128]{1,0:T(8,128)S(1)}, f32[160,128]{1,0:T(8,128)S(1)}, u32[]{:S(2)}, u32[]{:S(2)}) collective-permute-start(f32[160,128]{1,0:T(8,128)S(1)} %pad_maximum_fusion.4.own), channel_id=1, source_target_pairs={{1,0},{0,1},{3,2},{2,3},{5,4},{4,5},{7,6},{6,7},{9,8},{8,9},{11,10... | collective-permute-start | bytes 245768 | tf_op jit(solution)/shard_map/ppermute | solution.py:702

commit v6 on v5

--- a/solution.py
+++ b/solution.py
@@ -70,9 +70,18 @@
 def select(rows, *names):
     picks = jnp.concatenate(names, axis=1)
     hits = lax.broadcasted_iota(jnp.int32, (rows.shape[1], picks.shape[1]), 0) == picks
-    got = dot16(split(rows, 3), hits.astype(jnp.float32).astype(jnp.bfloat16))
-    count = rows.shape[0]
-    return got[:count] + (got[count : 2 * count] + got[2 * count :])
+    tail = 16
+    count = rows.shape[0] - tail
+    parts = jnp.concatenate([split(rows[:count], 2), split(rows[count:], 3)], axis=0)
+    got = dot16(parts, hits.astype(jnp.float32).astype(jnp.bfloat16))
+    last = got[2 * count :]
+    return jnp.concatenate(
+        [
+            got[:count] + got[count : 2 * count],
+            last[:tail] + (last[tail : 2 * tail] + last[2 * tail :]),
+        ],
+        axis=0,
+    )
 
 
 def rows_and_cols(size):
@@ -414,7 +423,7 @@
     bd[...] = bend
     low_row = lax.broadcasted_iota(jnp.int32, (basis, lanes), 1) < atoms
     for k in range(basis):
-        both[k] = 2.0 * dot32(vec * vec[k : k + 1, :], u)
+        both[k] = 2.0 * dot_split(vec * vec[k : k + 1, :], u)
 
     def block(i, column):
         accs = None
@@ -490,15 +499,15 @@
 
     rad, vec, mix = w_rad[...], w_vec[...], w_mix[...]
     radt, vect, mixt, outt = rad_t[...], vec_t[...], mix_t[...], out_t[:, 0:1]
-    flow = [dot32(vect, descr[c + 1]) for c in range(3)]
-    mixed = dot32(radt, descr[0]) + flow[0] * flow[0] + flow[1] * flow[1] + flow[2] * flow[2]
+    flow = [dot_split(vect, descr[c + 1]) for c in range(3)]
+    mixed = dot_split(radt, descr[0]) + flow[0] * flow[0] + flow[1] * flow[1] + flow[2] * flow[2]
     hidden = dot_split(mixt, mixed)
     gate = 1.0 / (1.0 + jnp.exp(-hidden))
     slope = gate * (1.0 + hidden * (1.0 - gate)) * outt
     bend = gate * (1.0 - gate) * (2.0 + hidden * (1.0 - 2.0 * gate)) * outt
     u = dot_split(mix, slope)
-    alpha = dot32(rad, u)
-    beta = [2.0 * dot32(vec, flow[c] * u) for c in range(3)]
+    alpha = dot_split(rad, u)
+    beta = [2.0 * dot_split(vec, flow[c] * u) for c in range(3)]
     edge_rows(alpha, beta, ef, ee, f2s, hs, e8, lanes)
     channel_lift(flow, radt, vect, mixt, qs, qr, lanes, atoms)
     descriptor_curvature(vec, u, bend, qs, qr, bd, both, pmat, rmat, lanes, atoms)

time: 78.3 us -> 77.9 us (level)
  no operation moved by 1% of the time
where the time goes in v6:
time: 77.9 us; the launch traced here: 77.7 us
  waiting for transfers between devices  23.7 us (30%)
  Pallas kernels  21.6 us (28%)
  starting transfers between devices  21.1 us (27%)
  blocking collectives  8.28 us (11%)
  other arithmetic  2.2 us (3%)
  between operations  0.79 us (1%)
    ppermute x19, waiting for transfers between devices, fetch(): return lax.ppermute(values, axis, [(s, i) for i, s in enumerate(sources)])  23.7 us
    pallas_call x8, Pallas kernels, call(): pl.pallas_call(kernel, out_shape=outs, in_specs=[pl.BlockSpec(memory_spac...  21.6 us
    ppermute x19, starting transfers between devices, fetch(): return lax.ppermute(values, axis, [(s, i) for i, s in enumerate(sources)])  21.1 us
    all_to_all x1, blocking collectives, shards(): got = lax.all_to_all(spread_sums, 'gx', 0, 0)  8.28 us
    add x2, other arithmetic, laid(): total = placed if total is None else total + placed  1.88 us
  transfers between devices with their start and end apart: 19, of which 13 were waited for; matrix products, arithmetic and copies ran while one was open for 2% of the time, Pallas kernels for 2%

profile of v6, /device:TPU:0, one launch (start us, length us, event | category | flops | bytes accessed | tf_op | source)
XLA Modules:
  0.0 77.7 jit_solution(7985851314963900516)
XLA Ops:
  0.6 1.0 %convert_add_fusion.1.table.cown = f32[104,128]{1,0:T(8,128)S(1)} fusion(s32[2,64]{1,0:T(2,128)} %bitcast.23, s32[2,64]{1,0:T(2,128)} %bitcast.24, f32[3,64]{1,0:T(4,128)} %param.11, f32[96,64]{1,0:T(8,128)} %bitcast.21, f32[96,64]{1,0:T(8,128)} %bitcast.22), kind=kLoop, calls=%fused_computation.8 | loop fusion | flops 79872 | bytes 104192 | tf_op jit(solution)/shard_map/add | solution.py:736
  1.6 4.6 %collective-permute-start.1 = (f32[104,128]{1,0:T(8,128)S(1)}, f32[104,128]{1,0:T(8,128)S(1)}, u32[]{:S(2)}, u32[]{:S(2)}) collective-permute-start(f32[104,128]{1,0:T(8,128)S(1)} %convert_add_fusion.1.table.cown), channel_id=1, source_target_pairs={{28,0},{8,4},{4,8},{16,12},{12,16},{24,20},{20,24},{0,28},{29,1},{... | collective-permute-start | bytes 159752 | tf_op jit(solution)/shard_map/ppermute | solution.py:711
  6.1 0.0 collective-permute-start
  6.1 0.1 pad_add_fusion.2.sides
  6.2 1.8 %collective-permute-done.1.from_other = f32[104,128]{1,0:T(8,128)S(1)} collective-permute-done((f32[104,128]{1,0:T(8,128)S(1)}, f32[104,128]{1,0:T(8,128)S(1)}, u32[]{:S(2)}, u32[]{:S(2)}) %collective-permute-start.1) | collective-permute-done | bytes 53280 | tf_op jit(solution)/shard_map/ppermute | solution.py:711
  8.1 1.1 %shard_map.122 = (f32[104,128]{1,0:T(8,128)S(1)}, f32[104,128]{1,0:T(8,128)S(1)}, f32[200,192]{1,0:T(8,128)S(1)}) custom-call(s32[2]{0:T(128)S(1)} %pad_add_fusion.2.sides, f32[104,128]{1,0:T(8,128)S(1)} %convert_add_fusion.1.table.cown, f32[104,128]{1,0:T(8,128)S(1)} %collective-permute-done.from_mate, f32[104,128]{1,0:T(8,128)S(1)} %collective-permute-done.1.from_other), custom_call_target="tpu_custom_call" | custom-call | flops 1048576 | bytes 65536 | tf_op jit(solution)/shard_map/pallas_call | solution.py:717
  9.2 2.2 %collective-permute-start.2 = (f32[104,128]{1,0:T(8,128)S(1)}, f32[104,128]{1,0:T(8,128)S(1)}, u32[]{:S(2)}, u32[]{:S(2)}) collective-permute-start(f32[104,128]{1,0:T(8,128)S(1)} %get-tuple-element.38), channel_id=1, source_target_pairs={{1,0},{0,1},{3,2},{2,3},{5,4},{4,5},{7,6},{6,7},{9,8},{8,9},{11,10... | collective-permute-start | bytes 159752 | tf_op jit(solution)/shard_map/ppermute | solution.py:711
  11.4 1.5 %collective-permute-start.3 = (f32[104,128]{1,0:T(8,128)S(1)}, f32[104,128]{1,0:T(8,128)S(1)}, u32[]{:S(2)}, u32[]{:S(2)}) collective-permute-start(f32[104,128]{1,0:T(8,128)S(1)} %get-tuple-element.39), channel_id=1, source_target_pairs={{3,0},{2,1},{1,2},{0,3},{7,4},{6,5},{5,6},{4,7},{11,8},{10,9},{9,1... | collective-permute-start | bytes 159752 | tf_op jit(solution)/shard_map/ppermute | solution.py:711
  12.9 0.9 %convert_add_fusion.table = f32[192,128]{1,0:T(8,128)S(1)} fusion(s32[1,64]{1,0:T(1,128)} %bitcast.25, s32[32,64]{1,0:T(8,128)} %param.14, f32[1,128]{1,0:T(1,128)} %bitcast.26, f32[8,128]{1,0:T(8,128)} %param.19, f32[8,128]{1,0:T(8,128)} %param.18, f32[128,128]{1,0:T(8,128)} %param.20), kind=kLoop, calls=%fused_computation.3 | loop fusion | flops 172032 | bytes 180992 | tf_op jit(solution)/shard_map/add | solution.py:736
  13.8 0.7 shard_map.123
  14.6 0.0 collective-permute-done.2.from_mate
  14.6 1.8 %collective-permute-done.3.from_other = f32[104,128]{1,0:T(8,128)S(1)} collective-permute-done((f32[104,128]{1,0:T(8,128)S(1)}, f32[104,128]{1,0:T(8,128)S(1)}, u32[]{:S(2)}, u32[]{:S(2)}) %collective-permute-start.3) | collective-permute-done | bytes 53280 | tf_op jit(solution)/shard_map/ppermute | solution.py:711
  16.4 8.4 %shard_map.124 = (f32[144,128]{1,0:T(8,128)S(1)}, f32[144,128]{1,0:T(8,128)S(1)}, f32[144,128]{1,0:T(8,128)S(1)}, f32[96,320]{1,0:T(8,128)S(1)}, f32[96,320]{1,0...) custom-call(s32[2]{0:T(128)S(1)} %pad_add_fusion.2.sides, ...), custom_call_target="tpu_custom_call" | custom-call | flops 2147483648 | bytes 65536 | tf_op jit(solution)/shard_map/pallas_call | solution.py:717
  24.8 0.1 collective-permute-start.4
  24.9 1.9 %collective-permute-start.5 = (f32[144,128]{1,0:T(8,128)S(1)}, f32[144,128]{1,0:T(8,128)S(1)}, u32[]{:S(2)}, u32[]{:S(2)}) collective-permute-start(f32[144,128]{1,0:T(8,128)S(1)} %get-tuple-element.51), channel_id=1, source_target_pairs={{28,0},{8,4},{4,8},{16,12},{12,16},{24,20},{20,24},{0,28},{29,1},{... | collective-permute-start | bytes 221192 | tf_op jit(solution)/shard_map/ppermute | solution.py:711
  26.8 0.5 shard_map.125
  27.3 0.1 collective-permute-start.6
  27.3 1.2 %collective-permute-done.6 = f32[32,128]{1,0:T(8,128)S(1)} collective-permute-done((f32[32,128]{1,0:T(8,128)S(1)}, f32[32,128]{1,0:T(8,128)S(1)}, u32[]{:S(2)}, u32[]{:S(2)}) %collective-permute-start.6) | collective-permute-done | bytes 16416 | tf_op jit(solution)/shard_map/ppermute | solution.py:711
  28.5 2.1 %collective-permute-done.5 = f32[144,128]{1,0:T(8,128)S(1)} collective-permute-done((f32[144,128]{1,0:T(8,128)S(1)}, f32[144,128]{1,0:T(8,128)S(1)}, u32[]{:S(2)}, u32[]{:S(2)}) %collective-permute-start.5) | collective-permute-done | bytes 73760 | tf_op jit(solution)/shard_map/ppermute | solution.py:711
  30.6 0.7 collective-permute-start.7
  31.3 1.4 %collective-permute-start.8 = (f32[128,128]{1,0:T(8,128)S(1)}, f32[128,128]{1,0:T(8,128)S(1)}, u32[]{:S(2)}, u32[]{:S(2)}) collective-permute-start(f32[128,128]{1,0:T(8,128)S(1)} %get-tuple-element.79), channel_id=1, source_target_pairs={{2,0},{3,1},{0,2},{1,3},{6,4},{7,5},{4,6},{5,7},{10,8},{11,9},{8,1... | collective-permute-start | bytes 196616 | tf_op jit(solution)/shard_map/ppermute | solution.py:711
  32.7 1.4 %collective-permute-start.9 = (f32[128,128]{1,0:T(8,128)S(1)}, f32[128,128]{1,0:T(8,128)S(1)}, u32[]{:S(2)}, u32[]{:S(2)}) collective-permute-start(f32[128,128]{1,0:T(8,128)S(1)} %get-tuple-element.80), channel_id=1, source_target_pairs={{3,0},{2,1},{1,2},{0,3},{7,4},{6,5},{5,6},{4,7},{11,8},{10,9},{9,1... | collective-permute-start | bytes 196616 | tf_op jit(solution)/shard_map/ppermute | solution.py:711
  34.2 0.8 collective-permute-done.7
  35.0 0.8 collective-permute-done.8
  35.7 2.2 %collective-permute-done.9 = f32[128,128]{1,0:T(8,128)S(1)} collective-permute-done((f32[128,128]{1,0:T(8,128)S(1)}, f32[128,128]{1,0:T(8,128)S(1)}, u32[]{:S(2)}, u32[]{:S(2)}) %collective-permute-start.9) | collective-permute-done | bytes 65568 | tf_op jit(solution)/shard_map/ppermute | solution.py:711
  37.9 0.1 collective-permute-start.13
  38.0 0.9 %collective-permute-start.12 = (f32[32,128]{1,0:T(8,128)S(1)}, f32[32,128]{1,0:T(8,128)S(1)}, u32[]{:S(2)}, u32[]{:S(2)}) collective-permute-start(f32[32,128]{1,0:T(8,128)S(1)} %fusion.1), channel_id=1, source_target_pairs={{8,0},{28,4},{16,8},{4,12},{24,16},{12,20},{0,24},{20,28},{9,1},{2... | collective-permute-start | bytes 49160 | tf_op jit(solution)/shard_map/ppermute | solution.py:711
  38.9 0.1 collective-permute-start.11
  39.0 1.5 %collective-permute-start.10 = (f32[176,128]{1,0:T(8,128)S(1)}, f32[176,128]{1,0:T(8,128)S(1)}, u32[]{:S(2)}, u32[]{:S(2)}) collective-permute-start(f32[176,128]{1,0:T(8,128)S(1)} %pad_maximum_fusion.3.own), channel_id=1, source_target_pairs={{4,0},{0,4},{12,8},{8,12},{20,16},{16,20},{28,24},{24,28},{5,1},{1... | collective-permute-start | bytes 270344 | tf_op jit(solution)/shard_map/ppermute | solution.py:711
  40.5 0.1 pad_add_fusion.1.order
  40.6 2.1 %collective-permute-done.13.rest_1_ = f32[32,128]{1,0:T(8,128)S(1)} collective-permute-done((f32[32,128]{1,0:T(8,128)S(1)}, f32[32,128]{1,0:T(8,128)S(1)}, u32[]{:S(2)}, u32[]{:S(2)}) %collective-permute-start.13) | collective-permute-done | bytes 16416 | tf_op jit(solution)/shard_map/ppermute | solution.py:711
  42.7 2.8 %collective-permute-done.11.other = f32[176,128]{1,0:T(8,128)S(1)} collective-permute-done((f32[176,128]{1,0:T(8,128)S(1)}, f32[176,128]{1,0:T(8,128)S(1)}, u32[]{:S(2)}, u32[]{:S(2)}) %collective-permute-start.11) | collective-permute-done | bytes 90144 | tf_op jit(solution)/shard_map/ppermute | solution.py:711
  45.5 0.0 collective-permute-done.10.mate
  45.5 6.2 %shard_map.126 = (f32[144,128]{1,0:T(8,128)S(1)}, f32[144,128]{1,0:T(8,128)S(1)}, f32[144,128]{1,0:T(8,128)S(1)}, f32[64,128]{1,0:T(8,128)S(1)}, f32[48,128]{1,0...) custom-call(s32[4]{0:T(128)S(1)} %pad_add_fusion.1.order, f32[176,128]{1,0:T(8,128)S(1)} %pad_maximum_fusion.3.own, ...), custom_call_target="tpu_custom_call" | custom-call | flops 1073741824 | bytes 65536 | tf_op jit(solution)/shard_map/pallas_call | solution.py:717
  51.7 0.1 collective-permute-start.14
  51.8 1.1 %collective-permute-start.15 = (f32[144,128]{1,0:T(8,128)S(1)}, f32[144,128]{1,0:T(8,128)S(1)}, u32[]{:S(2)}, u32[]{:S(2)}) collective-permute-start(f32[144,128]{1,0:T(8,128)S(1)} %get-tuple-element.63), channel_id=1, source_target_pairs={{28,0},{8,4},{4,8},{16,12},{12,16},{24,20},{20,24},{0,28},{29,1},{... | collective-permute-start | bytes 221192 | tf_op jit(solution)/shard_map/ppermute | solution.py:711
  52.8 0.3 shard_map.127
  53.1 4.3 %collective-permute-done.15 = f32[144,128]{1,0:T(8,128)S(1)} collective-permute-done((f32[144,128]{1,0:T(8,128)S(1)}, f32[144,128]{1,0:T(8,128)S(1)}, u32[]{:S(2)}, u32[]{:S(2)}) %collective-permute-start.15) | collective-permute-done | bytes 73760 | tf_op jit(solution)/shard_map/ppermute | solution.py:711
  57.5 1.2 %collective-permute-start.18 = (f32[160,128]{1,0:T(8,128)S(1)}, f32[160,128]{1,0:T(8,128)S(1)}, u32[]{:S(2)}, u32[]{:S(2)}) collective-permute-start(f32[160,128]{1,0:T(8,128)S(1)} %pad_maximum_fusion.4.own), channel_id=1, source_target_pairs={{2,0},{3,1},{0,2},{1,3},{6,4},{7,5},{4,6},{5,7},{10,8},{11,9},{8,1... | collective-permute-start | bytes 245768 | tf_op jit(solution)/shard_map/ppermute | solution.py:711
  58.6 1.8 %collective-permute-start.17 = (f32[160,128]{1,0:T(8,128)S(1)}, f32[160,128]{1,0:T(8,128)S(1)}, u32[]{:S(2)}, u32[]{:S(2)}) collective-permute-start(f32[160,128]{1,0:T(8,128)S(1)} %pad_maximum_fusion.4.own), channel_id=1, source_target_pairs={{3,0},{2,1},{1,2},{0,3},{7,4},{6,5},{5,6},{4,7},{11,8},{10,9},{9,1... | collective-permute-start | bytes 245768 | tf_op jit(solution)/shard_map/ppermute | solution.py:711
  60.5 0.5 collective-permute-start.16
  61.0 0.1 pad_add_fusion.order
  61.1 1.1 %collective-permute-done.18.far = f32[160,128]{1,0:T(8,128)S(1)} collective-permute-done((f32[160,128]{1,0:T(8,128)S(1)}, f32[160,128]{1,0:T(8,128)S(1)}, u32[]{:S(2)}, u32[]{:S(2)}) %collective-permute-start.18) | collective-permute-done | bytes 81952 | tf_op jit(solution)/shard_map/ppermute | solution.py:711
  62.2 1.7 %collective-permute-done.17.other = f32[160,128]{1,0:T(8,128)S(1)} collective-permute-done((f32[160,128]{1,0:T(8,128)S(1)}, f32[160,128]{1,0:T(8,128)S(1)}, u32[]{:S(2)}, u32[]{:S(2)}) %collective-permute-start.17) | collective-permute-done | bytes 81952 | tf_op jit(solution)/shard_map/ppermute | solution.py:711
  64.0 0.9 %collective-permute-done.16.mate = f32[160,128]{1,0:T(8,128)S(1)} collective-permute-done((f32[160,128]{1,0:T(8,128)S(1)}, f32[160,128]{1,0:T(8,128)S(1)}, u32[]{:S(2)}, u32[]{:S(2)}) %collective-permute-start.16) | collective-permute-done | bytes 81952 | tf_op jit(solution)/shard_map/ppermute | solution.py:711
  64.9 0.9 %shard_map.128 = (f32[8,16,128]{2,1,0:T(8,128)S(1)}, f32[48,128]{1,0:T(8,128)S(1)}) custom-call(s32[4]{0:T(128)S(1)} %pad_add_fusion.order, f32[160,128]{1,0:T(8,128)S(1)} %pad_maximum_fusion.4.own, f32[160,128]{1,0:T(8,128)S(1)} %collective-permute-done.16.mate, f32[160,128]{1,0:T(8,128)S(1)} %collective-permute-done.17.other, ...), custom_call_target="tpu_custom_call" | custom-call | flops 1048576 | bytes 65536 | tf_op jit(solution)/shard_map/pallas_call | solution.py:717
  65.8 8.3 %all_to_all.5.got = f32[8,16,128]{2,1,0:T(8,128)S(1)} all-to-all(f32[8,16,128]{2,1,0:T(8,128)S(1)} %get-tuple-element.66), channel_id=1, replica_groups=mesh['gx'=8,'gy'=4] {'gx'}, dimensions={0} | all-to-all | bytes 131072 | tf_op jit(solution)/shard_map/all_to_all | solution.py:933
  74.1 3.5 %shard_map.129 = (f32[2,3,32,64]{3,2,1,0:T(8,128)}, f32[2,32,32]{2,1,0:T(8,128)}) custom-call(f32[8,16,128]{2,1,0:T(8,128)S(1)} %all_to_all.5.got, f32[64,128]{1,0:T(8,128)S(1)} %get-tuple-element.67.sums, f32[48,128]{1,0:T(8,128)S(1)} %get-tuple-element.68.rown, f32[48,128]{1,0:T(8,128)S(1)} %get-tuple-element.69.yown, ...), custom_call_target="tpu_custom_call" | custom-call | flops 1048576 | bytes 65536 | tf_op jit(solution)/shard_map/pallas_call | solution.py:717
  (14 shorter events, 0.1 us)
Async XLA Ops:
  1.6 6.5 %collective-permute-start.1 = (f32[104,128]{1,0:T(8,128)S(1)}, f32[104,128]{1,0:T(8,128)S(1)}, u32[]{:S(2)}, u32[]{:S(2)}) collective-permute-start(f32[104,128]{1,0:T(8,128)S(1)} %convert_add_fusion.1.table.cown), channel_id=1, source_target_pairs={{28,0},{8,4},{4,8},{16,12},{12,16},{24,20},{20,24},{0,28},{29,1},{... | collective-permute-start | bytes 159752 | tf_op jit(solution)/shard_map/ppermute | solution.py:711
  6.1 1.9 %collective-permute-start = (f32[104,128]{1,0:T(8,128)S(1)}, f32[104,128]{1,0:T(8,128)S(1)}, u32[]{:S(2)}, u32[]{:S(2)}) collective-permute-start(f32[104,128]{1,0:T(8,128)S(1)} %convert_add_fusion.1.table.cown), channel_id=1, source_target_pairs={{4,0},{0,4},{12,8},{8,12},{20,16},{16,20},{28,24},{24,28},{5,1},{1... | collective-permute-start | bytes 159752 | tf_op jit(solution)/shard_map/ppermute | solution.py:711
  9.2 5.4 %collective-permute-start.2 = (f32[104,128]{1,0:T(8,128)S(1)}, f32[104,128]{1,0:T(8,128)S(1)}, u32[]{:S(2)}, u32[]{:S(2)}) collective-permute-start(f32[104,128]{1,0:T(8,128)S(1)} %get-tuple-element.38), channel_id=1, source_target_pairs={{1,0},{0,1},{3,2},{2,3},{5,4},{4,5},{7,6},{6,7},{9,8},{8,9},{11,10... | collective-permute-start | bytes 159752 | tf_op jit(solution)/shard_map/ppermute | solution.py:711
  11.4 5.0 %collective-permute-start.3 = (f32[104,128]{1,0:T(8,128)S(1)}, f32[104,128]{1,0:T(8,128)S(1)}, u32[]{:S(2)}, u32[]{:S(2)}) collective-permute-start(f32[104,128]{1,0:T(8,128)S(1)} %get-tuple-element.39), channel_id=1, source_target_pairs={{3,0},{2,1},{1,2},{0,3},{7,4},{6,5},{5,6},{4,7},{11,8},{10,9},{9,1... | collective-permute-start | bytes 159752 | tf_op jit(solution)/shard_map/ppermute | solution.py:711
  24.8 3.7 %collective-permute-start.4 = (f32[144,128]{1,0:T(8,128)S(1)}, f32[144,128]{1,0:T(8,128)S(1)}, u32[]{:S(2)}, u32[]{:S(2)}) collective-permute-start(f32[144,128]{1,0:T(8,128)S(1)} %get-tuple-element.50), channel_id=1, source_target_pairs={{4,0},{0,4},{12,8},{8,12},{20,16},{16,20},{28,24},{24,28},{5,1},{1... | collective-permute-start | bytes 221192 | tf_op jit(solution)/shard_map/ppermute | solution.py:711
  24.9 5.6 %collective-permute-start.5 = (f32[144,128]{1,0:T(8,128)S(1)}, f32[144,128]{1,0:T(8,128)S(1)}, u32[]{:S(2)}, u32[]{:S(2)}) collective-permute-start(f32[144,128]{1,0:T(8,128)S(1)} %get-tuple-element.51), channel_id=1, source_target_pairs={{28,0},{8,4},{4,8},{16,12},{12,16},{24,20},{20,24},{0,28},{29,1},{... | collective-permute-start | bytes 221192 | tf_op jit(solution)/shard_map/ppermute | solution.py:711
  27.3 1.2 %collective-permute-start.6 = (f32[32,128]{1,0:T(8,128)S(1)}, f32[32,128]{1,0:T(8,128)S(1)}, u32[]{:S(2)}, u32[]{:S(2)}) collective-permute-start(f32[32,128]{1,0:T(8,128)S(1)} %shard_map.125), channel_id=1, source_target_pairs={{4,0},{0,4},{12,8},{8,12},{20,16},{16,20},{28,24},{24,28},{5,1},{1... | collective-permute-start | bytes 49160 | tf_op jit(solution)/shard_map/ppermute | solution.py:711
  30.6 4.3 %collective-permute-start.7 = (f32[128,128]{1,0:T(8,128)S(1)}, f32[128,128]{1,0:T(8,128)S(1)}, u32[]{:S(2)}, u32[]{:S(2)}) collective-permute-start(f32[128,128]{1,0:T(8,128)S(1)} %get-tuple-element.78), channel_id=1, source_target_pairs={{1,0},{0,1},{3,2},{2,3},{5,4},{4,5},{7,6},{6,7},{9,8},{8,9},{11,10... | collective-permute-start | bytes 196616 | tf_op jit(solution)/shard_map/ppermute | solution.py:711
  31.3 4.4 %collective-permute-start.8 = (f32[128,128]{1,0:T(8,128)S(1)}, f32[128,128]{1,0:T(8,128)S(1)}, u32[]{:S(2)}, u32[]{:S(2)}) collective-permute-start(f32[128,128]{1,0:T(8,128)S(1)} %get-tuple-element.79), channel_id=1, source_target_pairs={{2,0},{3,1},{0,2},{1,3},{6,4},{7,5},{4,6},{5,7},{10,8},{11,9},{8,1... | collective-permute-start | bytes 196616 | tf_op jit(solution)/shard_map/ppermute | solution.py:711
  32.7 5.2 %collective-permute-start.9 = (f32[128,128]{1,0:T(8,128)S(1)}, f32[128,128]{1,0:T(8,128)S(1)}, u32[]{:S(2)}, u32[]{:S(2)}) collective-permute-start(f32[128,128]{1,0:T(8,128)S(1)} %get-tuple-element.80), channel_id=1, source_target_pairs={{3,0},{2,1},{1,2},{0,3},{7,4},{6,5},{5,6},{4,7},{11,8},{10,9},{9,1... | collective-permute-start | bytes 196616 | tf_op jit(solution)/shard_map/ppermute | solution.py:711
  37.9 4.8 %collective-permute-start.13 = (f32[32,128]{1,0:T(8,128)S(1)}, f32[32,128]{1,0:T(8,128)S(1)}, u32[]{:S(2)}, u32[]{:S(2)}) collective-permute-start(f32[32,128]{1,0:T(8,128)S(1)} %fusion.1), channel_id=1, source_target_pairs={{16,0},{20,4},{24,8},{28,12},{0,16},{4,20},{8,24},{12,28},{17,1},{... | collective-permute-start | bytes 49160 | tf_op jit(solution)/shard_map/ppermute | solution.py:711
  38.0 4.7 %collective-permute-start.12 = (f32[32,128]{1,0:T(8,128)S(1)}, f32[32,128]{1,0:T(8,128)S(1)}, u32[]{:S(2)}, u32[]{:S(2)}) collective-permute-start(f32[32,128]{1,0:T(8,128)S(1)} %fusion.1), channel_id=1, source_target_pairs={{8,0},{28,4},{16,8},{4,12},{24,16},{12,20},{0,24},{20,28},{9,1},{2... | collective-permute-start | bytes 49160 | tf_op jit(solution)/shard_map/ppermute | solution.py:711
  38.9 6.6 %collective-permute-start.11 = (f32[176,128]{1,0:T(8,128)S(1)}, f32[176,128]{1,0:T(8,128)S(1)}, u32[]{:S(2)}, u32[]{:S(2)}) collective-permute-start(f32[176,128]{1,0:T(8,128)S(1)} %pad_maximum_fusion.3.own), channel_id=1, source_target_pairs={{28,0},{8,4},{4,8},{16,12},{12,16},{24,20},{20,24},{0,28},{29,1},{... | collective-permute-start | bytes 270344 | tf_op jit(solution)/shard_map/ppermute | solution.py:711
  39.0 6.5 %collective-permute-start.10 = (f32[176,128]{1,0:T(8,128)S(1)}, f32[176,128]{1,0:T(8,128)S(1)}, u32[]{:S(2)}, u32[]{:S(2)}) collective-permute-start(f32[176,128]{1,0:T(8,128)S(1)} %pad_maximum_fusion.3.own), channel_id=1, source_target_pairs={{4,0},{0,4},{12,8},{8,12},{20,16},{16,20},{28,24},{24,28},{5,1},{1... | collective-permute-start | bytes 270344 | tf_op jit(solution)/shard_map/ppermute | solution.py:711
  51.7 1.4 %collective-permute-start.14 = (f32[144,128]{1,0:T(8,128)S(1)}, f32[144,128]{1,0:T(8,128)S(1)}, u32[]{:S(2)}, u32[]{:S(2)}) collective-permute-start(f32[144,128]{1,0:T(8,128)S(1)} %get-tuple-element.62), channel_id=1, source_target_pairs={{4,0},{0,4},{12,8},{8,12},{20,16},{16,20},{28,24},{24,28},{5,1},{1... | collective-permute-start | bytes 221192 | tf_op jit(solution)/shard_map/ppermute | solution.py:711
  51.8 5.6 %collective-permute-start.15 = (f32[144,128]{1,0:T(8,128)S(1)}, f32[144,128]{1,0:T(8,128)S(1)}, u32[]{:S(2)}, u32[]{:S(2)}) collective-permute-start(f32[144,128]{1,0:T(8,128)S(1)} %get-tuple-element.63), channel_id=1, source_target_pairs={{28,0},{8,4},{4,8},{16,12},{12,16},{24,20},{20,24},{0,28},{29,1},{... | collective-permute-start | bytes 221192 | tf_op jit(solution)/shard_map/ppermute | solution.py:711
  57.5 4.8 %collective-permute-start.18 = (f32[160,128]{1,0:T(8,128)S(1)}, f32[160,128]{1,0:T(8,128)S(1)}, u32[]{:S(2)}, u32[]{:S(2)}) collective-permute-start(f32[160,128]{1,0:T(8,128)S(1)} %pad_maximum_fusion.4.own), channel_id=1, source_target_pairs={{2,0},{3,1},{0,2},{1,3},{6,4},{7,5},{4,6},{5,7},{10,8},{11,9},{8,1... | collective-permute-start | bytes 245768 | tf_op jit(solution)/shard_map/ppermute | solution.py:711
  58.6 5.3 %collective-permute-start.17 = (f32[160,128]{1,0:T(8,128)S(1)}, f32[160,128]{1,0:T(8,128)S(1)}, u32[]{:S(2)}, u32[]{:S(2)}) collective-permute-start(f32[160,128]{1,0:T(8,128)S(1)} %pad_maximum_fusion.4.own), channel_id=1, source_target_pairs={{3,0},{2,1},{1,2},{0,3},{7,4},{6,5},{5,6},{4,7},{11,8},{10,9},{9,1... | collective-permute-start | bytes 245768 | tf_op jit(solution)/shard_map/ppermute | solution.py:711
  60.5 4.4 %collective-permute-start.16 = (f32[160,128]{1,0:T(8,128)S(1)}, f32[160,128]{1,0:T(8,128)S(1)}, u32[]{:S(2)}, u32[]{:S(2)}) collective-permute-start(f32[160,128]{1,0:T(8,128)S(1)} %pad_maximum_fusion.4.own), channel_id=1, source_target_pairs={{1,0},{0,1},{3,2},{2,3},{5,4},{4,5},{7,6},{6,7},{9,8},{8,9},{11,10... | collective-permute-start | bytes 245768 | tf_op jit(solution)/shard_map/ppermute | solution.py:711
